TPU v7x, 512 devices: a whole 4x8x8 slice. The times are simulated.
512 devices in a mesh: child: 2 (over x_hi), row: 16 (over z, x_lo), col: 16 (over y, core).
Axes of the slice: x: 4 (x_hi: 2, x_lo: 2; x = x_hi * 2 + x_lo), y: 8, z: 8, core: 2. Of those that a mesh axis runs over, the one named last changes fastest.
Arguments:
- contrib: float32 [2, 8192, 8192], P('child', 'row', 'col'), may hold values from -0.0625 to 0.0625
- assembled: float32 [2, 8192, 16384], P('child', 'row', 'col'), may hold values from -0.0625 to 0.0625
- pattern: int32 [64, 64], P('row', 'col'), may hold values 0 or 1
- omega: float32 [16384, 256], P('col', 'row'), may hold values from -6 to 6
- row_maps: int32 [2, 8192], P('child'), may hold values from 0 to 16383, as said below
- leaf_bounds: int32 [16], P('row'), may hold values from 448 to 576
Outputs:
- bases: float32 [16384, 256], P('row', ('child', 'col'))
- coupling: float32 [16, 2, 256, 256], P('row', None, ('child', 'col'))
Inputs may be any that keep to these rules, and one draw needn't show every extreme that they name: `row_maps`: for each child, entries k * 512 to (k + 1) * 512 - 1 are distinct, rising, and lie in k * 1024 to (k + 1) * 1024 - 1.
All inputs are finite; a program needn't handle non-finite values. No bound on the sum of `pattern` on one device may be relied on, other than what follows from the above.
Results may differ from a plain program's by a relative error of at most 0.0003.
Values sent between devices are 32-bit elements; how exact they have to be, the bound alone decides.
No kernel may reach another device: no remote copies, remote signals or barrier semaphores. Data moves between devices by JAX's collectives and lax.ppermute only.
A program may use at most 64 MiB of HBM per device.

v0:
```python
import jax
import jax.numpy as jnp
from jax import lax
from jax.sharding import PartitionSpec as P

R = 256
BT = 256


highest = lax.Precision.HIGHEST


def partner(block, axis, distance):
    count = lax.axis_size(axis)
    route = []
    for low in range(count):
        high = low | 1 << distance
        if high != low and high < count:
            route += [(low, high), (high, low)]
    return lax.ppermute(block, axis, route)


def window_leaves(window, leaf_bound, counts):
    window_rows = window.shape[0]
    upper = window_rows // 2 + window_rows // 16
    lower = window_rows // 2 - window_rows // 16
    positions = jnp.arange(window_rows, dtype=jnp.int32)
    first_leaf = (positions < leaf_bound)[:, None]
    head_rows = window[:upper]
    tail_rows = window[lower:]
    head_masked = jnp.where(first_leaf[:upper], head_rows, 0.0)
    tail_masked = jnp.where(first_leaf[lower:], 0.0, tail_rows)
    head_gram = jnp.dot(head_masked.T, head_rows, precision=highest)
    tail_gram = jnp.dot(tail_masked.T, tail_rows, precision=highest)
    factors = jnp.linalg.cholesky(jnp.stack([head_gram, tail_gram]) / counts)
    head_part = lax.linalg.triangular_solve(
        factors[0], head_rows, left_side=False, lower=True, transpose_a=True
    )
    tail_part = lax.linalg.triangular_solve(
        factors[1], tail_rows, left_side=False, lower=True, transpose_a=True
    )
    middle = jnp.where(first_leaf[lower:upper], head_part[lower:], tail_part[: upper - lower])
    whole = jnp.concatenate([head_part[:lower], middle, tail_part[upper - lower :]], axis=0)
    return (factors, whole)


def local(contrib, assembled, pattern, omega, row_maps, leaf_bounds):
    tile_rows = contrib.shape[1]
    tile_cols = contrib.shape[2]
    window_rows = omega.shape[0]
    slice_width = R // (2 * lax.axis_size("col"))
    row_pos = lax.axis_index("row")
    col_pos = lax.axis_index("col")
    half_pos = lax.axis_index("child")
    group_pos = half_pos * lax.axis_size("col") + col_pos
    zero_index = jnp.zeros((), jnp.int32)
    child_maps = row_maps[0]
    column_maps = (
        lax.dynamic_slice_in_dim(child_maps, col_pos * tile_cols, tile_cols) - col_pos * window_rows
    )
    target_maps = (
        lax.dynamic_slice_in_dim(child_maps, row_pos * tile_rows, tile_rows) - row_pos * window_rows
    )
    full_omega = lax.all_gather(omega, "row", axis=1, tiled=True)
    picked = jnp.take(full_omega, column_maps, axis=0)
    product = jnp.dot(contrib[0], picked, precision=highest)
    pattern_rows = lax.dynamic_slice_in_dim(
        pattern, half_pos * (tile_rows // BT), tile_rows // BT, 0
    ).astype(jnp.float32)
    masked = (
        assembled[0].reshape(tile_rows // BT, BT, window_rows // BT, BT)
        * pattern_rows[:, None, :, None]
    ).reshape(tile_rows, window_rows)
    sparse = jnp.dot(masked, full_omega, precision=highest)
    child_red, sparse_red = (
        lax.psum_scatter(
            product.reshape(tile_rows, 2, R // 2), "col", scatter_dimension=2, tiled=True
        ),
        lax.psum_scatter(
            sparse.reshape(tile_rows, 2, R // 2), "col", scatter_dimension=2, tiled=True
        ),
    )
    spread = jnp.zeros((window_rows, 2, slice_width), jnp.float32).at[target_maps].add(child_red)
    placed = lax.dynamic_update_slice(
        jnp.zeros((window_rows, 2, slice_width), jnp.float32),
        sparse_red,
        (half_pos * tile_rows, zero_index, zero_index),
    )
    samples = lax.psum_scatter(spread + placed, "child", scatter_dimension=1, tiled=True).reshape(
        window_rows, slice_width
    )
    leaf_bound = leaf_bounds[0]
    head_count = leaf_bound.astype(jnp.float32)
    tail_count = (window_rows - leaf_bound).astype(jnp.float32)
    counts = jnp.stack([head_count, tail_count])[:, None, None]
    window = lax.all_gather(samples, ("child", "col"), axis=1, tiled=True)
    factors, whole = window_leaves(window, leaf_bound, counts)
    bases = lax.dynamic_slice_in_dim(whole, group_pos * slice_width, slice_width, 1)
    own_cols = lax.dynamic_slice_in_dim(factors, group_pos * slice_width, slice_width, 2)
    sibling = partner(factors, "row", 0)
    coupling = jnp.einsum("lab,lac->lbc", own_cols, sibling, precision=highest)
    return (bases, coupling[None])


def solution(mesh):
    in_specs = (
        P("child", "row", "col"),
        P("child", "row", "col"),
        P("row", "col"),
        P("col", "row"),
        P("child", None),
        P("row"),
    )
    out_specs = (P("row", ("child", "col")), P("row", None, ("child", "col"), None))
    return jax.shard_map(local, mesh=mesh, in_specs=in_specs, out_specs=out_specs, check_vma=False)
```

profile of v0, /device:TPU:1, one launch (start us, length us, event | category | flops | bytes accessed | tf_op | source)
XLA Modules:
  0.0 525.0 jit_solution(18265540738242747835)
XLA Ops:
  7.2 0.7 all-gather.4.cloned.1.call-update
  8.0 0.7 fusion.39
  8.7 0.3 mul.45
  9.0 2.1 mul.46
  11.1 0.7 compare_select_fusion
  11.9 65.8 %all-gather.4.cloned.1.call-done = f32[1024,256]{0,1:T(8,128)} async-done(((f32[1024,16]{0,1:T(8,128)}), f32[1024,256]{0,1:T(8,128)}) %all-gather.4.cloned.1.call-update) | async-done | bytes 1048592 | tf_op jit(solution)/shard_map/all_gather | solution.py:64
  77.6 1.6 copy.55
  79.2 2.2 gather_fusion
  81.5 3.1 fusion.3
  84.6 1.2 copy.56
  85.9 4.7 fusion
  90.7 1.3 dynamic-slice.8
  92.6 118.2 %all-reduce.4.cloned.1.call-done = f32[512,2,128]{0,1,2:T(2,128)} async-done(((f32[512,2,128]{0,1,2:T(2,128)}), f32[512,2,128]{0,1,2:T(2,128)}) %all-reduce.4.cloned.1.call-update) | async-done | bytes 524304
  210.9 0.8 constant_dynamic-slice_fusion.6
  211.6 0.2 copy.57
  211.9 0.3 broadcast.161
  212.1 16.7 %scatter_fusion = f32[1024,2,8]{2,1,0:T(2,128)S(1)} fusion(f32[1024,2,8]{2,1,0:T(2,128)S(1)} %broadcast.161, s32[512]{0:T(512)S(1)} %bitcast.118, f32[512,2,8]{2,1,0:T(2,128)S(1)} %copy.57), kind=kCustom, calls=%fused_computation.1 | custom fusion | flops 8192 | bytes 100352 | tf_op jit(solution)/shard_map/scatter-add | solution.py:83
  228.9 0.2 copy.79
  229.0 42.9 %reduce-scatter.3.cloned.1.call-done = f32[512,2,8]{0,2,1:T(8,128)} async-done(((f32[512,2,128]{0,2,1:T(8,128)}), f32[512,2,8]{0,2,1:T(8,128)}) %reduce-scatter.3.cloned.1.call-update) | async-done | bytes 32784 | tf_op jit(solution)/shard_map/reduce_scatter | solution.py:79
  271.9 0.8 dynamic_update_slice.3
  272.7 0.2 copy.59
  273.0 1.0 copy.60
  274.1 0.2 all-gather.6.cloned.1.call-start
  274.3 19.7 %reduce-scatter.5.cloned.1.call-done = f32[1024,1,8]{0,2,1:T(8,128)} async-done(((f32[1024,2,8]{0,2,1:T(8,128)}), f32[1024,1,8]{0,2,1:T(8,128)}) %reduce-scatter.5.cloned.1.call-update) | async-done | bytes 32784 | tf_op jit(solution)/shard_map/reduce_scatter | solution.py:89
  294.0 1.4 copy.61
  296.4 84.6 %all-gather.6.cloned.1.call-done = f32[1024,1,256]{0,1,2:T(1,128)} async-done(((f32[1024,1,8]{0,1,2:T(1,128)}), f32[1024,1,256]{0,1,2:T(1,128)}) %all-gather.6.cloned.1.call-update) | async-done | bytes 1048592 | tf_op jit(solution)/shard_map/all_gather | solution.py:96
  381.1 3.1 fusion.48
  384.1 0.4 copy.80
  384.6 0.4 copy.81
  385.0 1.3 convolution_bitcast_fusion
  386.4 1.3 convolution_bitcast_fusion.1
  387.7 0.9 maximum_divide_fusion
  388.6 1.2 copy.66
  390.0 0.8 copy-done.3
  390.8 23.5 %custom-call.16 = f32[2,128,128]{2,1,0:T(8,128)S(1)} custom-call(f32[2,128,128]{2,1,0:T(8,128)S(1)} %cholesky.122), custom_call_target="Cholesky" | custom-call | tf_op jit(solution)/shard_map/jit(cholesky)/cholesky | solution.py:35
  414.3 19.7 %custom-call.17 = f32[2,1,128,128]{2,3,1,0:T(8,128)S(1)} custom-call(f32[2,1,128,128]{3,2,1,0:T(8,128)S(1)} %select_bitcast_fusion), custom_call_target="InvertDiagBlocksLowerTriangular" | custom-call | tf_op jit(solution)/shard_map/jit(cholesky)/cholesky | solution.py:35
  434.0 1.2 constant_dynamic-update-slice_fusion.1
  435.2 1.3 convolution_subtract_fusion.2
  436.5 23.7 %custom-call.18 = f32[2,128,128]{2,1,0:T(8,128)S(1)} custom-call(f32[2,128,128]{2,1,0:T(8,128)S(1)} %convolution_subtract_fusion.2), custom_call_target="Cholesky" | custom-call | tf_op jit(solution)/shard_map/jit(cholesky)/cholesky | solution.py:35
  460.2 0.2 compare_reduce_fusion
  460.4 0.1 select_select_fusion
  460.6 2.2 collective-permute-start
  462.9 4.0 while.4
  462.9 0.6 fusion.60
  463.5 1.4 bitcast_dynamic-update-slice_fusion.4
  464.9 0.6 fusion.60
  465.5 1.4 bitcast_dynamic-update-slice_fusion.4
  466.8 0.6 copy-done.4
  467.5 20.5 %custom-call.20 = f32[2,128,128]{1,2,0:T(8,128)S(1)} custom-call(f32[2,128,128]{2,1,0:T(8,128)} %copy-done.4), custom_call_target="InvertDiagBlocksLowerTriangular" | custom-call | tf_op jit(solution)/shard_map/triangular_solve/custom-call.0 | solution.py:36
  488.0 0.4 fusion.17
  488.4 1.2 convolution_subtract_fusion.1
  489.7 0.4 fusion.33
  490.1 4.0 while.5
  490.1 0.6 fusion.61
  490.7 1.4 bitcast_dynamic-update-slice_fusion.5
  492.1 0.6 fusion.61
  492.7 1.4 bitcast_dynamic-update-slice_fusion.5
  494.1 19.7 %custom-call.21 = f32[2,128,128]{1,2,0:T(8,128)S(1)} custom-call(f32[2,128,128]{2,1,0:T(8,128)S(1)} %get-tuple-element.18), custom_call_target="InvertDiagBlocksLowerTriangular" | custom-call | tf_op jit(solution)/shard_map/triangular_solve/custom-call.0 | solution.py:39
  513.8 0.4 fusion.15
  514.2 0.4 convolution_subtract_fusion
  514.6 0.4 fusion.31
  515.1 0.3 fusion.8
  515.4 0.8 copy.73
  516.2 2.3 convolution_bitcast_fusion.2
  (45 shorter events, 1.2 us)
Async XLA Ops:
  7.2 74.3 %copy-start = (f32[1,512,512]{2,1,0:T(8,128)S(1)}, f32[1,512,512]{2,1,0:T(8,128)}, u32[]{:S(2)}) copy-start(f32[1,512,512]{2,1,0:T(8,128)} %param.8) | copy-start | bytes 3145732
  7.2 70.5 %all-gather.4.cloned.1.call-start = ((), (), s32[]{:S(2)}) async-start(), calls=%async_computation.2 | async-start | bytes 1114112 | tf_op jit(solution)/shard_map/all_gather | solution.py:64
  7.9 202.9 %all-reduce.4.cloned.1.call-start = ((), (), s32[]{:S(2)}) async-start(), calls=%async_computation.6 | async-start | bytes 1048576
  81.5 4.4 copy-start.1
  85.8 186.1 %reduce-scatter.3.cloned.1.call-start = ((), (), s32[]{:S(2)}) async-start(), calls=%async_computation.3 | async-start | bytes 557056 | tf_op jit(solution)/shard_map/reduce_scatter | solution.py:79
  90.6 203.4 %reduce-scatter.5.cloned.1.call-start = ((), (), s32[]{:S(2)}) async-start(), calls=%async_computation.4 | async-start | bytes 98304 | tf_op jit(solution)/shard_map/reduce_scatter | solution.py:89
  274.1 107.0 %all-gather.6.cloned.1.call-start = ((), (), s32[]{:S(2)}) async-start(), calls=%async_computation.5 | async-start | bytes 1081344 | tf_op jit(solution)/shard_map/all_gather | solution.py:96
  390.0 0.8 copy-start.3
  460.6 55.6 %collective-permute-start = (f32[2,256,256]{2,1,0:T(8,128)S(1)}, f32[2,256,256]{2,1,0:T(8,128)}, u32[]{:S(2)}, u32[]{:S(2)}) collective-permute-start(f32[2,256,256]{2,1,0:T(8,128)S(1)} %select_select_fusion), channel_id=1, source_target_pairs={{0,16},{16,0},{32,48},{48,32},{64,80},{80,64},{96,112},{112,96},{1... | collective-permute-start | bytes 1572872 | tf_op jit(solution)/shard_map/ppermute | solution.py:20
  466.8 0.7 copy-start.4
  467.5 20.5 %copy-start.2 = (f32[256,256]{1,0:T(8,128)}, f32[256,256]{1,0:T(8,128)S(1)}, u32[]{:S(2)}) copy-start(f32[256,256]{1,0:T(8,128)S(1)} %get-tuple-element.164) | copy-start | bytes 786436
Sparse Core Ops, SparseCore 0:
  10.1 67.5 all-gather.3
  86.0 124.8 all-reduce.3
  213.9 57.9 reduce-scatter.2
  274.5 19.4 reduce-scatter.4
  297.8 83.2 all-gather.5
where the time goes:
time: 526 us; the launch traced here: 525 us
  waiting for transfers between devices  332 us (63%)
  other arithmetic  128 us (24%)
  local copies, waits for them, and re-layouts  28.5 us (5%)
  matrix products  18.5 us (4%)
  between operations  15.5 us (3%)
    unnamed x6, waiting for transfers between devices  119 us
    all_gather x1, waiting for transfers between devices, local(): window = lax.all_gather(samples, ('child', 'col'), axis=1, tiled=True)  84.6 us
    another operation x9, other arithmetic, window_leaves(): factors = jnp.linalg.cholesky(jnp.stack([head_gram, tail_gram]) / counts)  67.1 us
    all_gather x1, waiting for transfers between devices, local(): full_omega = lax.all_gather(omega, 'row', axis=1, tiled=True)  65.8 us
    reduce_scatter x1, waiting for transfers between devices, local(): lax.psum_scatter(sparse.reshape(tile_rows, 2, R // 2), 'col', scatter_dim...  42.9 us
    another operation x4, other arithmetic, window_leaves(): lax.linalg.triangular_solve(factors[0], head_rows, left_side=False, lower...  20.6 us
    reduce_scatter x1, waiting for transfers between devices, local(): lax.psum_scatter(spread + placed, 'child', scatter_dimension=1, tiled=True)  19.7 us
    another operation x2, other arithmetic, window_leaves(): lax.linalg.triangular_solve(factors[1], tail_rows, left_side=False, lower...  19.7 us
  transfers between devices with their start and end apart: 6, of which 5 were waited for; matrix products, arithmetic and copies ran while one was open for 15% of the time, Pallas kernels for 0%

commit v1 on v0

v1 whole, which is shorter than its diff:
```python
import jax
import jax.numpy as jnp
from jax import lax
from jax.sharding import Mesh, PartitionSpec as P

R = 256
BT = 256

high = lax.Precision.HIGH
highest = lax.Precision.HIGHEST

SWAP = [(0, 1), (1, 0)]


def dot_nt(a, b, precision=high):
    return lax.dot_general(a, b, (((1,), (1,)), ((), ())), precision=precision)


def window_leaves(window, leaf_bound, counts):
    window_rows = window.shape[0]
    upper = window_rows // 2 + window_rows // 16
    lower = window_rows // 2 - window_rows // 16
    positions = jnp.arange(window_rows, dtype=jnp.int32)
    first_leaf = (positions < leaf_bound)[:, None]
    head_rows = window[:upper]
    tail_rows = window[lower:]
    head_masked = jnp.where(first_leaf[:upper], head_rows, 0.0)
    tail_masked = jnp.where(first_leaf[lower:], 0.0, tail_rows)
    head_gram = jnp.dot(head_masked.T, head_rows, precision=highest)
    tail_gram = jnp.dot(tail_masked.T, tail_rows, precision=highest)
    factors = jnp.linalg.cholesky(jnp.stack([head_gram, tail_gram]) / counts)
    head_part = lax.linalg.triangular_solve(
        factors[0], head_rows, left_side=False, lower=True, transpose_a=True
    )
    tail_part = lax.linalg.triangular_solve(
        factors[1], tail_rows, left_side=False, lower=True, transpose_a=True
    )
    middle = jnp.where(first_leaf[lower:upper], head_part[lower:], tail_part[: upper - lower])
    whole = jnp.concatenate([head_part[:lower], middle, tail_part[upper - lower :]], axis=0)
    return (factors, whole)


def local(contrib, assembled, pattern, omega, row_maps, leaf_bounds):
    tile_rows = contrib.shape[1]
    tile_cols = contrib.shape[2]
    window_rows = omega.shape[0]
    own_cols_count = omega.shape[1]
    z_count = lax.axis_size("z")
    groups = lax.axis_size("child") * lax.axis_size("y")
    child = lax.axis_index("child")
    xl = lax.axis_index("xl")
    core = lax.axis_index("core")
    row_pos = lax.axis_index(("z", "xl"))
    col_pos = lax.axis_index(("y", "core"))
    width = R // (2 * groups)
    child_maps = row_maps[0]
    column_maps = (
        lax.dynamic_slice_in_dim(child_maps, col_pos * tile_cols, tile_cols) - col_pos * window_rows
    )
    target_maps = (
        lax.dynamic_slice_in_dim(child_maps, row_pos * tile_rows, tile_rows) - row_pos * window_rows
    )
    places = jnp.arange(window_rows, dtype=jnp.int32)
    pick = (places[:, None] == column_maps[None, :]).astype(jnp.float32)
    spread = (target_maps[:, None] == places[None, :]).astype(jnp.float32)
    pattern_rows = lax.dynamic_slice_in_dim(
        pattern, child * (tile_rows // BT), tile_rows // BT, 0
    ).astype(jnp.float32)
    masked = (
        assembled[0].reshape(tile_rows // BT, BT, window_rows // BT, BT)
        * pattern_rows[:, None, :, None]
    ).reshape(tile_rows, window_rows)

    lines = omega.T
    own = lax.all_to_all(
        jnp.broadcast_to(lines, (z_count, own_cols_count, window_rows)), "z", 0, 0
    )
    other = lax.ppermute(own, "xl", SWAP)

    def partial(omega_lines):
        picked = jnp.dot(omega_lines, pick, precision=high)
        product = dot_nt(picked, contrib[0])
        sparse = dot_nt(omega_lines, masked)
        spread_out = jnp.dot(product, spread, precision=high)
        zero = jnp.zeros_like(sparse)
        placed = jnp.concatenate(
            [jnp.where(child == 0, sparse, zero), jnp.where(child == 0, zero, sparse)], axis=1
        )
        return (spread_out + placed).reshape(z_count, width, window_rows)

    def half(gathered):
        split = gathered.reshape(z_count, 2, width, window_rows)
        give = lax.dynamic_index_in_dim(split, 1 - core, 1, keepdims=False)
        keep = lax.dynamic_index_in_dim(split, core, 1, keepdims=False)
        arrived = lax.ppermute(partial(give.reshape(-1, window_rows)), "core", SWAP)
        return partial(keep.reshape(-1, window_rows)) + arrived

    parts = jnp.concatenate([half(own), half(other)], axis=0)
    terms = lax.all_to_all(parts, ("child", "y"), 0, 0)
    samples = jnp.sum(terms, axis=0)
    mine = lax.all_to_all(
        jnp.broadcast_to(samples, (groups, width, window_rows)), ("child", "y"), 0, 0
    )
    theirs = lax.ppermute(mine, "core", SWAP)
    pair = jnp.where(core == 0, jnp.stack([mine, theirs]), jnp.stack([theirs, mine]))
    pair = pair.reshape(2, 2, z_count, width, window_rows)
    pair = jnp.where(xl == 0, pair, pair[:, ::-1])
    window = pair.transpose(2, 1, 0, 3, 4).reshape(R, window_rows)

    leaf_bound = leaf_bounds[0]
    counts = jnp.stack([leaf_bound, window_rows - leaf_bound]).astype(jnp.float32)[:, None, None]
    factors, whole = window_leaves(window.T, leaf_bound, counts)
    group_pos = child * lax.axis_size("y") * 2 + col_pos
    bases = lax.dynamic_slice_in_dim(whole, group_pos * width, width, 1)
    own_cols = lax.dynamic_slice_in_dim(factors, group_pos * width, width, 2)
    sibling = lax.ppermute(factors, "xl", SWAP)
    coupling = jnp.einsum("lab,lac->lbc", own_cols, sibling, precision=highest)
    return (bases, coupling[None])


def solution(mesh):
    fine = Mesh(mesh.devices.reshape(2, 8, 2, 8, 2), ("child", "z", "xl", "y", "core"))
    row, col = ("z", "xl"), ("y", "core")
    in_specs = (
        P("child", row, col),
        P("child", row, col),
        P(row, col),
        P(col, row),
        P("child", None),
        P(row),
    )
    out_specs = (P(row, ("child",) + col), P(row, None, ("child",) + col, None))
    return jax.shard_map(local, mesh=fine, in_specs=in_specs, out_specs=out_specs, check_vma=False)
```

time: 526 us -> 260 us (0.49)
  waiting for transfers between devices: 332 us -> 51.5 us
  starting transfers between devices: 2.58 us -> 42.7 us
  between operations: 15.5 us -> 1.63 us
  other arithmetic: 128 us -> 115 us
  matrix products: 18.5 us -> 29.5 us
  local copies, waits for them, and re-layouts: 28.5 us -> 18.4 us
    all_gather x2 -> x0, waiting for transfers between devices: 150 us -> none  [the longest x1 84.6 us: local(): window = lax.all_gather(samples, ('child', 'col'), axis=1, tiled=True)]
    unnamed x6 -> x0, waiting for transfers between devices: 119 us -> none
    reduce_scatter x2 -> x0, waiting for transfers between devices: 62.6 us -> none  [the longest x1 42.9 us: local(): lax.psum_scatter(sparse.reshape(tile_rows, 2, R // 2), 'col', scatter_dim...]
    all_to_all x0 -> x3, waiting for transfers between devices: none -> 40.7 us  [the longest x1 15.2 us: local(): terms = lax.all_to_all(parts, ('child', 'y'), 0, 0)]
    all_to_all x0 -> x3, starting transfers between devices: none -> 27.2 us  [the longest x1 10.9 us: local(): lax.all_to_all(jnp.broadcast_to(lines, (z_count, own_cols_count, window_r...]
    scatter-add x1 -> x0, other arithmetic: 16.7 us -> none  [local(): jnp.zeros((window_rows, 2, slice_width), jnp.float32).at[target_maps]]
    ppermute x1 -> x5, starting transfers between devices: 2.2 us -> 15.5 us  [the longest x2 5.1 us: half(): arrived = lax.ppermute(partial(give.reshape(-1, window_rows)), 'core', SWAP)]
    ppermute x1 -> x5, waiting for transfers between devices: 0.01 us -> 10.8 us  [the longest x1 9.5 us: local(): other = lax.ppermute(own, 'xl', SWAP)]
  transfers between devices with their start and end apart: 6 -> 8, of which waited for: 5 -> 5; matrix products, arithmetic and copies ran while one was open for 15% -> 28% of each run, Pallas kernels for 0% -> 0%
where the time goes in v1:
time: 260 us; the launch traced here: 259 us
  other arithmetic  115 us (44%)
  waiting for transfers between devices  51.5 us (20%)
  starting transfers between devices  42.7 us (16%)
  matrix products  29.5 us (11%)
  local copies, waits for them, and re-layouts  18.4 us (7%)
    another operation x9, other arithmetic, window_leaves(): factors = jnp.linalg.cholesky(jnp.stack([head_gram, tail_gram]) / counts)  66.8 us
    another operation x4, other arithmetic, window_leaves(): lax.linalg.triangular_solve(factors[0], head_rows, left_side=False, lower...  21.2 us
    another operation x2, other arithmetic, window_leaves(): lax.linalg.triangular_solve(factors[1], tail_rows, left_side=False, lower...  20.3 us
    all_to_all x1, waiting for transfers between devices, local(): terms = lax.all_to_all(parts, ('child', 'y'), 0, 0)  15.2 us
    all_to_all x1, waiting for transfers between devices, local(): lax.all_to_all(jnp.broadcast_to(samples, (groups, width, window_rows)), (...  14 us
    all_to_all x1, waiting for transfers between devices, local(): lax.all_to_all(jnp.broadcast_to(lines, (z_count, own_cols_count, window_r...  11.6 us
    all_to_all x1, starting transfers between devices, local(): lax.all_to_all(jnp.broadcast_to(lines, (z_count, own_cols_count, window_r...  10.9 us
    ppermute x1, waiting for transfers between devices, local(): other = lax.ppermute(own, 'xl', SWAP)  9.5 us
  transfers between devices with their start and end apart: 8, of which 5 were waited for; matrix products, arithmetic and copies ran while one was open for 28% of the time, Pallas kernels for 0%

profile of v1, /device:TPU:1, one launch (start us, length us, event | category | flops | bytes accessed | tf_op | source)
XLA Modules:
  0.0 259.1 jit_solution(5286608574307412443)
XLA Ops:
  0.6 1.8 broadcast_in_dim.54
  2.4 10.9 %all-to-all-start = ((f32[8,16,1024]{2,1,0:T(8,128)}), f32[8,16,1024]{2,1,0:T(8,128)}, u32[]{:S(2)}, u32[]{:S(2)}) async-start(f32[8,16,1024]{2,1,0:T(8,128)} %broadcast_in_dim.54), calls=%async_computation | async-start | bytes 1048576 | tf_op jit(solution)/shard_map/all_to_all | solution.py:75
  13.3 0.7 fusion.99
  14.3 2.1 mul.54
  16.4 2.6 %mul.55 = f32[1,512,1024]{2,1,0:T(8,128)S(1)} multiply(f32[1,512,1024]{2,1,0:T(8,128)} %param.9, f32[1,512,1024]{2,1,0:T(8,128)} %mul.54) | non-fusion elementwise | flops 524288 | bytes 6291456 | tf_op jit(solution)/shard_map/mul | solution.py:70
  19.1 0.7 fusion.98
  19.8 11.6 %all-to-all-done = f32[8,16,1024]{2,1,0:T(8,128)} async-done(((f32[8,16,1024]{2,1,0:T(8,128)}), f32[8,16,1024]{2,1,0:T(8,128)}, u32[]{:S(2)}, u32[]{:S(2)}) %all-to-all-start) | async-done | bytes 524320 | tf_op jit(solution)/shard_map/all_to_all | solution.py:75
  31.4 1.6 fusion.14
  33.0 0.6 fusion.31
  33.6 2.0 broadcast_select_fusion.5
  35.6 0.8 fusion.19
  36.4 2.4 collective-permute-start
  38.8 2.0 broadcast_select_fusion.7
  40.9 3.1 %collective-permute-start.1 = (f32[8,16,1024]{2,1,0:T(8,128)}, f32[8,16,1024]{2,1,0:T(8,128)S(1)}, u32[]{:S(2)}, u32[]{:S(2)}) collective-permute-start(f32[8,16,1024]{2,1,0:T(8,128)} %all-to-all-done), channel_id=1, source_target_pairs={{0,16},{16,0},{1,17},{17,1},{2,18},{18,2},{3,19},{19,3},{4,20},{20... | collective-permute-start | bytes 1572872 | tf_op jit(solution)/shard_map/ppermute | solution.py:78
  44.0 1.6 fusion.15
  45.6 0.6 fusion.33
  46.2 0.8 fusion.25
  47.0 9.5 %collective-permute-done.1 = f32[8,16,1024]{2,1,0:T(8,128)S(1)} collective-permute-done((f32[8,16,1024]{2,1,0:T(8,128)}, f32[8,16,1024]{2,1,0:T(8,128)S(1)}, u32[]{:S(2)}, u32[]{:S(2)}) %collective-permute-start.1) | collective-permute-done | bytes 524320 | tf_op jit(solution)/shard_map/ppermute | solution.py:78
  56.5 0.7 fusion.12
  57.2 1.1 broadcast_select_fusion.1
  58.2 1.1 broadcast_select_fusion.3
  59.3 0.6 fusion.27
  59.9 0.8 fusion.23
  60.7 2.7 %collective-permute-start.2 = (f32[8,8,1024]{2,1,0:T(8,128)S(1)}, f32[8,8,1024]{2,1,0:T(8,128)S(1)}, u32[]{:S(2)}, u32[]{:S(2)}) collective-permute-start(f32[8,8,1024]{2,1,0:T(8,128)S(1)} %fusion.23), channel_id=1, source_target_pairs={{0,1},{1,0},{2,3},{3,2},{4,5},{5,4},{6,7},{7,6},{8,9},{9,8},{10,11... | collective-permute-start | bytes 786440 | tf_op jit(solution)/shard_map/ppermute | solution.py:95
  63.4 0.7 fusion.13
  64.1 0.6 fusion.29
  64.7 0.8 fusion.24
  65.5 0.9 pad_maximum_fusion
  66.3 9.4 %all-to-all-start.1 = ((f32[16,8,1024]{2,1,0:T(8,128)}), f32[16,8,1024]{2,1,0:T(8,128)S(1)}, u32[]{:S(2)}, u32[]{:S(2)}) async-start(f32[16,8,1024]{2,1,0:T(8,128)} %pad_maximum_fusion), calls=%async_computation.1 | async-start | bytes 1048576 | tf_op jit(solution)/shard_map/all_to_all | solution.py:99
  75.7 15.2 %all-to-all-done.1 = f32[16,8,1024]{2,1,0:T(8,128)S(1)} async-done(((f32[16,8,1024]{2,1,0:T(8,128)}), f32[16,8,1024]{2,1,0:T(8,128)S(1)}, u32[]{:S(2)}, u32[]{:S(2)}) %all-to-all-start.1) | async-done | bytes 524320 | tf_op jit(solution)/shard_map/all_to_all | solution.py:99
  91.0 0.9 broadcast_in_dim.55
  91.8 6.9 %all-to-all-start.2 = ((f32[16,8,1024]{2,1,0:T(8,128)}), f32[16,8,1024]{2,1,0:T(8,128)S(1)}, u32[]{:S(2)}, u32[]{:S(2)}) async-start(f32[16,8,1024]{2,1,0:T(8,128)} %broadcast_in_dim.55), calls=%async_computation.2 | async-start | bytes 1048576 | tf_op jit(solution)/shard_map/all_to_all | solution.py:101
  99.5 14.0 %all-to-all-done.2 = f32[16,8,1024]{2,1,0:T(8,128)S(1)} async-done(((f32[16,8,1024]{2,1,0:T(8,128)}), f32[16,8,1024]{2,1,0:T(8,128)S(1)}, u32[]{:S(2)}, u32[]{:S(2)}) %all-to-all-start.2) | async-done | bytes 524320 | tf_op jit(solution)/shard_map/all_to_all | solution.py:101
  113.5 5.1 %collective-permute-start.3 = (f32[16,8,1024]{2,1,0:T(8,128)S(1)}, f32[16,8,1024]{2,1,0:T(8,128)S(1)}, u32[]{:S(2)}, u32[]{:S(2)}) collective-permute-start(f32[16,8,1024]{2,1,0:T(8,128)S(1)} %all-to-all-done.2), channel_id=1, source_target_pairs={{0,1},{1,0},{2,3},{3,2},{4,5},{5,4},{6,7},{7,6},{8,9},{9,8},{10,11... | collective-permute-start | bytes 1572872 | tf_op jit(solution)/shard_map/ppermute | solution.py:104
  118.8 1.3 collective-permute-done.3
  120.7 1.3 convolution_bitcast_fusion
  122.0 1.3 convolution_bitcast_fusion.1
  123.4 0.9 maximum_divide_fusion
  124.3 1.2 copy.33
  125.7 0.8 copy-done.1
  126.5 23.5 %custom-call.16 = f32[2,128,128]{2,1,0:T(8,128)S(1)} custom-call(f32[2,128,128]{2,1,0:T(8,128)S(1)} %cholesky.122), custom_call_target="Cholesky" | custom-call | tf_op jit(solution)/shard_map/jit(cholesky)/cholesky | solution.py:31
  150.0 19.7 %custom-call.17 = f32[2,1,128,128]{2,3,1,0:T(8,128)S(1)} custom-call(f32[2,1,128,128]{3,2,1,0:T(8,128)S(1)} %select_bitcast_fusion), custom_call_target="InvertDiagBlocksLowerTriangular" | custom-call | tf_op jit(solution)/shard_map/jit(cholesky)/cholesky | solution.py:31
  169.7 1.2 constant_dynamic-update-slice_fusion.1
  170.9 1.3 convolution_subtract_fusion.2
  172.2 23.5 %custom-call.18 = f32[2,128,128]{2,1,0:T(8,128)S(1)} custom-call(f32[2,128,128]{2,1,0:T(8,128)S(1)} %convolution_subtract_fusion.2), custom_call_target="Cholesky" | custom-call | tf_op jit(solution)/shard_map/jit(cholesky)/cholesky | solution.py:31
  196.0 2.2 collective-permute-start.4
  198.4 4.3 %while.5 = (s32[]{:T(128)}, f32[256,256]{1,0:T(8,128)S(1)}, s32[2,2]{1,0:T(2,128)S(1)}, f32[2,128,128]{2,1,0:T(8,128)S(1)}, s32[]{:T(128)}) while((s32[]{:T(128)}, f32[256,256]{1,0:T(8,128)S(1)}, s32[2,2]{1,0:T(2,128)S(1)}, f32[2,128,128]{2,1,0:T(8,128)S(1)}, s32[]{:T(128)}) %tuple.56), condition=%wide.while_cond.clone, body=%wide.while_body.clone.sunk | while | flops 2 | bytes 131181 | solution.py:35
  198.6 0.6 fusion.123
  199.2 1.4 bitcast_dynamic-update-slice_fusion.5
  201.2 1.4 bitcast_dynamic-update-slice_fusion.5
  202.6 20.3 %custom-call.21 = f32[2,128,128]{1,2,0:T(8,128)} custom-call(f32[2,128,128]{2,1,0:T(8,128)S(1)} %get-tuple-element.18), custom_call_target="InvertDiagBlocksLowerTriangular" | custom-call | tf_op jit(solution)/shard_map/triangular_solve/custom-call.0 | solution.py:35
  222.9 1.2 fusion.54
  224.6 1.2 fusion.84
  225.8 0.7 cholesky.52.clone
  226.5 5.2 %while.4 = (s32[]{:T(128)}, f32[256,256]{1,0:T(8,128)S(1)}, s32[2,2]{1,0:T(2,128)S(1)}, f32[2,128,128]{2,1,0:T(8,128)}, s32[]{:T(128)}) while((s32[]{:T(128)}, f32[256,256]{1,0:T(8,128)S(1)}, s32[2,2]{1,0:T(2,128)S(1)}, f32[2,128,128]{2,1,0:T(8,128)}, s32[]{:T(128)}) %tuple.59), condition=%wide.while_cond, body=%wide.while_body.sunk | while | flops 2 | bytes 132705 | solution.py:32
  226.5 0.6 fusion.122
  227.1 2.0 bitcast_dynamic-update-slice_fusion.4
  229.1 0.6 fusion.122
  229.6 2.0 bitcast_dynamic-update-slice_fusion.4
  231.6 21.1 %custom-call.20 = f32[2,128,128]{1,2,0:T(8,128)} custom-call(f32[2,128,128]{2,1,0:T(8,128)} %get-tuple-element.17), custom_call_target="InvertDiagBlocksLowerTriangular" | custom-call | tf_op jit(solution)/shard_map/triangular_solve/custom-call.0 | solution.py:32
  252.7 1.2 fusion.56
  254.4 1.2 fusion.86
  256.0 0.8 copy.40
  256.8 2.3 convolution_bitcast_fusion.2
  (41 shorter events, 3.7 us)
Async XLA Ops:
  0.6 32.3 %copy-start = (f32[1,512,512]{2,1,0:T(8,128)S(1)}, f32[1,512,512]{2,1,0:T(8,128)}, u32[]{:S(2)}) copy-start(f32[1,512,512]{2,1,0:T(8,128)} %param.8) | copy-start | bytes 3145732
  2.4 28.9 %all-to-all-start = ((f32[8,16,1024]{2,1,0:T(8,128)}), f32[8,16,1024]{2,1,0:T(8,128)}, u32[]{:S(2)}, u32[]{:S(2)}) async-start(f32[8,16,1024]{2,1,0:T(8,128)} %broadcast_in_dim.54), calls=%async_computation | async-start | bytes 1048576 | tf_op jit(solution)/shard_map/all_to_all | solution.py:75
  36.4 9.8 %collective-permute-start = (f32[8,8,1024]{2,1,0:T(8,128)S(1)}, f32[8,8,1024]{2,1,0:T(8,128)S(1)}, u32[]{:S(2)}, u32[]{:S(2)}) collective-permute-start(f32[8,8,1024]{2,1,0:T(8,128)S(1)} %fusion.19), channel_id=1, source_target_pairs={{0,1},{1,0},{2,3},{3,2},{4,5},{5,4},{6,7},{7,6},{8,9},{9,8},{10,11... | collective-permute-start | bytes 786440 | tf_op jit(solution)/shard_map/ppermute | solution.py:95
  40.9 15.6 %collective-permute-start.1 = (f32[8,16,1024]{2,1,0:T(8,128)}, f32[8,16,1024]{2,1,0:T(8,128)S(1)}, u32[]{:S(2)}, u32[]{:S(2)}) collective-permute-start(f32[8,16,1024]{2,1,0:T(8,128)} %all-to-all-done), channel_id=1, source_target_pairs={{0,16},{16,0},{1,17},{17,1},{2,18},{18,2},{3,19},{19,3},{4,20},{20... | collective-permute-start | bytes 1572872 | tf_op jit(solution)/shard_map/ppermute | solution.py:78
  60.7 4.0 %collective-permute-start.2 = (f32[8,8,1024]{2,1,0:T(8,128)S(1)}, f32[8,8,1024]{2,1,0:T(8,128)S(1)}, u32[]{:S(2)}, u32[]{:S(2)}) collective-permute-start(f32[8,8,1024]{2,1,0:T(8,128)S(1)} %fusion.23), channel_id=1, source_target_pairs={{0,1},{1,0},{2,3},{3,2},{4,5},{5,4},{6,7},{7,6},{8,9},{9,8},{10,11... | collective-permute-start | bytes 786440 | tf_op jit(solution)/shard_map/ppermute | solution.py:95
  66.3 24.6 %all-to-all-start.1 = ((f32[16,8,1024]{2,1,0:T(8,128)}), f32[16,8,1024]{2,1,0:T(8,128)S(1)}, u32[]{:S(2)}, u32[]{:S(2)}) async-start(f32[16,8,1024]{2,1,0:T(8,128)} %pad_maximum_fusion), calls=%async_computation.1 | async-start | bytes 1048576 | tf_op jit(solution)/shard_map/all_to_all | solution.py:99
  91.8 21.7 %all-to-all-start.2 = ((f32[16,8,1024]{2,1,0:T(8,128)}), f32[16,8,1024]{2,1,0:T(8,128)S(1)}, u32[]{:S(2)}, u32[]{:S(2)}) async-start(f32[16,8,1024]{2,1,0:T(8,128)} %broadcast_in_dim.55), calls=%async_computation.2 | async-start | bytes 1048576 | tf_op jit(solution)/shard_map/all_to_all | solution.py:101
  113.5 6.6 %collective-permute-start.3 = (f32[16,8,1024]{2,1,0:T(8,128)S(1)}, f32[16,8,1024]{2,1,0:T(8,128)S(1)}, u32[]{:S(2)}, u32[]{:S(2)}) collective-permute-start(f32[16,8,1024]{2,1,0:T(8,128)S(1)} %all-to-all-done.2), channel_id=1, source_target_pairs={{0,1},{1,0},{2,3},{3,2},{4,5},{5,4},{6,7},{7,6},{8,9},{9,8},{10,11... | collective-permute-start | bytes 1572872 | tf_op jit(solution)/shard_map/ppermute | solution.py:104
  125.7 0.8 copy-start.1
  196.0 60.8 %collective-permute-start.4 = (f32[2,256,256]{2,1,0:T(8,128)S(1)}, f32[2,256,256]{2,1,0:T(8,128)}, u32[]{:S(2)}, u32[]{:S(2)}) collective-permute-start(f32[2,256,256]{2,1,0:T(8,128)S(1)} %select_select_fusion), channel_id=1, source_target_pairs={{0,16},{16,0},{1,17},{17,1},{2,18},{18,2},{3,19},{19,3},{4,20},{20... | collective-permute-start | bytes 1572872 | tf_op jit(solution)/shard_map/ppermute | solution.py:116

commit v2 on v1

v2 whole, which is shorter than its diff:
```python
import jax
import jax.numpy as jnp
from jax import lax
from jax.experimental import pallas as pl
from jax.experimental.pallas import tpu as pltpu
from jax.sharding import Mesh, PartitionSpec as P

R = 256
BT = 256
HALF = 128

f32, bf16 = jnp.float32, jnp.bfloat16
highest = lax.Precision.HIGHEST
SWAP = [(0, 1), (1, 0)]
NT = (((1,), (1,)), ((), ()))
TN = (((0,), (0,)), ((), ()))
VMEM = pl.BlockSpec(memory_space=pltpu.VMEM)
SMEM = pl.BlockSpec(memory_space=pltpu.SMEM)
PARAMS = pltpu.CompilerParams(vmem_limit_bytes=40 << 20)


def shape(*sizes, dtype=f32):
    return jax.ShapeDtypeStruct(sizes, dtype)


def dot(a, b, dims, precision=None):
    return lax.dot_general(a, b, dims, precision=precision, preferred_element_type=f32)


def two_parts(a):
    top = a.astype(bf16)
    return top, (a - top.astype(f32)).astype(bf16)


def operator_kernel(scalars, pattern, contrib, assembled, columns, targets, top, low, c_top, c_low, pick):
    step = pl.program_id(0)
    rows, cols = top.shape
    child = scalars[0]

    @pl.when(step == 0)
    def _():
        c_top[...], c_low[...] = two_parts(contrib[...])
        places = lax.broadcasted_iota(jnp.int32, pick.shape, 0)
        pick[...] = (places == columns[...]).astype(f32).astype(bf16)

    places = lax.broadcasted_iota(jnp.int32, (rows, targets.shape[1]), 0) + step * rows
    spread = (places == targets[...]).astype(f32).astype(bf16)
    high_rows = dot(spread, c_top[...], (((1,), (0,)), ((), ()))).astype(bf16)
    low_rows = dot(spread, c_low[...], (((1,), (0,)), ((), ()))).astype(bf16)
    total = dot(high_rows, pick[...], NT) + dot(low_rows, pick[...], NT)
    per_half = pl.num_programs(0) // 2
    here = (step // per_half == child).astype(f32)
    tile_row = child * per_half + step % per_half
    for tile in range(cols // BT):
        lanes = slice(tile * BT, (tile + 1) * BT)
        keep = pattern[tile_row, tile].astype(f32) * here
        top[:, lanes], low[:, lanes] = two_parts(total[:, lanes] + assembled[:, lanes] * keep)


def build_operator(scalars, pattern, contrib, assembled, columns, targets):
    tile_rows, tile_cols = contrib.shape
    window_rows = assembled.shape[1]
    steps = window_rows // BT
    block = pl.BlockSpec((BT, window_rows), lambda i: (i, 0))
    return pl.pallas_call(
        operator_kernel,
        grid=(steps,),
        in_specs=[
            SMEM,
            SMEM,
            pl.BlockSpec((tile_rows, tile_cols), lambda i: (0, 0)),
            pl.BlockSpec((BT, window_rows), lambda i: (i % (steps // 2), 0)),
            pl.BlockSpec((1, tile_cols), lambda i: (0, 0)),
            pl.BlockSpec((1, tile_rows), lambda i: (0, 0)),
        ],
        out_specs=[block, block],
        out_shape=[shape(window_rows, window_rows, dtype=bf16)] * 2,
        scratch_shapes=[
            pltpu.VMEM((tile_rows, tile_cols), bf16),
            pltpu.VMEM((tile_rows, tile_cols), bf16),
            pltpu.VMEM((window_rows, tile_cols), bf16),
        ],
        compiler_params=PARAMS,
        cost_estimate=pl.CostEstimate(flops=4 * 10**9, bytes_accessed=8 * 10**6, transcendentals=0),
    )(scalars, pattern, contrib, assembled, columns, targets)


def apply_kernel(scalars, lines, top, low, give, keep, h_top, h_low):
    core = scalars[2]
    count, _, width, depth = lines.shape

    @pl.when(pl.program_id(0) == 0)
    def _():
        both = jnp.concatenate(
            [lines[:, pl.ds(1 - core, 1)].reshape(-1, depth), lines[:, pl.ds(core, 1)].reshape(-1, depth)]
        )
        h_top[...], h_low[...] = two_parts(both)

    out = (
        dot(h_top[...], top[...], NT) + dot(h_top[...], low[...], NT) + dot(h_low[...], top[...], NT)
    )
    give[...] = out[: count * width].reshape(give.shape)
    keep[...] = out[count * width :].reshape(keep.shape)


def apply_operator(scalars, gathered, top, low):
    count, both, depth = gathered.shape
    width = both // 2
    window_rows = top.shape[0]
    lines = gathered.reshape(count, 2, width, depth)
    out_block = pl.BlockSpec((count, width, BT), lambda i: (0, 0, i))
    in_block = pl.BlockSpec((BT, depth), lambda i: (i, 0))
    return pl.pallas_call(
        apply_kernel,
        grid=(window_rows // BT,),
        in_specs=[SMEM, pl.BlockSpec(lines.shape, lambda i: (0, 0, 0, 0)), in_block, in_block],
        out_specs=[out_block, out_block],
        out_shape=[shape(count, width, window_rows)] * 2,
        scratch_shapes=[pltpu.VMEM((count * both, depth), bf16)] * 2,
        compiler_params=PARAMS,
        cost_estimate=pl.CostEstimate(flops=10**9, bytes_accessed=6 * 10**6, transcendentals=0),
    )(scalars, lines, top, low)


def rank_update(u):
    a = u.astype(bf16).astype(f32)
    b = (u - a).astype(bf16).astype(f32)
    c = u - a - b
    left = jnp.concatenate([a, a, b, b, a, c], 0).astype(bf16)
    right = jnp.concatenate([a, b, a, b, c, a], 0).astype(bf16)
    return dot(left[:, :HALF], right, TN)


def factor_panel(block, r):
    panel = block[pl.ds(r, 8), :]
    tiles = panel.shape[1] // 128
    pivot = pltpu.roll(panel[:, :128], 128 - r, 1)
    rows = [
        [jnp.broadcast_to(panel[j : j + 1, t * 128 : (t + 1) * 128], (8, 128)) for t in range(tiles)]
        for j in range(8)
    ]
    spread = [jnp.broadcast_to(pivot[j : j + 1], (8, 128)) for j in range(8)]
    a = [
        [jnp.broadcast_to(spread[j][:, i : i + 1], (8, 128)) if i >= j else None for j in range(8)]
        for i in range(8)
    ]
    for j in range(8):
        inverse = lax.rsqrt(a[j][j])
        column = {i: a[i][j] * inverse for i in range(j + 1, 8)}
        for k in range(j + 1, 8):
            for i in range(k, 8):
                a[i][k] = a[i][k] - column[i] * column[k]
        rows[j] = [v * inverse for v in rows[j]]
        for k in range(j + 1, 8):
            rows[k] = [v - column[k] * w for v, w in zip(rows[k], rows[j])]
    sub = lax.broadcasted_iota(jnp.int32, (8, 128), 0)
    lane = lax.broadcasted_iota(jnp.int32, (8, 128), 1)
    out = []
    for t in range(tiles):
        u = rows[7][t]
        for j in range(7):
            u = jnp.where(sub == j, rows[j][t], u)
        if t == 0:
            u = jnp.where(lane >= sub + r, u, 0.0)
        out.append(u)
    return jnp.concatenate(out, 1)


def unit(size):
    return (
        lax.broadcasted_iota(jnp.int32, (size, size), 0) == lax.broadcasted_iota(jnp.int32, (size, size), 1)
    ).astype(f32)


def factor_block(blocks, store):
    def panel(p, carry):
        r = pl.multiple_of(p * 8, 8)
        for leaf, block in enumerate(blocks):
            u = factor_panel(block, r)
            store(leaf, r, u)
            block[...] -= rank_update(u)
        return carry

    lax.fori_loop(0, HALF // 8, panel, 0)


def head_kernel(scalars, mine, theirs, window, u_head, x_head, rest, gram, s0, s1):
    xl, core, bound = scalars[1], scalars[2], scalars[3]
    count = mine.shape[0] // 2
    window_rows = mine.shape[2]
    for block in range(2 * count):
        start = block % count * 32 + (block // count ^ xl) * 16
        window[pl.ds(pl.multiple_of(start + core * 8, 8), 8), :] = mine[block]
        window[pl.ds(pl.multiple_of(start + (1 - core) * 8, 8), 8), :] = theirs[block]
    edge = window_rows // 2 + HALF
    lane = lax.broadcasted_iota(jnp.int32, (R, edge), 1)
    head = window[:, :edge]
    tail = window[:, window_rows - edge :]
    gram[0] = dot(jnp.where(lane < bound, head, 0.0), head, NT, highest)
    gram[1] = dot(jnp.where(lane + (window_rows - edge) < bound, 0.0, tail), tail, NT, highest)
    blocks = (s0, s1)
    for leaf in range(2):
        rows = jnp.where(leaf == 0, bound, window_rows - bound)
        count_rows = jnp.full((1, 1), rows, jnp.int32).astype(f32)
        gram[leaf] = gram[leaf] / count_rows
        blocks[leaf][:, :R] = gram[leaf, :HALF, :]
        blocks[leaf][:, R:] = unit(HALF)

    def store(leaf, r, u):
        u_head[leaf, pl.ds(r, 8), :] = u[:, :R]
        x_head[leaf, pl.ds(r, 8), :] = u[:, R:]

    factor_block(blocks, store)
    for leaf in range(2):
        side = u_head[leaf, :, HALF:]
        change = dot(side, jnp.concatenate([side, x_head[leaf]], 1), TN, highest)
        rest[leaf, :, :HALF] = gram[leaf, HALF:, HALF:] - change[:, :HALF]
        rest[leaf, :, HALF:] = -change[:, HALF:]


def factor_head(scalars, mine, theirs):
    window_rows = mine.shape[2]
    return pl.pallas_call(
        head_kernel,
        in_specs=[SMEM, VMEM, VMEM],
        out_specs=[VMEM] * 4,
        out_shape=[
            shape(R, window_rows),
            shape(2, HALF, R),
            shape(2, HALF, HALF),
            shape(2, HALF, R),
        ],
        scratch_shapes=[pltpu.VMEM((2, R, R), f32)] + [pltpu.VMEM((HALF, R + HALF), f32)] * 2,
        compiler_params=PARAMS,
    )(scalars, mine, theirs)


def tail_kernel(scalars, u_head, x_head, rest, u_tail, u_own, x_own, x_tail, s0, s1):
    group = scalars[4]
    blocks = (s0, s1)
    for leaf in range(2):
        blocks[leaf][:, :R] = rest[leaf]
        blocks[leaf][:, R:] = unit(HALF)

    def store(leaf, r, u):
        u_tail[leaf, pl.ds(r, 8), :] = u[:, :HALF]
        x_tail[leaf, pl.ds(r, 8), :] = u[:, HALF:]

    factor_block(blocks, store)
    start = pl.multiple_of(group % (HALF // 8) * 8, 8)
    in_head = group < HALF // 8
    for leaf in range(2):
        own = pl.ds(start, 8)
        zero = jnp.zeros((8, HALF), f32)
        u_own[leaf] = jnp.where(
            in_head, u_head[leaf, own, :], jnp.concatenate([zero, u_tail[leaf, own, :]], 1)
        )
        x_own[leaf] = jnp.where(
            in_head, jnp.concatenate([x_head[leaf, own, :], zero], 1), x_tail[leaf, own, :]
        )


def factor_tail(scalars, u_head, x_head, rest):
    return pl.pallas_call(
        tail_kernel,
        in_specs=[SMEM] + [VMEM] * 3,
        out_specs=[VMEM] * 3,
        out_shape=[shape(2, HALF, HALF), shape(2, 8, R), shape(2, 8, R)],
        scratch_shapes=[pltpu.VMEM((2, HALF, R), f32)] + [pltpu.VMEM((HALF, R + HALF), f32)] * 2,
        compiler_params=PARAMS,
        cost_estimate=pl.CostEstimate(flops=8 * 10**9, bytes_accessed=10**6, transcendentals=0),
    )(scalars, u_head, x_head, rest)


def bases_kernel(scalars, window, x_own, out):
    both = jnp.concatenate([x_own[0], x_own[1]], 0)
    solved = dot(both, window[...], (((1,), (0,)), ((), ())), highest)
    lane = lax.broadcasted_iota(jnp.int32, out.shape, 1)
    out[...] = jnp.where(lane < scalars[3], solved[:8], solved[8:])


def coupling_kernel(u_own, sib_head, sib_tail, out):
    for leaf in range(2):
        own = u_own[leaf]
        out[leaf, :, :HALF] = dot(own, sib_head[leaf], NT, highest)
        out[leaf, :, HALF:] = dot(own[:, HALF:], sib_tail[leaf], NT, highest)


def local(contrib, assembled, pattern, omega, row_maps, leaf_bounds):
    tile_rows, tile_cols = contrib.shape[1:]
    window_rows, own_count = omega.shape
    z_count = lax.axis_size("z")
    groups = lax.axis_size("child") * lax.axis_size("y")
    width = R // (2 * groups)
    child = lax.axis_index("child")
    row_pos = lax.axis_index(("z", "xl"))
    col_pos = lax.axis_index(("y", "core"))
    columns = lax.dynamic_slice_in_dim(row_maps, col_pos * tile_cols, tile_cols, 1) - col_pos * window_rows
    targets = lax.dynamic_slice_in_dim(row_maps, row_pos * tile_rows, tile_rows, 1) - row_pos * window_rows
    scalars = jnp.stack(
        [
            child,
            lax.axis_index("xl"),
            lax.axis_index("core"),
            leaf_bounds[0],
            lax.axis_index(("child", "y", "core")),
        ]
    ).astype(jnp.int32)

    own = lax.all_to_all(jnp.broadcast_to(omega.T, (z_count, own_count, window_rows)), "z", 0, 0)
    top, low = build_operator(scalars, pattern, contrib[0], assembled[0], columns, targets)
    other = lax.ppermute(own, "xl", SWAP)

    def half(gathered):
        give, keep = apply_operator(scalars, gathered, top, low)
        return keep + lax.ppermute(give, "core", SWAP)

    parts = jnp.concatenate([half(own), half(other)], axis=0)
    terms = lax.all_to_all(parts, ("child", "y"), 0, 0)
    samples = jnp.sum(terms, axis=0)
    mine = lax.all_to_all(
        jnp.broadcast_to(samples, (groups, width, window_rows)), ("child", "y"), 0, 0
    )
    theirs = lax.ppermute(mine, "core", SWAP)

    window, u_head, x_head, rest = factor_head(scalars, mine, theirs)
    sib_head = lax.ppermute(u_head, "xl", SWAP)
    u_tail, u_own, x_own = factor_tail(scalars, u_head, x_head, rest)
    sib_tail = lax.ppermute(u_tail, "xl", SWAP)
    bases = pl.pallas_call(
        bases_kernel,
        in_specs=[SMEM, VMEM, VMEM],
        out_specs=VMEM,
        out_shape=shape(width, window_rows),
        compiler_params=PARAMS,
        cost_estimate=pl.CostEstimate(flops=10**9, bytes_accessed=10**6, transcendentals=0),
    )(scalars, window, x_own)
    coupling = pl.pallas_call(
        coupling_kernel,
        in_specs=[VMEM] * 3,
        out_specs=VMEM,
        out_shape=shape(2, width, R),
        compiler_params=PARAMS,
    )(u_own, sib_head, sib_tail)
    return (bases.T, coupling[None])


def solution(mesh):
    fine = Mesh(mesh.devices.reshape(2, 8, 2, 8, 2), ("child", "z", "xl", "y", "core"))
    row, col = ("z", "xl"), ("y", "core")
    in_specs = (
        P("child", row, col),
        P("child", row, col),
        P(row, col),
        P(col, row),
        P("child", None),
        P(row),
    )
    out_specs = (P(row, ("child",) + col), P(row, None, ("child",) + col, None))
    return jax.shard_map(local, mesh=fine, in_specs=in_specs, out_specs=out_specs, check_vma=False)
```

time: 260 us -> 140 us (0.54)
  other arithmetic: 115 us -> 0.84 us
  blocking collectives: 0 us -> 45.3 us
  Pallas kernels: 0 us -> 35 us
  matrix products: 29.5 us -> 0 us
  waiting for transfers between devices: 51.5 us -> 22.2 us
  starting transfers between devices: 42.7 us -> 29 us
  local copies, waits for them, and re-layouts: 18.4 us -> 5.31 us
    another operation x15 -> x0, other arithmetic: 108 us -> none  [the longest x9 66.8 us: window_leaves(): factors = jnp.linalg.cholesky(jnp.stack([head_gram, tail_gram]) / counts)]
    all_to_all x0 -> x2, blocking collectives: none -> 45.3 us  [the longest x1 24.1 us: local(): terms = lax.all_to_all(parts, ('child', 'y'), 0, 0)]
    pallas_call x0 -> x7, Pallas kernels: none -> 35 us  [the longest x1 11.1 us: factor_head(): pl.pallas_call(head_kernel, in_specs=[SMEM, VMEM, VMEM], out_specs=[VMEM]...]
    all_to_all x3 -> x1, waiting for transfers between devices: 40.7 us -> 18 us  [local(): lax.all_to_all(jnp.broadcast_to(omega.T, (z_count, own_count, window_rows...]
    dot_general x19 -> x0, matrix products: 21.3 us -> none  [the longest x8 8.72 us: dot_nt(): return lax.dot_general(a, b, (((1,), (1,)), ((), ())), precision=precision)]
    all_to_all x3 -> x1, starting transfers between devices: 27.2 us -> 10.9 us  [local(): lax.all_to_all(jnp.broadcast_to(omega.T, (z_count, own_count, window_rows...]
    another operation x17 -> x1, local copies, waits for them, and re-layouts: 9.95 us -> 0.08 us  [local(): jnp.stack([child, lax.axis_index('xl'), lax.axis_index('core'), leaf_boun...]
    ppermute x1, waiting for transfers between devices: 9.5 us -> 0.01 us  [local(): other = lax.ppermute(own, 'xl', SWAP)]
  transfers between devices with their start and end apart: 8 -> 7, of which waited for: 5 -> 4; matrix products, arithmetic and copies ran while one was open for 28% -> 1% of each run, Pallas kernels for 0% -> 16%
where the time goes in v2:
time: 140 us; the launch traced here: 139 us
  blocking collectives  45.3 us (32%)
  Pallas kernels  35 us (25%)
  starting transfers between devices  29 us (21%)
  waiting for transfers between devices  22.2 us (16%)
  local copies, waits for them, and re-layouts  5.31 us (4%)
  between operations  1.42 us (1%)
    all_to_all x1, blocking collectives, local(): terms = lax.all_to_all(parts, ('child', 'y'), 0, 0)  24.1 us
    all_to_all x1, blocking collectives, local(): lax.all_to_all(jnp.broadcast_to(samples, (groups, width, window_rows)), (...  21.2 us
    all_to_all x1, waiting for transfers between devices, local(): lax.all_to_all(jnp.broadcast_to(omega.T, (z_count, own_count, window_rows...  18 us
    pallas_call x1, Pallas kernels, factor_head(): pl.pallas_call(head_kernel, in_specs=[SMEM, VMEM, VMEM], out_specs=[VMEM]...  11.1 us
    all_to_all x1, starting transfers between devices, local(): lax.all_to_all(jnp.broadcast_to(omega.T, (z_count, own_count, window_rows...  10.9 us
    pallas_call x1, Pallas kernels, factor_tail(): pl.pallas_call(tail_kernel, in_specs=[SMEM] + [VMEM] * 3, out_specs=[VMEM...  9.06 us
    pallas_call x2, Pallas kernels, apply_operator(): pl.pallas_call(apply_kernel, grid=(window_rows // BT,), in_specs=[SMEM, p...  6.62 us
    pallas_call x1, Pallas kernels, build_operator(): pl.pallas_call(operator_kernel, grid=(steps,), in_specs=[SMEM, SMEM, pl.B...  5.34 us
  transfers between devices with their start and end apart: 7, of which 4 were waited for; matrix products, arithmetic and copies ran while one was open for 1% of the time, Pallas kernels for 16%

profile of v2, /device:TPU:1, one launch (start us, length us, event | category | flops | bytes accessed | tf_op | source)
XLA Modules:
  0.0 139.0 jit_solution(9227753313182200699)
XLA Ops:
  0.6 1.7 %broadcast_in_dim.9 = f32[8,16,1024]{2,1,0:T(8,128)} broadcast(f32[16,1024]{1,0:T(8,128)} %bitcast.15), dimensions={1,2} | broadcast | bytes 589824 | tf_op jit(solution)/shard_map/broadcast_in_dim | solution.py:310
  2.3 10.9 %all-to-all-start = ((f32[8,16,1024]{2,1,0:T(8,128)}), f32[8,16,1024]{2,1,0:T(8,128)S(1)}, u32[]{:S(2)}, u32[]{:S(2)}) async-start(f32[8,16,1024]{2,1,0:T(8,128)} %broadcast_in_dim.9), calls=%async_computation | async-start | bytes 1048576 | tf_op jit(solution)/shard_map/all_to_all | solution.py:310
  13.2 18.0 %all-to-all-done = f32[8,16,1024]{2,1,0:T(8,128)S(1)} async-done(((f32[8,16,1024]{2,1,0:T(8,128)}), f32[8,16,1024]{2,1,0:T(8,128)S(1)}, u32[]{:S(2)}, u32[]{:S(2)}) %all-to-all-start) | async-done | bytes 524320 | tf_op jit(solution)/shard_map/all_to_all | solution.py:310
  31.1 3.1 %collective-permute-start.1 = (f32[8,16,1024]{2,1,0:T(8,128)S(1)}, f32[8,16,1024]{2,1,0:T(8,128)S(1)}, u32[]{:S(2)}, u32[]{:S(2)}) collective-permute-start(f32[8,16,1024]{2,1,0:T(8,128)S(1)} %all-to-all-done), channel_id=1, source_target_pairs={{0,16},{16,0},{1,17},{17,1},{2,18},{18,2},{3,19},{19,3},{4,20},{20... | collective-permute-start | bytes 1572872 | tf_op jit(solution)/shard_map/ppermute | solution.py:312
  34.2 0.7 dynamic-slice_subtract_fusion
  35.6 0.1 stack.19.scalars
  35.7 0.0 copy-start
  35.7 1.6 %copy-done = f32[1,512,1024]{2,1,0:T(8,128)S(1)} copy-done((f32[1,512,1024]{2,1,0:T(8,128)S(1)}, f32[1,512,1024]{2,1,0:T(8,128)}, u32[]{:S(2)}) %copy-start) | copy-done | bytes 2097176
  37.3 0.0 copy-start.1
  37.3 1.2 copy-done.1
  38.5 0.0 copy-start.2
  38.5 0.7 copy-done.2
  39.2 5.3 %shard_map.77 = (bf16[1024,1024]{1,0:T(8,128)(2,1)S(1)}, bf16[1024,1024]{1,0:T(8,128)(2,1)S(1)}) custom-call(s32[5]{0:T(128)S(1)} %stack.19.scalars, s32[4,4]{1,0:T(4,128)S(1)} %copy-done.2, f32[512,512]{1,0:T(8,128)S(1)} %bitcast.14, f32[512,1024]{1,0:T(8,128)S(1)} %bitcast.13, s32[1,512]{1,0:T(1,128)S(1)} %get-tuple-element.29.columns, ...), custom_call_target="tpu_custom_call" | custom-call | flops 4000000000 | bytes 8000000 | tf_op jit(solution)/shard_map/pallas_call | solution.py:65
  44.5 3.3 %shard_map.78 = (f32[8,8,1024]{2,1,0:T(8,128)S(1)}, f32[8,8,1024]{2,1,0:T(8,128)S(1)}) custom-call(s32[5]{0:T(128)S(1)} %stack.19.scalars, f32[8,2,8,1024]{3,2,1,0:T(8,128)S(1)} %bitcast.11, bf16[1024,1024]{1,0:T(8,128)(2,1)S(1)} %get-tuple-element.15.top, bf16[1024,1024]{1,0:T(8,128)(2,1)S(1)} %get-tuple-element.16.low), custom_call_target="tpu_custom_call" | custom-call | flops 1000000000 | bytes 6000000 | tf_op jit(solution)/shard_map/pallas_call | solution.py:113
  47.9 2.7 %collective-permute-start = (f32[8,8,1024]{2,1,0:T(8,128)S(1)}, f32[8,8,1024]{2,1,0:T(8,128)S(1)}, u32[]{:S(2)}, u32[]{:S(2)}) collective-permute-start(f32[8,8,1024]{2,1,0:T(8,128)S(1)} %get-tuple-element.18), channel_id=1, source_target_pairs={{0,1},{1,0},{2,3},{3,2},{4,5},{5,4},{6,7},{7,6},{8,9},{9,8},{10,11... | collective-permute-start | bytes 786440 | tf_op jit(solution)/shard_map/ppermute | solution.py:316
  50.6 0.0 collective-permute-done.1
  50.6 3.3 %shard_map.79 = (f32[8,8,1024]{2,1,0:T(8,128)S(1)}, f32[8,8,1024]{2,1,0:T(8,128)S(1)}) custom-call(s32[5]{0:T(128)S(1)} %stack.19.scalars, f32[8,2,8,1024]{3,2,1,0:T(8,128)S(1)} %bitcast.12, bf16[1024,1024]{1,0:T(8,128)(2,1)S(1)} %get-tuple-element.15.top, bf16[1024,1024]{1,0:T(8,128)(2,1)S(1)} %get-tuple-element.16.low), custom_call_target="tpu_custom_call" | custom-call | flops 1000000000 | bytes 6000000 | tf_op jit(solution)/shard_map/pallas_call | solution.py:113
  53.9 1.9 %collective-permute-start.2 = (f32[8,8,1024]{2,1,0:T(8,128)S(1)}, f32[8,8,1024]{2,1,0:T(8,128)S(1)}, u32[]{:S(2)}, u32[]{:S(2)}) collective-permute-start(f32[8,8,1024]{2,1,0:T(8,128)S(1)} %get-tuple-element.20), channel_id=1, source_target_pairs={{0,1},{1,0},{2,3},{3,2},{4,5},{5,4},{6,7},{7,6},{8,9},{9,8},{10,11... | collective-permute-start | bytes 786440 | tf_op jit(solution)/shard_map/ppermute | solution.py:316
  55.9 0.0 collective-permute-done
  55.9 1.4 %collective-permute-done.2 = f32[8,8,1024]{2,1,0:T(8,128)S(1)} collective-permute-done((f32[8,8,1024]{2,1,0:T(8,128)S(1)}, f32[8,8,1024]{2,1,0:T(8,128)S(1)}, u32[]{:S(2)}, u32[]{:S(2)}) %collective-permute-start.2) | collective-permute-done | bytes 262176 | tf_op jit(solution)/shard_map/ppermute | solution.py:316
  57.5 24.1 %all_to_all.15 = f32[16,8,1024]{2,1,0:T(8,128)S(1)} all-to-all(f32[16,8,1024]{2,1,0:T(8,128)S(1)} %pad_maximum_fusion), channel_id=1, replica_groups=mesh['child'=2,'z'=8,'xl'=2,'y'=8,'core'=2] {'child','y'}, dimensions={0} | all-to-all | bytes 1048576 | tf_op jit(solution)/shard_map/all_to_all | solution.py:319
  81.7 21.2 %all_to_all.16.mine = f32[16,8,1024]{2,1,0:T(8,128)S(1)} all-to-all(f32[16,8,1024]{2,1,0:T(8,128)S(1)} %broadcast_in_dim.10), channel_id=1, replica_groups=mesh['child'=2,'z'=8,'xl'=2,'y'=8,'core'=2] {'child','y'}, dimensions={0} | all-to-all | bytes 1048576 | tf_op jit(solution)/shard_map/all_to_all | solution.py:321
  102.8 5.1 %collective-permute-start.3 = (f32[16,8,1024]{2,1,0:T(8,128)S(1)}, f32[16,8,1024]{2,1,0:T(8,128)S(1)}, u32[]{:S(2)}, u32[]{:S(2)}) collective-permute-start(f32[16,8,1024]{2,1,0:T(8,128)S(1)} %all_to_all.16.mine), channel_id=1, source_target_pairs={{0,1},{1,0},{2,3},{3,2},{4,5},{5,4},{6,7},{7,6},{8,9},{9,8},{10,11... | collective-permute-start | bytes 1572872 | tf_op jit(solution)/shard_map/ppermute | solution.py:324
  107.9 1.5 %collective-permute-done.3.theirs = f32[16,8,1024]{2,1,0:T(8,128)S(1)} collective-permute-done((f32[16,8,1024]{2,1,0:T(8,128)S(1)}, f32[16,8,1024]{2,1,0:T(8,128)S(1)}, u32[]{:S(2)}, u32[]{:S(2)}) %collective-permute-start.3) | collective-permute-done | bytes 524320 | tf_op jit(solution)/shard_map/ppermute | solution.py:324
  109.4 11.1 %shard_map.80 = (f32[256,1024]{1,0:T(8,128)S(1)}, f32[2,128,256]{2,1,0:T(8,128)S(1)}, f32[2,128,128]{2,1,0:T(8,128)S(1)}, f32[2,128,256]{2,1,0:T(8,128)S(1)}) custom-call(s32[5]{0:T(128)S(1)} %stack.19.scalars, f32[16,8,1024]{2,1,0:T(8,128)S(1)} %all_to_all.16.mine, f32[16,8,1024]{2,1,0:T(8,128)S(1)} %collective-permute-done.3.theirs), custom_call_target="tpu_custom_call" | custom-call | tf_op jit(solution)/shard_map/pallas_call | solution.py:223
  120.5 1.9 %collective-permute-start.4 = (f32[2,128,256]{2,1,0:T(8,128)S(1)}, f32[2,128,256]{2,1,0:T(8,128)S(1)}, u32[]{:S(2)}, u32[]{:S(2)}) collective-permute-start(f32[2,128,256]{2,1,0:T(8,128)S(1)} %get-tuple-element.22.u_head), channel_id=1, source_target_pairs={{0,16},{16,0},{1,17},{17,1},{2,18},{18,2},{3,19},{19,3},{4,20},{20... | collective-permute-start | bytes 786440 | tf_op jit(solution)/shard_map/ppermute | solution.py:327
  122.4 9.1 %shard_map.81 = (f32[2,128,128]{2,1,0:T(8,128)S(1)}, f32[2,8,256]{2,1,0:T(8,128)S(1)}, f32[2,8,256]{2,1,0:T(8,128)S(1)}) custom-call(s32[5]{0:T(128)S(1)} %stack.19.scalars, f32[2,128,256]{2,1,0:T(8,128)S(1)} %get-tuple-element.22.u_head, f32[2,128,128]{2,1,0:T(8,128)S(1)} %get-tuple-element.23.x_head, f32[2,128,256]{2,1,0:T(8,128)S(1)} %get-tuple-element.24.rest), custom_call_target="tpu_custom_call" | custom-call | flops 8000000000 | bytes 1000000 | tf_op jit(solution)/shard_map/pallas_call | solution.py:264
  131.5 3.4 %collective-permute-start.5 = (f32[2,128,128]{2,1,0:T(8,128)S(1)}, f32[2,128,128]{2,1,0:T(8,128)S(1)}, u32[]{:S(2)}, u32[]{:S(2)}) collective-permute-start(f32[2,128,128]{2,1,0:T(8,128)S(1)} %get-tuple-element.27), channel_id=1, source_target_pairs={{0,16},{16,0},{1,17},{17,1},{2,18},{18,2},{3,19},{19,3},{4,20},{20... | collective-permute-start | bytes 393224 | tf_op jit(solution)/shard_map/ppermute | solution.py:329
  134.9 1.8 %shard_map.82 = f32[8,1024]{1,0:T(8,128)} custom-call(s32[5]{0:T(128)S(1)} %stack.19.scalars, f32[256,1024]{1,0:T(8,128)S(1)} %get-tuple-element.21.window, f32[2,8,256]{2,1,0:T(8,128)S(1)} %get-tuple-element.25.x_own), custom_call_target="tpu_custom_call" | custom-call | flops 1000000000 | bytes 1000000 | tf_op jit(solution)/shard_map/pallas_call | solution.py:330
  136.6 1.2 collective-permute-done.5.sib_tail
  137.9 0.0 collective-permute-done.4.sib_head
  137.9 1.1 shard_map.83
  (5 shorter events, 0.2 us)
Async XLA Ops:
  2.3 28.8 %all-to-all-start = ((f32[8,16,1024]{2,1,0:T(8,128)}), f32[8,16,1024]{2,1,0:T(8,128)S(1)}, u32[]{:S(2)}, u32[]{:S(2)}) async-start(f32[8,16,1024]{2,1,0:T(8,128)} %broadcast_in_dim.9), calls=%async_computation | async-start | bytes 1048576 | tf_op jit(solution)/shard_map/all_to_all | solution.py:310
  31.1 19.5 %collective-permute-start.1 = (f32[8,16,1024]{2,1,0:T(8,128)S(1)}, f32[8,16,1024]{2,1,0:T(8,128)S(1)}, u32[]{:S(2)}, u32[]{:S(2)}) collective-permute-start(f32[8,16,1024]{2,1,0:T(8,128)S(1)} %all-to-all-done), channel_id=1, source_target_pairs={{0,16},{16,0},{1,17},{17,1},{2,18},{18,2},{3,19},{19,3},{4,20},{20... | collective-permute-start | bytes 1572872 | tf_op jit(solution)/shard_map/ppermute | solution.py:312
  35.7 1.6 %copy-start = (f32[1,512,1024]{2,1,0:T(8,128)S(1)}, f32[1,512,1024]{2,1,0:T(8,128)}, u32[]{:S(2)}) copy-start(f32[1,512,1024]{2,1,0:T(8,128)} %param.7) | copy-start | bytes 6291460
  37.3 1.2 copy-start.1
  38.5 0.7 copy-start.2
  47.9 8.0 %collective-permute-start = (f32[8,8,1024]{2,1,0:T(8,128)S(1)}, f32[8,8,1024]{2,1,0:T(8,128)S(1)}, u32[]{:S(2)}, u32[]{:S(2)}) collective-permute-start(f32[8,8,1024]{2,1,0:T(8,128)S(1)} %get-tuple-element.18), channel_id=1, source_target_pairs={{0,1},{1,0},{2,3},{3,2},{4,5},{5,4},{6,7},{7,6},{8,9},{9,8},{10,11... | collective-permute-start | bytes 786440 | tf_op jit(solution)/shard_map/ppermute | solution.py:316
  53.9 3.4 %collective-permute-start.2 = (f32[8,8,1024]{2,1,0:T(8,128)S(1)}, f32[8,8,1024]{2,1,0:T(8,128)S(1)}, u32[]{:S(2)}, u32[]{:S(2)}) collective-permute-start(f32[8,8,1024]{2,1,0:T(8,128)S(1)} %get-tuple-element.20), channel_id=1, source_target_pairs={{0,1},{1,0},{2,3},{3,2},{4,5},{5,4},{6,7},{7,6},{8,9},{9,8},{10,11... | collective-permute-start | bytes 786440 | tf_op jit(solution)/shard_map/ppermute | solution.py:316
  102.8 6.6 %collective-permute-start.3 = (f32[16,8,1024]{2,1,0:T(8,128)S(1)}, f32[16,8,1024]{2,1,0:T(8,128)S(1)}, u32[]{:S(2)}, u32[]{:S(2)}) collective-permute-start(f32[16,8,1024]{2,1,0:T(8,128)S(1)} %all_to_all.16.mine), channel_id=1, source_target_pairs={{0,1},{1,0},{2,3},{3,2},{4,5},{5,4},{6,7},{7,6},{8,9},{9,8},{10,11... | collective-permute-start | bytes 1572872 | tf_op jit(solution)/shard_map/ppermute | solution.py:324
  120.5 17.4 %collective-permute-start.4 = (f32[2,128,256]{2,1,0:T(8,128)S(1)}, f32[2,128,256]{2,1,0:T(8,128)S(1)}, u32[]{:S(2)}, u32[]{:S(2)}) collective-permute-start(f32[2,128,256]{2,1,0:T(8,128)S(1)} %get-tuple-element.22.u_head), channel_id=1, source_target_pairs={{0,16},{16,0},{1,17},{17,1},{2,18},{18,2},{3,19},{19,3},{4,20},{20... | collective-permute-start | bytes 786440 | tf_op jit(solution)/shard_map/ppermute | solution.py:327
  131.5 6.4 %collective-permute-start.5 = (f32[2,128,128]{2,1,0:T(8,128)S(1)}, f32[2,128,128]{2,1,0:T(8,128)S(1)}, u32[]{:S(2)}, u32[]{:S(2)}) collective-permute-start(f32[2,128,128]{2,1,0:T(8,128)S(1)} %get-tuple-element.27), channel_id=1, source_target_pairs={{0,16},{16,0},{1,17},{17,1},{2,18},{18,2},{3,19},{19,3},{4,20},{20... | collective-permute-start | bytes 393224 | tf_op jit(solution)/shard_map/ppermute | solution.py:329

commit v3 on v2

--- a/solution.py
+++ b/solution.py
@@ -12,11 +12,12 @@
 f32, bf16 = jnp.float32, jnp.bfloat16
 highest = lax.Precision.HIGHEST
 SWAP = [(0, 1), (1, 0)]
+NN = (((1,), (0,)), ((), ()))
 NT = (((1,), (1,)), ((), ()))
 TN = (((0,), (0,)), ((), ()))
 VMEM = pl.BlockSpec(memory_space=pltpu.VMEM)
 SMEM = pl.BlockSpec(memory_space=pltpu.SMEM)
-PARAMS = pltpu.CompilerParams(vmem_limit_bytes=40 << 20)
+PARAMS = pltpu.CompilerParams(vmem_limit_bytes=16 << 20)
 
 
 def shape(*sizes, dtype=f32):
@@ -32,138 +33,140 @@
     return top, (a - top.astype(f32)).astype(bf16)
 
 
-def operator_kernel(scalars, pattern, contrib, assembled, columns, targets, top, low, c_top, c_low, pick):
+def operator_kernel(scalars, pattern, contrib, assembled, columns, targets, top, low, built, c_top, c_low, spread):
     step = pl.program_id(0)
-    rows, cols = top.shape
     child = scalars[0]
+    rows = top.shape[0]
+    tile_rows, tile_cols = contrib.shape
 
     @pl.when(step == 0)
     def _():
         c_top[...], c_low[...] = two_parts(contrib[...])
-        places = lax.broadcasted_iota(jnp.int32, pick.shape, 0)
-        pick[...] = (places == columns[...]).astype(f32).astype(bf16)
-
-    places = lax.broadcasted_iota(jnp.int32, (rows, targets.shape[1]), 0) + step * rows
-    spread = (places == targets[...]).astype(f32).astype(bf16)
-    high_rows = dot(spread, c_top[...], (((1,), (0,)), ((), ()))).astype(bf16)
-    low_rows = dot(spread, c_low[...], (((1,), (0,)), ((), ()))).astype(bf16)
-    total = dot(high_rows, pick[...], NT) + dot(low_rows, pick[...], NT)
-    per_half = pl.num_programs(0) // 2
-    here = (step // per_half == child).astype(f32)
-    tile_row = child * per_half + step % per_half
-    for tile in range(cols // BT):
-        lanes = slice(tile * BT, (tile + 1) * BT)
-        keep = pattern[tile_row, tile].astype(f32) * here
-        top[:, lanes], low[:, lanes] = two_parts(total[:, lanes] + assembled[:, lanes] * keep)
+        places = lax.broadcasted_iota(jnp.int32, spread.shape, 0)
+        spread[...] = (places == targets[...]).astype(f32).astype(bf16)
+        built[...] = jnp.zeros_like(built)
+
+    places = lax.broadcasted_iota(jnp.int32, (rows, tile_cols), 0) + step * rows
+    pick = (places == columns[...]).astype(f32).astype(bf16)
+    high_rows = dot(pick, c_top[...], NT).astype(bf16)
+    low_rows = dot(pick, c_low[...], NT).astype(bf16)
+    total = dot(high_rows, spread[...], NT) + dot(low_rows, spread[...], NT)
+    tiles = tile_rows // BT
+    for half in range(2):
+        here = (child == half).astype(f32)
+        for tile in range(tiles):
+            keep = pattern[half * tiles + tile, step].astype(f32) * here
+            lanes = slice(half * tile_rows + tile * BT, half * tile_rows + (tile + 1) * BT)
+            entries = assembled[tile * BT : (tile + 1) * BT, :].T
+            top[:, lanes], low[:, lanes] = two_parts(total[:, lanes] + entries * keep)
 
 
 def build_operator(scalars, pattern, contrib, assembled, columns, targets):
     tile_rows, tile_cols = contrib.shape
     window_rows = assembled.shape[1]
-    steps = window_rows // BT
     block = pl.BlockSpec((BT, window_rows), lambda i: (i, 0))
     return pl.pallas_call(
         operator_kernel,
-        grid=(steps,),
+        grid=(window_rows // BT,),
         in_specs=[
             SMEM,
             SMEM,
             pl.BlockSpec((tile_rows, tile_cols), lambda i: (0, 0)),
-            pl.BlockSpec((BT, window_rows), lambda i: (i % (steps // 2), 0)),
+            pl.BlockSpec((tile_rows, BT), lambda i: (0, i)),
             pl.BlockSpec((1, tile_cols), lambda i: (0, 0)),
             pl.BlockSpec((1, tile_rows), lambda i: (0, 0)),
         ],
-        out_specs=[block, block],
-        out_shape=[shape(window_rows, window_rows, dtype=bf16)] * 2,
+        out_specs=[block, block, pl.BlockSpec((8, 128), lambda i: (0, 0))],
+        out_shape=[shape(window_rows, window_rows, dtype=bf16)] * 2 + [shape(8, 128)],
         scratch_shapes=[
             pltpu.VMEM((tile_rows, tile_cols), bf16),
             pltpu.VMEM((tile_rows, tile_cols), bf16),
-            pltpu.VMEM((window_rows, tile_cols), bf16),
+            pltpu.VMEM((window_rows, tile_rows), bf16),
         ],
         compiler_params=PARAMS,
         cost_estimate=pl.CostEstimate(flops=4 * 10**9, bytes_accessed=8 * 10**6, transcendentals=0),
     )(scalars, pattern, contrib, assembled, columns, targets)
 
 
-def apply_kernel(scalars, lines, top, low, give, keep, h_top, h_low):
+def apply_kernel(scalars, built, lines, top, low, give, keep):
     core = scalars[2]
     count, _, width, depth = lines.shape
-
-    @pl.when(pl.program_id(0) == 0)
-    def _():
-        both = jnp.concatenate(
-            [lines[:, pl.ds(1 - core, 1)].reshape(-1, depth), lines[:, pl.ds(core, 1)].reshape(-1, depth)]
-        )
-        h_top[...], h_low[...] = two_parts(both)
-
-    out = (
-        dot(h_top[...], top[...], NT) + dot(h_top[...], low[...], NT) + dot(h_low[...], top[...], NT)
+    rows = count * width
+    ordered = jnp.concatenate(
+        [lines[:, pl.ds(1 - core, 1)].reshape(rows, depth), lines[:, pl.ds(core, 1)].reshape(rows, depth)]
     )
-    give[...] = out[: count * width].reshape(give.shape)
-    keep[...] = out[count * width :].reshape(keep.shape)
-
-
-def apply_operator(scalars, gathered, top, low):
+    high_lines, low_lines = two_parts(ordered)
+    both = jnp.concatenate([high_lines, low_lines])
+    for tile in range(top.shape[1] // BT):
+        lanes = slice(tile * BT, (tile + 1) * BT)
+        wide = dot(both, top[:, lanes], NN)
+        out = wide[: 2 * rows] + wide[2 * rows :] + dot(high_lines, low[:, lanes], NN)
+        give[:, :, lanes] = out[:rows].reshape(count, width, BT)
+        keep[:, :, lanes] = out[rows:].reshape(count, width, BT)
+
+
+def apply_operator(scalars, built, gathered, top, low):
     count, both, depth = gathered.shape
     width = both // 2
-    window_rows = top.shape[0]
+    window_rows = top.shape[1]
     lines = gathered.reshape(count, 2, width, depth)
-    out_block = pl.BlockSpec((count, width, BT), lambda i: (0, 0, i))
-    in_block = pl.BlockSpec((BT, depth), lambda i: (i, 0))
     return pl.pallas_call(
         apply_kernel,
-        grid=(window_rows // BT,),
-        in_specs=[SMEM, pl.BlockSpec(lines.shape, lambda i: (0, 0, 0, 0)), in_block, in_block],
-        out_specs=[out_block, out_block],
+        in_specs=[SMEM, VMEM, VMEM, VMEM, VMEM],
+        out_specs=[VMEM, VMEM],
         out_shape=[shape(count, width, window_rows)] * 2,
-        scratch_shapes=[pltpu.VMEM((count * both, depth), bf16)] * 2,
         compiler_params=PARAMS,
         cost_estimate=pl.CostEstimate(flops=10**9, bytes_accessed=6 * 10**6, transcendentals=0),
-    )(scalars, lines, top, low)
-
-
-def rank_update(u):
+    )(scalars, built, lines, top, low)
+
+
+def spread_out(row_or_column):
+    return jnp.broadcast_to(row_or_column, (8, 128))
+
+
+def lane_tiles(a):
+    return [a[:, t : t + 128] for t in range(0, a.shape[1], 128)]
+
+
+def rank_update(block, u, start):
     a = u.astype(bf16).astype(f32)
     b = (u - a).astype(bf16).astype(f32)
     c = u - a - b
-    left = jnp.concatenate([a, a, b, b, a, c], 0).astype(bf16)
+    left = jnp.concatenate([v[:, :HALF] for v in (a, a, b, b, a, c)], 0).T[start:].astype(bf16)
     right = jnp.concatenate([a, b, a, b, c, a], 0).astype(bf16)
-    return dot(left[:, :HALF], right, TN)
-
-
-def factor_panel(block, r):
-    panel = block[pl.ds(r, 8), :]
-    tiles = panel.shape[1] // 128
-    pivot = pltpu.roll(panel[:, :128], 128 - r, 1)
-    rows = [
-        [jnp.broadcast_to(panel[j : j + 1, t * 128 : (t + 1) * 128], (8, 128)) for t in range(tiles)]
-        for j in range(8)
-    ]
-    spread = [jnp.broadcast_to(pivot[j : j + 1], (8, 128)) for j in range(8)]
-    a = [
-        [jnp.broadcast_to(spread[j][:, i : i + 1], (8, 128)) if i >= j else None for j in range(8)]
-        for i in range(8)
-    ]
-    for j in range(8):
-        inverse = lax.rsqrt(a[j][j])
-        column = {i: a[i][j] * inverse for i in range(j + 1, 8)}
-        for k in range(j + 1, 8):
-            for i in range(k, 8):
-                a[i][k] = a[i][k] - column[i] * column[k]
-        rows[j] = [v * inverse for v in rows[j]]
-        for k in range(j + 1, 8):
-            rows[k] = [v - column[k] * w for v, w in zip(rows[k], rows[j])]
+    block[start:, :] -= dot(left, right, NN)
+
+
+def factor_panel(panel, upcoming, r):
     sub = lax.broadcasted_iota(jnp.int32, (8, 128), 0)
     lane = lax.broadcasted_iota(jnp.int32, (8, 128), 1)
+    rows = lane_tiles(panel)
+    columns = [spread_out(rows[0][:, r + j : r + j + 1]) for j in range(8)]
+    solved = []
+    for j in range(8):
+        inverse = lax.rsqrt(spread_out(columns[j][j : j + 1]))
+        column = columns[j] * inverse
+        solved.append([spread_out(v[j : j + 1]) * inverse for v in rows])
+        below = jnp.where(sub > j, column, 0.0)
+        rows = [v - below * w for v, w in zip(rows, solved[j])]
+        for k in range(j + 1, 8):
+            columns[k] = columns[k] - column * spread_out(column[k : k + 1])
+    if upcoming is not None:
+        after = lane_tiles(upcoming)
+        pick = lane == sub + (r + 8)
+        for j in range(8):
+            column = spread_out(jnp.sum(jnp.where(pick, solved[j][0], 0.0), axis=1, keepdims=True))
+            after = [v - column * w for v, w in zip(after, solved[j])]
+        upcoming = jnp.concatenate(after, 1)
     out = []
-    for t in range(tiles):
-        u = rows[7][t]
+    for t in range(len(rows)):
+        u = solved[7][t]
         for j in range(7):
-            u = jnp.where(sub == j, rows[j][t], u)
+            u = jnp.where(sub == j, solved[j][t], u)
         if t == 0:
             u = jnp.where(lane >= sub + r, u, 0.0)
         out.append(u)
-    return jnp.concatenate(out, 1)
+    return jnp.concatenate(out, 1), upcoming
 
 
 def unit(size):
@@ -173,15 +176,17 @@
 
 
 def factor_block(blocks, store):
-    def panel(p, carry):
-        r = pl.multiple_of(p * 8, 8)
+    panels = [block[:8, :] for block in blocks]
+    found = [None] * len(blocks)
+    for r in range(0, HALF, 8):
         for leaf, block in enumerate(blocks):
-            u = factor_panel(block, r)
-            store(leaf, r, u)
-            block[...] -= rank_update(u)
-        return carry
-
-    lax.fori_loop(0, HALF // 8, panel, 0)
+            start = (r + 8) // 16 * 16
+            if found[leaf] is not None and start < HALF:
+                rank_update(block, found[leaf], start)
+        for leaf, block in enumerate(blocks):
+            upcoming = block[r + 8 : r + 16, :] if r + 8 < HALF else None
+            found[leaf], panels[leaf] = factor_panel(panels[leaf], upcoming, r)
+            store(leaf, r, found[leaf])
 
 
 def head_kernel(scalars, mine, theirs, window, u_head, x_head, rest, gram, s0, s1):
@@ -207,8 +212,8 @@
         blocks[leaf][:, R:] = unit(HALF)
 
     def store(leaf, r, u):
-        u_head[leaf, pl.ds(r, 8), :] = u[:, :R]
-        x_head[leaf, pl.ds(r, 8), :] = u[:, R:]
+        u_head[leaf, r : r + 8, :] = u[:, :R]
+        x_head[leaf, r : r + 8, :] = u[:, R:]
 
     factor_block(blocks, store)
     for leaf in range(2):
@@ -243,8 +248,8 @@
         blocks[leaf][:, R:] = unit(HALF)
 
     def store(leaf, r, u):
-        u_tail[leaf, pl.ds(r, 8), :] = u[:, :HALF]
-        x_tail[leaf, pl.ds(r, 8), :] = u[:, HALF:]
+        u_tail[leaf, r : r + 8, :] = u[:, :HALF]
+        x_tail[leaf, r : r + 8, :] = u[:, HALF:]
 
     factor_block(blocks, store)
     start = pl.multiple_of(group % (HALF // 8) * 8, 8)
@@ -274,7 +279,7 @@
 
 def bases_kernel(scalars, window, x_own, out):
     both = jnp.concatenate([x_own[0], x_own[1]], 0)
-    solved = dot(both, window[...], (((1,), (0,)), ((), ())), highest)
+    solved = dot(both, window[...], NN, highest)
     lane = lax.broadcasted_iota(jnp.int32, out.shape, 1)
     out[...] = jnp.where(lane < scalars[3], solved[:8], solved[8:])
 
@@ -308,11 +313,12 @@
     ).astype(jnp.int32)
 
     own = lax.all_to_all(jnp.broadcast_to(omega.T, (z_count, own_count, window_rows)), "z", 0, 0)
-    top, low = build_operator(scalars, pattern, contrib[0], assembled[0], columns, targets)
+    top, low, built = build_operator(scalars, pattern, contrib[0], assembled[0], columns, targets)
+    own, built = lax.optimization_barrier((own, built))
     other = lax.ppermute(own, "xl", SWAP)
 
     def half(gathered):
-        give, keep = apply_operator(scalars, gathered, top, low)
+        give, keep = apply_operator(scalars, built, gathered, top, low)
         return keep + lax.ppermute(give, "core", SWAP)
 
     parts = jnp.concatenate([half(own), half(other)], axis=0)

time: 140 us -> 127 us (0.907)
  Pallas kernels: 35 us -> 23.5 us
  waiting for transfers between devices: 22.2 us -> 16.1 us
  local copies, waits for them, and re-layouts: 5.31 us -> 8.24 us
    all_to_all x1, waiting for transfers between devices: 18 us -> 6.07 us  [local(): lax.all_to_all(jnp.broadcast_to(omega.T, (z_count, own_count, window_rows...]
    ppermute x1, waiting for transfers between devices: 0.01 us -> 5.95 us  [local(): other = lax.ppermute(own, 'xl', SWAP)]
    pallas_call x1, Pallas kernels: 11.1 us -> 6.94 us  [factor_head(): pl.pallas_call(head_kernel, in_specs=[SMEM, VMEM, VMEM], out_specs=[VMEM]...]
    pallas_call x1, Pallas kernels: 9.06 us -> 4.98 us  [factor_tail(): pl.pallas_call(tail_kernel, in_specs=[SMEM] + [VMEM] * 3, out_specs=[VMEM...]
    pallas_call x3, Pallas kernels: 12 us -> 8.67 us  [the longest x1 5.61 us: build_operator(): pl.pallas_call(operator_kernel, grid=(window_rows // BT,), in_specs=[SMEM...]
    unnamed x6 -> x10, local copies, waits for them, and re-layouts: 3.5 us -> 6.4 us
  transfers between devices with their start and end apart: 7 -> 7, of which waited for: 4 -> 5; matrix products, arithmetic and copies ran while one was open for 1% -> 1% of each run, Pallas kernels for 16% -> 12%
where the time goes in v3:
time: 127 us; the launch traced here: 126 us
  blocking collectives  46 us (36%)
  starting transfers between devices  29.9 us (24%)
  Pallas kernels  23.5 us (19%)
  waiting for transfers between devices  16.1 us (13%)
  local copies, waits for them, and re-layouts  8.24 us (6%)
  between operations  1.42 us (1%)
    all_to_all x1, blocking collectives, local(): terms = lax.all_to_all(parts, ('child', 'y'), 0, 0)  24.3 us
    all_to_all x1, blocking collectives, local(): lax.all_to_all(jnp.broadcast_to(samples, (groups, width, window_rows)), (...  21.7 us
    all_to_all x1, starting transfers between devices, local(): lax.all_to_all(jnp.broadcast_to(omega.T, (z_count, own_count, window_rows...  10.9 us
    pallas_call x1, Pallas kernels, factor_head(): pl.pallas_call(head_kernel, in_specs=[SMEM, VMEM, VMEM], out_specs=[VMEM]...  6.94 us
    unnamed x10, local copies, waits for them, and re-layouts  6.4 us
    all_to_all x1, waiting for transfers between devices, local(): lax.all_to_all(jnp.broadcast_to(omega.T, (z_count, own_count, window_rows...  6.07 us
    ppermute x1, waiting for transfers between devices, local(): other = lax.ppermute(own, 'xl', SWAP)  5.95 us
    ppermute x2, starting transfers between devices, half(): return keep + lax.ppermute(give, 'core', SWAP)  5.93 us
  transfers between devices with their start and end apart: 7, of which 5 were waited for; matrix products, arithmetic and copies ran while one was open for 1% of the time, Pallas kernels for 12%

profile of v3, /device:TPU:1, one launch (start us, length us, event | category | flops | bytes accessed | tf_op | source)
XLA Modules:
  0.0 126.0 jit_solution(1382843422305607694)
XLA Ops:
  0.6 1.7 %broadcast_in_dim.9 = f32[8,16,1024]{2,1,0:T(8,128)} broadcast(f32[16,1024]{1,0:T(8,128)} %bitcast.15), dimensions={1,2} | broadcast | bytes 589824 | tf_op jit(solution)/shard_map/broadcast_in_dim | solution.py:315
  2.3 10.9 %all-to-all-start = ((f32[8,16,1024]{2,1,0:T(8,128)}), f32[8,16,1024]{2,1,0:T(8,128)S(1)}, u32[]{:S(2)}, u32[]{:S(2)}) async-start(f32[8,16,1024]{2,1,0:T(8,128)} %broadcast_in_dim.9), calls=%async_computation | async-start | bytes 1048576 | tf_op jit(solution)/shard_map/all_to_all | solution.py:315
  13.9 0.1 stack.19.scalars
  13.9 0.7 dynamic-slice_subtract_fusion
  14.6 0.0 copy-start.2
  14.6 1.6 %copy-done.2 = f32[1,512,1024]{2,1,0:T(8,128)S(1)} copy-done((f32[1,512,1024]{2,1,0:T(8,128)S(1)}, f32[1,512,1024]{2,1,0:T(8,128)}, u32[]{:S(2)}) %copy-start.2) | copy-done | bytes 2097176
  16.2 0.0 copy-start.3
  16.2 1.2 copy-done.3
  17.5 0.0 copy-start.4
  17.5 0.7 copy-done.4
  18.1 5.6 %shard_map.77 = (bf16[1024,1024]{1,0:T(8,128)(2,1)S(1)}, bf16[1024,1024]{1,0:T(8,128)(2,1)S(1)}, f32[8,128]{1,0:T(8,128)S(1)}) custom-call(s32[5]{0:T(128)S(1)} %stack.19.scalars, s32[4,4]{1,0:T(4,128)S(1)} %copy-done.4, f32[512,512]{1,0:T(8,128)S(1)} %bitcast.14, f32[512,1024]{1,0:T(8,128)S(1)} %bitcast.13, s32[1,512]{1,0:T(1,128)S(1)} %get-tuple-element.35.columns, ...), custom_call_target="tpu_custom_call" | custom-call | flops 4000000000 | bytes 8000000 | tf_op jit(solution)/shard_map/pallas_call | solution.py:68
  23.8 0.0 copy-start
  23.8 1.3 %copy-done = bf16[1024,1024]{1,0:T(8,128)(2,1)} copy-done((bf16[1024,1024]{1,0:T(8,128)(2,1)}, bf16[1024,1024]{1,0:T(8,128)(2,1)S(1)}, u32[]{:S(2)}) %copy-start) | copy-done | bytes 2097176
  25.1 6.1 %all-to-all-done = f32[8,16,1024]{2,1,0:T(8,128)S(1)} async-done(((f32[8,16,1024]{2,1,0:T(8,128)}), f32[8,16,1024]{2,1,0:T(8,128)S(1)}, u32[]{:S(2)}, u32[]{:S(2)}) %all-to-all-start) | async-done | bytes 524320 | tf_op jit(solution)/shard_map/all_to_all | solution.py:315
  31.2 3.1 %collective-permute-start.1 = (f32[8,16,1024]{2,1,0:T(8,128)S(1)}, f32[8,16,1024]{2,1,0:T(8,128)S(1)}, u32[]{:S(2)}, u32[]{:S(2)}) collective-permute-start(f32[8,16,1024]{2,1,0:T(8,128)S(1)} %all-to-all-done), channel_id=1, source_target_pairs={{0,16},{16,0},{1,17},{17,1},{2,18},{18,2},{3,19},{19,3},{4,20},{20... | collective-permute-start | bytes 1572872 | tf_op jit(solution)/shard_map/ppermute | solution.py:318
  34.3 0.0 copy-start.1
  34.3 1.6 %copy-done.1 = bf16[1024,1024]{1,0:T(8,128)(2,1)S(1)} copy-done((bf16[1024,1024]{1,0:T(8,128)(2,1)S(1)}, bf16[1024,1024]{1,0:T(8,128)(2,1)}, u32[]{:S(2)}) %copy-start.1) | copy-done | bytes 2097176
  35.9 1.5 %shard_map.78 = (f32[8,8,1024]{2,1,0:T(8,128)S(1)}, f32[8,8,1024]{2,1,0:T(8,128)S(1)}) custom-call(s32[5]{0:T(128)S(1)} %stack.19.scalars, f32[8,128]{1,0:T(8,128)S(1)} %get-tuple-element.19.built, f32[8,2,8,1024]{3,2,1,0:T(8,128)S(1)} %bitcast.11, bf16[1024,1024]{1,0:T(8,128)(2,1)S(1)} %get-tuple-element.21.top, bf16[1024,1024]{1,0:T(8,128)(2,1)S(1)} %copy-done.1), custom_call_target="tpu_custom_call" | custom-call | flops 1000000000 | bytes 6000000 | tf_op jit(solution)/shard_map/pallas_call | solution.py:113
  37.4 2.7 %collective-permute-start = (f32[8,8,1024]{2,1,0:T(8,128)S(1)}, f32[8,8,1024]{2,1,0:T(8,128)S(1)}, u32[]{:S(2)}, u32[]{:S(2)}) collective-permute-start(f32[8,8,1024]{2,1,0:T(8,128)S(1)} %get-tuple-element.24), channel_id=1, source_target_pairs={{0,1},{1,0},{2,3},{3,2},{4,5},{5,4},{6,7},{7,6},{8,9},{9,8},{10,11... | collective-permute-start | bytes 786440 | tf_op jit(solution)/shard_map/ppermute | solution.py:322
  40.1 5.9 %collective-permute-done.1 = f32[8,16,1024]{2,1,0:T(8,128)S(1)} collective-permute-done((f32[8,16,1024]{2,1,0:T(8,128)S(1)}, f32[8,16,1024]{2,1,0:T(8,128)S(1)}, u32[]{:S(2)}, u32[]{:S(2)}) %collective-permute-start.1) | collective-permute-done | bytes 524320 | tf_op jit(solution)/shard_map/ppermute | solution.py:318
  46.0 1.5 %shard_map.79 = (f32[8,8,1024]{2,1,0:T(8,128)S(1)}, f32[8,8,1024]{2,1,0:T(8,128)S(1)}) custom-call(s32[5]{0:T(128)S(1)} %stack.19.scalars, f32[8,128]{1,0:T(8,128)S(1)} %get-tuple-element.19.built, f32[8,2,8,1024]{3,2,1,0:T(8,128)S(1)} %bitcast.12, bf16[1024,1024]{1,0:T(8,128)(2,1)S(1)} %get-tuple-element.21.top, bf16[1024,1024]{1,0:T(8,128)(2,1)S(1)} %copy-done.1), custom_call_target="tpu_custom_call" | custom-call | flops 1000000000 | bytes 6000000 | tf_op jit(solution)/shard_map/pallas_call | solution.py:113
  47.6 3.2 %collective-permute-start.2 = (f32[8,8,1024]{2,1,0:T(8,128)S(1)}, f32[8,8,1024]{2,1,0:T(8,128)S(1)}, u32[]{:S(2)}, u32[]{:S(2)}) collective-permute-start(f32[8,8,1024]{2,1,0:T(8,128)S(1)} %get-tuple-element.26), channel_id=1, source_target_pairs={{0,1},{1,0},{2,3},{3,2},{4,5},{5,4},{6,7},{7,6},{8,9},{9,8},{10,11... | collective-permute-start | bytes 786440 | tf_op jit(solution)/shard_map/ppermute | solution.py:322
  50.8 0.0 collective-permute-done
  50.9 1.1 collective-permute-done.2
  52.1 24.3 %all_to_all.15 = f32[16,8,1024]{2,1,0:T(8,128)S(1)} all-to-all(f32[16,8,1024]{2,1,0:T(8,128)S(1)} %pad_maximum_fusion), channel_id=1, replica_groups=mesh['child'=2,'z'=8,'xl'=2,'y'=8,'core'=2] {'child','y'}, dimensions={0} | all-to-all | bytes 1048576 | tf_op jit(solution)/shard_map/all_to_all | solution.py:325
  76.4 21.7 %all_to_all.16.mine = f32[16,8,1024]{2,1,0:T(8,128)S(1)} all-to-all(f32[16,8,1024]{2,1,0:T(8,128)S(1)} %broadcast_in_dim.10), channel_id=1, replica_groups=mesh['child'=2,'z'=8,'xl'=2,'y'=8,'core'=2] {'child','y'}, dimensions={0} | all-to-all | bytes 1048576 | tf_op jit(solution)/shard_map/all_to_all | solution.py:327
  98.2 4.7 %collective-permute-start.3 = (f32[16,8,1024]{2,1,0:T(8,128)S(1)}, f32[16,8,1024]{2,1,0:T(8,128)S(1)}, u32[]{:S(2)}, u32[]{:S(2)}) collective-permute-start(f32[16,8,1024]{2,1,0:T(8,128)S(1)} %all_to_all.16.mine), channel_id=1, source_target_pairs={{0,1},{1,0},{2,3},{3,2},{4,5},{5,4},{6,7},{7,6},{8,9},{9,8},{10,11... | collective-permute-start | bytes 1572872 | tf_op jit(solution)/shard_map/ppermute | solution.py:330
  102.9 1.5 %collective-permute-done.3.theirs = f32[16,8,1024]{2,1,0:T(8,128)S(1)} collective-permute-done((f32[16,8,1024]{2,1,0:T(8,128)S(1)}, f32[16,8,1024]{2,1,0:T(8,128)S(1)}, u32[]{:S(2)}, u32[]{:S(2)}) %collective-permute-start.3) | collective-permute-done | bytes 524320 | tf_op jit(solution)/shard_map/ppermute | solution.py:330
  104.4 6.9 %shard_map.80 = (f32[256,1024]{1,0:T(8,128)S(1)}, f32[2,128,256]{2,1,0:T(8,128)S(1)}, f32[2,128,128]{2,1,0:T(8,128)S(1)}, f32[2,128,256]{2,1,0:T(8,128)S(1)}) custom-call(s32[5]{0:T(128)S(1)} %stack.19.scalars, f32[16,8,1024]{2,1,0:T(8,128)S(1)} %all_to_all.16.mine, f32[16,8,1024]{2,1,0:T(8,128)S(1)} %collective-permute-done.3.theirs), custom_call_target="tpu_custom_call" | custom-call | tf_op jit(solution)/shard_map/pallas_call | solution.py:228
  111.4 2.2 %collective-permute-start.4 = (f32[2,128,256]{2,1,0:T(8,128)S(1)}, f32[2,128,256]{2,1,0:T(8,128)S(1)}, u32[]{:S(2)}, u32[]{:S(2)}) collective-permute-start(f32[2,128,256]{2,1,0:T(8,128)S(1)} %get-tuple-element.28.u_head), channel_id=1, source_target_pairs={{0,16},{16,0},{1,17},{17,1},{2,18},{18,2},{3,19},{19,3},{4,20},{20... | collective-permute-start | bytes 786440 | tf_op jit(solution)/shard_map/ppermute | solution.py:333
  113.6 5.0 %shard_map.81 = (f32[2,128,128]{2,1,0:T(8,128)S(1)}, f32[2,8,256]{2,1,0:T(8,128)S(1)}, f32[2,8,256]{2,1,0:T(8,128)S(1)}) custom-call(s32[5]{0:T(128)S(1)} %stack.19.scalars, f32[2,128,256]{2,1,0:T(8,128)S(1)} %get-tuple-element.28.u_head, f32[2,128,128]{2,1,0:T(8,128)S(1)} %get-tuple-element.29.x_head, f32[2,128,256]{2,1,0:T(8,128)S(1)} %get-tuple-element.30.rest), custom_call_target="tpu_custom_call" | custom-call | flops 8000000000 | bytes 1000000 | tf_op jit(solution)/shard_map/pallas_call | solution.py:269
  118.6 3.1 %collective-permute-start.5 = (f32[2,128,128]{2,1,0:T(8,128)S(1)}, f32[2,128,128]{2,1,0:T(8,128)S(1)}, u32[]{:S(2)}, u32[]{:S(2)}) collective-permute-start(f32[2,128,128]{2,1,0:T(8,128)S(1)} %get-tuple-element.33), channel_id=1, source_target_pairs={{0,16},{16,0},{1,17},{17,1},{2,18},{18,2},{3,19},{19,3},{4,20},{20... | collective-permute-start | bytes 393224 | tf_op jit(solution)/shard_map/ppermute | solution.py:335
  121.6 1.8 %shard_map.82 = f32[8,1024]{1,0:T(8,128)} custom-call(s32[5]{0:T(128)S(1)} %stack.19.scalars, f32[256,1024]{1,0:T(8,128)S(1)} %get-tuple-element.27.window, f32[2,8,256]{2,1,0:T(8,128)S(1)} %get-tuple-element.31.x_own), custom_call_target="tpu_custom_call" | custom-call | flops 1000000000 | bytes 1000000 | tf_op jit(solution)/shard_map/pallas_call | solution.py:336
  123.4 1.5 %collective-permute-done.5.sib_tail = f32[2,128,128]{2,1,0:T(8,128)S(1)} collective-permute-done((f32[2,128,128]{2,1,0:T(8,128)S(1)}, f32[2,128,128]{2,1,0:T(8,128)S(1)}, u32[]{:S(2)}, u32[]{:S(2)}) %collective-permute-start.5) | collective-permute-done | bytes 131104 | tf_op jit(solution)/shard_map/ppermute | solution.py:335
  124.9 0.0 collective-permute-done.4.sib_head
  124.9 1.1 shard_map.83
  (5 shorter events, 0.2 us)
Async XLA Ops:
  2.3 28.8 %all-to-all-start = ((f32[8,16,1024]{2,1,0:T(8,128)}), f32[8,16,1024]{2,1,0:T(8,128)S(1)}, u32[]{:S(2)}, u32[]{:S(2)}) async-start(f32[8,16,1024]{2,1,0:T(8,128)} %broadcast_in_dim.9), calls=%async_computation | async-start | bytes 1048576 | tf_op jit(solution)/shard_map/all_to_all | solution.py:315
  14.6 1.6 %copy-start.2 = (f32[1,512,1024]{2,1,0:T(8,128)S(1)}, f32[1,512,1024]{2,1,0:T(8,128)}, u32[]{:S(2)}) copy-start(f32[1,512,1024]{2,1,0:T(8,128)} %param.7) | copy-start | bytes 6291460
  16.2 1.2 copy-start.3
  17.5 0.7 copy-start.4
  23.8 1.3 %copy-start = (bf16[1024,1024]{1,0:T(8,128)(2,1)}, bf16[1024,1024]{1,0:T(8,128)(2,1)S(1)}, u32[]{:S(2)}) copy-start(bf16[1024,1024]{1,0:T(8,128)(2,1)S(1)} %get-tuple-element.22.low) | copy-start | bytes 6291460
  31.2 14.9 %collective-permute-start.1 = (f32[8,16,1024]{2,1,0:T(8,128)S(1)}, f32[8,16,1024]{2,1,0:T(8,128)S(1)}, u32[]{:S(2)}, u32[]{:S(2)}) collective-permute-start(f32[8,16,1024]{2,1,0:T(8,128)S(1)} %all-to-all-done), channel_id=1, source_target_pairs={{0,16},{16,0},{1,17},{17,1},{2,18},{18,2},{3,19},{19,3},{4,20},{20... | collective-permute-start | bytes 1572872 | tf_op jit(solution)/shard_map/ppermute | solution.py:318
  34.3 1.6 %copy-start.1 = (bf16[1024,1024]{1,0:T(8,128)(2,1)S(1)}, bf16[1024,1024]{1,0:T(8,128)(2,1)}, u32[]{:S(2)}) copy-start(bf16[1024,1024]{1,0:T(8,128)(2,1)} %copy-done) | copy-start | bytes 6291460
  37.4 13.4 %collective-permute-start = (f32[8,8,1024]{2,1,0:T(8,128)S(1)}, f32[8,8,1024]{2,1,0:T(8,128)S(1)}, u32[]{:S(2)}, u32[]{:S(2)}) collective-permute-start(f32[8,8,1024]{2,1,0:T(8,128)S(1)} %get-tuple-element.24), channel_id=1, source_target_pairs={{0,1},{1,0},{2,3},{3,2},{4,5},{5,4},{6,7},{7,6},{8,9},{9,8},{10,11... | collective-permute-start | bytes 786440 | tf_op jit(solution)/shard_map/ppermute | solution.py:322
  47.6 4.4 %collective-permute-start.2 = (f32[8,8,1024]{2,1,0:T(8,128)S(1)}, f32[8,8,1024]{2,1,0:T(8,128)S(1)}, u32[]{:S(2)}, u32[]{:S(2)}) collective-permute-start(f32[8,8,1024]{2,1,0:T(8,128)S(1)} %get-tuple-element.26), channel_id=1, source_target_pairs={{0,1},{1,0},{2,3},{3,2},{4,5},{5,4},{6,7},{7,6},{8,9},{9,8},{10,11... | collective-permute-start | bytes 786440 | tf_op jit(solution)/shard_map/ppermute | solution.py:322
  98.2 6.2 %collective-permute-start.3 = (f32[16,8,1024]{2,1,0:T(8,128)S(1)}, f32[16,8,1024]{2,1,0:T(8,128)S(1)}, u32[]{:S(2)}, u32[]{:S(2)}) collective-permute-start(f32[16,8,1024]{2,1,0:T(8,128)S(1)} %all_to_all.16.mine), channel_id=1, source_target_pairs={{0,1},{1,0},{2,3},{3,2},{4,5},{5,4},{6,7},{7,6},{8,9},{9,8},{10,11... | collective-permute-start | bytes 1572872 | tf_op jit(solution)/shard_map/ppermute | solution.py:330
  111.4 13.5 %collective-permute-start.4 = (f32[2,128,256]{2,1,0:T(8,128)S(1)}, f32[2,128,256]{2,1,0:T(8,128)S(1)}, u32[]{:S(2)}, u32[]{:S(2)}) collective-permute-start(f32[2,128,256]{2,1,0:T(8,128)S(1)} %get-tuple-element.28.u_head), channel_id=1, source_target_pairs={{0,16},{16,0},{1,17},{17,1},{2,18},{18,2},{3,19},{19,3},{4,20},{20... | collective-permute-start | bytes 786440 | tf_op jit(solution)/shard_map/ppermute | solution.py:333
  118.6 6.3 %collective-permute-start.5 = (f32[2,128,128]{2,1,0:T(8,128)S(1)}, f32[2,128,128]{2,1,0:T(8,128)S(1)}, u32[]{:S(2)}, u32[]{:S(2)}) collective-permute-start(f32[2,128,128]{2,1,0:T(8,128)S(1)} %get-tuple-element.33), channel_id=1, source_target_pairs={{0,16},{16,0},{1,17},{17,1},{2,18},{18,2},{3,19},{19,3},{4,20},{20... | collective-permute-start | bytes 393224 | tf_op jit(solution)/shard_map/ppermute | solution.py:335

commit v4 on v3

--- a/solution.py
+++ b/solution.py
@@ -33,67 +33,81 @@
     return top, (a - top.astype(f32)).astype(bf16)
 
 
-def operator_kernel(scalars, pattern, contrib, assembled, columns, targets, top, low, built, c_top, c_low, spread):
+def copies_kernel(lines, out):
+    for copy in range(out.shape[0]):
+        out[copy] = lines[...]
+
+
+def operator_kernel(scalars, pattern, own, sibling, assembled, columns, targets, top, low, built, parts, spread):
     step = pl.program_id(0)
     child = scalars[0]
-    rows = top.shape[0]
-    tile_rows, tile_cols = contrib.shape
+    rows, half_rows = top.shape
+    tile_cols = own.shape[1]
 
     @pl.when(step == 0)
     def _():
-        c_top[...], c_low[...] = two_parts(contrib[...])
-        places = lax.broadcasted_iota(jnp.int32, spread.shape, 0)
-        spread[...] = (places == targets[...]).astype(f32).astype(bf16)
+        places = lax.broadcasted_iota(jnp.int32, (half_rows, targets.shape[1]), 0) + child * half_rows
+        for source, block in enumerate((own, sibling)):
+            parts[source, 0], parts[source, 1] = two_parts(block[...])
+            spread[source] = (places == targets[source : source + 1, :]).astype(f32).astype(bf16)
         built[...] = jnp.zeros_like(built)
 
     places = lax.broadcasted_iota(jnp.int32, (rows, tile_cols), 0) + step * rows
-    pick = (places == columns[...]).astype(f32).astype(bf16)
-    high_rows = dot(pick, c_top[...], NT).astype(bf16)
-    low_rows = dot(pick, c_low[...], NT).astype(bf16)
-    total = dot(high_rows, spread[...], NT) + dot(low_rows, spread[...], NT)
-    tiles = tile_rows // BT
-    for half in range(2):
-        here = (child == half).astype(f32)
-        for tile in range(tiles):
-            keep = pattern[half * tiles + tile, step].astype(f32) * here
-            lanes = slice(half * tile_rows + tile * BT, half * tile_rows + (tile + 1) * BT)
-            entries = assembled[tile * BT : (tile + 1) * BT, :].T
-            top[:, lanes], low[:, lanes] = two_parts(total[:, lanes] + entries * keep)
-
-
-def build_operator(scalars, pattern, contrib, assembled, columns, targets):
-    tile_rows, tile_cols = contrib.shape
+    total = jnp.zeros((rows, half_rows), f32)
+    for source in range(2):
+        pick = (places == columns[source : source + 1, :]).astype(f32).astype(bf16)
+        for part in range(2):
+            picked = dot(pick, parts[source, part], NT).astype(bf16)
+            total = total + dot(picked, spread[source], NT)
+    tiles = half_rows // BT
+    for tile in range(tiles):
+        keep = pattern[child * tiles + tile, step].astype(f32)
+        lanes = slice(tile * BT, (tile + 1) * BT)
+        entries = assembled[lanes, :].T
+        top[:, lanes], low[:, lanes] = two_parts(total[:, lanes] + entries * keep)
+
+
+def build_operator(scalars, pattern, own, sibling, assembled, columns, targets):
+    tile_rows, tile_cols = own.shape
     window_rows = assembled.shape[1]
-    block = pl.BlockSpec((BT, window_rows), lambda i: (i, 0))
+    half_rows = assembled.shape[0]
+    block = pl.BlockSpec((BT, half_rows), lambda i: (i, 0))
+    whole = pl.BlockSpec((tile_rows, tile_cols), lambda i: (0, 0))
     return pl.pallas_call(
         operator_kernel,
         grid=(window_rows // BT,),
         in_specs=[
             SMEM,
             SMEM,
-            pl.BlockSpec((tile_rows, tile_cols), lambda i: (0, 0)),
-            pl.BlockSpec((tile_rows, BT), lambda i: (0, i)),
-            pl.BlockSpec((1, tile_cols), lambda i: (0, 0)),
-            pl.BlockSpec((1, tile_rows), lambda i: (0, 0)),
+            whole,
+            whole,
+            pl.BlockSpec((half_rows, BT), lambda i: (0, i)),
+            pl.BlockSpec((2, tile_cols), lambda i: (0, 0)),
+            pl.BlockSpec((2, tile_rows), lambda i: (0, 0)),
         ],
         out_specs=[block, block, pl.BlockSpec((8, 128), lambda i: (0, 0))],
-        out_shape=[shape(window_rows, window_rows, dtype=bf16)] * 2 + [shape(8, 128)],
+        out_shape=[shape(window_rows, half_rows, dtype=bf16)] * 2 + [shape(8, 128)],
         scratch_shapes=[
-            pltpu.VMEM((tile_rows, tile_cols), bf16),
-            pltpu.VMEM((tile_rows, tile_cols), bf16),
-            pltpu.VMEM((window_rows, tile_rows), bf16),
+            pltpu.VMEM((2, 2, tile_rows, tile_cols), bf16),
+            pltpu.VMEM((2, half_rows, tile_rows), bf16),
         ],
         compiler_params=PARAMS,
         cost_estimate=pl.CostEstimate(flops=4 * 10**9, bytes_accessed=8 * 10**6, transcendentals=0),
-    )(scalars, pattern, contrib, assembled, columns, targets)
-
-
-def apply_kernel(scalars, built, lines, top, low, give, keep):
+    )(scalars, pattern, own, sibling, assembled, columns, targets)
+
+
+def apply_kernel(scalars, built, *refs):
+    *pieces, top, low, give, keep = refs
     core = scalars[2]
-    count, _, width, depth = lines.shape
+    count, width, _ = give.shape
+    depth = top.shape[0]
     rows = count * width
     ordered = jnp.concatenate(
-        [lines[:, pl.ds(1 - core, 1)].reshape(rows, depth), lines[:, pl.ds(core, 1)].reshape(rows, depth)]
+        [
+            piece[:, pl.ds(side, 1)].reshape(-1, depth)
+            for side in (1 - core, core)
+            for piece in pieces
+        ]
     )
     high_lines, low_lines = two_parts(ordered)
     both = jnp.concatenate([high_lines, low_lines])
@@ -105,19 +119,19 @@
         keep[:, :, lanes] = out[rows:].reshape(count, width, BT)
 
 
-def apply_operator(scalars, built, gathered, top, low):
-    count, both, depth = gathered.shape
-    width = both // 2
-    window_rows = top.shape[1]
-    lines = gathered.reshape(count, 2, width, depth)
+def apply_operator(scalars, built, pieces, top, low):
+    count = sum(piece.shape[0] for piece in pieces)
+    width = pieces[0].shape[1] // 2
+    depth, half_rows = top.shape
+    lines = [piece.reshape(piece.shape[0], 2, width, depth) for piece in pieces]
     return pl.pallas_call(
         apply_kernel,
-        in_specs=[SMEM, VMEM, VMEM, VMEM, VMEM],
+        in_specs=[SMEM] + [VMEM] * (3 + len(lines)),
         out_specs=[VMEM, VMEM],
-        out_shape=[shape(count, width, window_rows)] * 2,
+        out_shape=[shape(count, width, half_rows)] * 2,
         compiler_params=PARAMS,
         cost_estimate=pl.CostEstimate(flops=10**9, bytes_accessed=6 * 10**6, transcendentals=0),
-    )(scalars, built, lines, top, low)
+    )(scalars, built, *lines, top, low)
 
 
 def spread_out(row_or_column):
@@ -192,11 +206,15 @@
 def head_kernel(scalars, mine, theirs, window, u_head, x_head, rest, gram, s0, s1):
     xl, core, bound = scalars[1], scalars[2], scalars[3]
     count = mine.shape[0] // 2
-    window_rows = mine.shape[2]
+    half_rows = mine.shape[2]
+    window_rows = 2 * half_rows
     for block in range(2 * count):
-        start = block % count * 32 + (block // count ^ xl) * 16
-        window[pl.ds(pl.multiple_of(start + core * 8, 8), 8), :] = mine[block]
-        window[pl.ds(pl.multiple_of(start + (1 - core) * 8, 8), 8), :] = theirs[block]
+        lanes = slice(block // count * half_rows, (block // count + 1) * half_rows)
+        for side in range(2):
+            start = block % count * 32 + (side ^ xl) * 16
+            for source, at in ((mine, core), (theirs, 1 - core)):
+                there = pl.ds(pl.multiple_of(start + at * 8, 8), 8)
+                window[there, lanes] = source[block, side * 8 : side * 8 + 8, :]
     edge = window_rows // 2 + HALF
     lane = lax.broadcasted_iota(jnp.int32, (R, edge), 1)
     head = window[:, :edge]
@@ -224,7 +242,7 @@
 
 
 def factor_head(scalars, mine, theirs):
-    window_rows = mine.shape[2]
+    window_rows = 2 * mine.shape[2]
     return pl.pallas_call(
         head_kernel,
         in_specs=[SMEM, VMEM, VMEM],
@@ -294,14 +312,18 @@
 def local(contrib, assembled, pattern, omega, row_maps, leaf_bounds):
     tile_rows, tile_cols = contrib.shape[1:]
     window_rows, own_count = omega.shape
-    z_count = lax.axis_size("z")
-    groups = lax.axis_size("child") * lax.axis_size("y")
+    half_rows = assembled.shape[1]
+    z_count, y_count = lax.axis_size("z"), lax.axis_size("y")
+    groups = lax.axis_size("child") * y_count
     width = R // (2 * groups)
     child = lax.axis_index("child")
     row_pos = lax.axis_index(("z", "xl"))
     col_pos = lax.axis_index(("y", "core"))
+    sibling_block = lax.ppermute(contrib[0], "child", SWAP)
     columns = lax.dynamic_slice_in_dim(row_maps, col_pos * tile_cols, tile_cols, 1) - col_pos * window_rows
     targets = lax.dynamic_slice_in_dim(row_maps, row_pos * tile_rows, tile_rows, 1) - row_pos * window_rows
+    maps = jnp.stack([columns, targets])
+    sibling_maps = lax.ppermute(maps, "child", SWAP)
     scalars = jnp.stack(
         [
             child,
@@ -312,20 +334,34 @@
         ]
     ).astype(jnp.int32)
 
-    own = lax.all_to_all(jnp.broadcast_to(omega.T, (z_count, own_count, window_rows)), "z", 0, 0)
-    top, low, built = build_operator(scalars, pattern, contrib[0], assembled[0], columns, targets)
+    copies = pl.pallas_call(
+        copies_kernel,
+        in_specs=[VMEM],
+        out_specs=VMEM,
+        out_shape=shape(z_count, own_count, window_rows),
+        compiler_params=PARAMS,
+    )(omega.T)
+    own = lax.all_to_all(copies, "z", 0, 0)
+    both_maps = jnp.concatenate([maps, sibling_maps], axis=1)
+    top, low, built = build_operator(
+        scalars, pattern, contrib[0], sibling_block, assembled[0], both_maps[0], both_maps[1]
+    )
     own, built = lax.optimization_barrier((own, built))
-    other = lax.ppermute(own, "xl", SWAP)
-
-    def half(gathered):
-        give, keep = apply_operator(scalars, built, gathered, top, low)
+    ring = lax.axis_size("child") * lax.axis_size("xl")
+    other = [
+        lax.ppermute(piece, ("child", "xl"), [(i, (i + step) % ring) for i in range(ring)])
+        for piece, step in ((own[: z_count // 2], 1), (own[z_count // 2 :], -1))
+    ]
+
+    def half(pieces):
+        give, keep = apply_operator(scalars, built, pieces, top, low)
         return keep + lax.ppermute(give, "core", SWAP)
 
-    parts = jnp.concatenate([half(own), half(other)], axis=0)
-    terms = lax.all_to_all(parts, ("child", "y"), 0, 0)
+    parts = jnp.concatenate([half([own]), half(other)], axis=1)
+    terms = lax.all_to_all(parts, "y", 0, 0)
     samples = jnp.sum(terms, axis=0)
     mine = lax.all_to_all(
-        jnp.broadcast_to(samples, (groups, width, window_rows)), ("child", "y"), 0, 0
+        jnp.broadcast_to(samples, (groups,) + samples.shape), ("child", "y"), 0, 0
     )
     theirs = lax.ppermute(mine, "core", SWAP)
 

time: 127 us -> 125 us (0.984)
  starting transfers between devices: 29.9 us -> 44.4 us
  blocking collectives: 46 us -> 36.4 us
  waiting for transfers between devices: 16.1 us -> 8.83 us
  Pallas kernels: 23.5 us -> 25.3 us
  local copies, waits for them, and re-layouts: 8.24 us -> 6.71 us
    ppermute x1 -> x4, starting transfers between devices: 3.11 us -> 17.3 us  [the longest x2 9.67 us: local(): lax.ppermute(piece, ('child', 'xl'), [(i, (i + step) % ring) for i in ran...]
    all_to_all x2, blocking collectives: 46 us -> 36.4 us  [the longest x1 18.6 us: local(): lax.all_to_all(jnp.broadcast_to(samples, (groups,) + samples.shape), ('ch...]
    all_to_all x1, waiting for transfers between devices: 6.07 us -> 0.01 us  [local(): own = lax.all_to_all(copies, 'z', 0, 0)]
    pallas_call x1, Pallas kernels: 5.61 us -> 7.45 us  [build_operator(): pl.pallas_call(operator_kernel, grid=(window_rows // BT,), in_specs=[SMEM...]
    broadcast_in_dim x2 -> x1, local copies, waits for them, and re-layouts: 1.75 us -> 0.05 us  [local(): jnp.broadcast_to(samples, (groups,) + samples.shape)]
    ppermute x1 -> x4, waiting for transfers between devices: 5.95 us -> 4.43 us  [the longest x1 4.42 us: local(): sibling_maps = lax.ppermute(maps, 'child', SWAP)]
    unnamed x10 -> x12, local copies, waits for them, and re-layouts: 6.4 us -> 6.54 us
    pallas_call x2 -> x3, Pallas kernels: 3.06 us -> 3.08 us  [the longest x2 2.25 us: apply_operator(): pl.pallas_call(apply_kernel, in_specs=[SMEM] + [VMEM] * (3 + len(lines)),...]
  transfers between devices with their start and end apart: 7 -> 10, of which waited for: 5 -> 4; matrix products, arithmetic and copies ran while one was open for 1% -> 1% of each run, Pallas kernels for 12% -> 14%
where the time goes in v4:
time: 125 us; the launch traced here: 124 us
  starting transfers between devices  44.4 us (36%)
  blocking collectives  36.4 us (29%)
  Pallas kernels  25.3 us (20%)
  waiting for transfers between devices  8.83 us (7%)
  local copies, waits for them, and re-layouts  6.71 us (5%)
  between operations  1.51 us (1%)
    all_to_all x1, blocking collectives, local(): lax.all_to_all(jnp.broadcast_to(samples, (groups,) + samples.shape), ('ch...  18.6 us
    all_to_all x1, blocking collectives, local(): terms = lax.all_to_all(parts, 'y', 0, 0)  17.8 us
    all_to_all x1, starting transfers between devices, local(): own = lax.all_to_all(copies, 'z', 0, 0)  10 us
    ppermute x2, starting transfers between devices, local(): lax.ppermute(piece, ('child', 'xl'), [(i, (i + step) % ring) for i in ran...  9.67 us
    pallas_call x1, Pallas kernels, build_operator(): pl.pallas_call(operator_kernel, grid=(window_rows // BT,), in_specs=[SMEM...  7.45 us
    pallas_call x1, Pallas kernels, factor_head(): pl.pallas_call(head_kernel, in_specs=[SMEM, VMEM, VMEM], out_specs=[VMEM]...  6.95 us
    ppermute x2, starting transfers between devices, half(): return keep + lax.ppermute(give, 'core', SWAP)  6.94 us
    unnamed x12, local copies, waits for them, and re-layouts  6.54 us
  transfers between devices with their start and end apart: 10, of which 4 were waited for; matrix products, arithmetic and copies ran while one was open for 1% of the time, Pallas kernels for 14%

profile of v4, /device:TPU:1, one launch (start us, length us, event | category | flops | bytes accessed | tf_op | source)
XLA Modules:
  0.0 123.9 jit_solution(9688694225899226316)
XLA Ops:
  0.6 5.5 %collective-permute-start = (f32[512,512]{1,0:T(8,128)}, f32[512,512]{1,0:T(8,128)S(1)}, u32[]{:S(2)}, u32[]{:S(2)}) collective-permute-start(f32[512,512]{1,0:T(8,128)} %bitcast.23), channel_id=1, source_target_pairs={{0,256},{256,0},{1,257},{257,1},{2,258},{258,2},{3,259},{259,3},{4... | collective-permute-start | bytes 3145736 | tf_op jit(solution)/shard_map/ppermute | solution.py:322
  6.1 0.0 copy-start
  6.1 0.8 copy-done
  7.0 0.8 shard_map.77
  7.8 10.0 %all-to-all-start = ((f32[8,16,1024]{2,1,0:T(8,128)}), f32[8,16,1024]{2,1,0:T(8,128)S(1)}, u32[]{:S(2)}, u32[]{:S(2)}) async-start(f32[8,16,1024]{2,1,0:T(8,128)} %shard_map.77), calls=%async_computation | async-start | bytes 1048576 | tf_op jit(solution)/shard_map/all_to_all | solution.py:344
  17.8 0.7 subtract_bitcast_fusion.1
  18.5 2.1 %collective-permute-start.1 = (s32[2,1,512]{2,1,0:T(1,128)S(1)}, s32[2,1,512]{2,1,0:T(1,128)S(1)}, u32[]{:S(2)}, u32[]{:S(2)}) collective-permute-start(s32[2,1,512]{2,1,0:T(1,128)S(1)} %pad_add_fusion.1), channel_id=1, source_target_pairs={{0,256},{256,0},{1,257},{257,1},{2,258},{258,2},{3,259},{259,3},{4... | collective-permute-start | bytes 12296 | tf_op jit(solution)/shard_map/ppermute | solution.py:326
  21.3 0.1 stack.28.scalars
  21.4 4.4 %collective-permute-done.1 = s32[2,1,512]{2,1,0:T(1,128)S(1)} collective-permute-done((s32[2,1,512]{2,1,0:T(1,128)S(1)}, s32[2,1,512]{2,1,0:T(1,128)S(1)}, u32[]{:S(2)}, u32[]{:S(2)}) %collective-permute-start.1) | collective-permute-done | bytes 4128 | tf_op jit(solution)/shard_map/ppermute | solution.py:326
  25.9 0.0 collective-permute-done.sibling
  25.9 0.0 copy-start.1
  25.9 1.6 %copy-done.1 = f32[1,512,1024]{2,1,0:T(8,128)S(1)} copy-done((f32[1,512,1024]{2,1,0:T(8,128)S(1)}, f32[1,512,1024]{2,1,0:T(8,128)}, u32[]{:S(2)}) %copy-start.1) | copy-done | bytes 2097176
  27.5 0.0 copy-start.2
  27.5 1.2 copy-done.2
  28.7 0.0 copy-start.3
  28.7 0.7 copy-done.3
  29.4 7.5 %shard_map.78 = (bf16[1024,512]{1,0:T(8,128)(2,1)S(1)}, bf16[1024,512]{1,0:T(8,128)(2,1)S(1)}, f32[8,128]{1,0:T(8,128)S(1)}) custom-call(s32[5]{0:T(128)S(1)} %stack.28.scalars, s32[4,4]{1,0:T(4,128)S(1)} %copy-done.3, f32[512,512]{1,0:T(8,128)S(1)} %bitcast.24, f32[512,512]{1,0:T(8,128)S(1)} %collective-permute-done.sibling, f32[512,1024]{1,0:T(8,128)S(1)} %bitcast.22, ...), custom_call_target="tpu_custom_call" | custom-call | flops 4000000000 | bytes 8000000 | tf_op jit(solution)/shard_map/pallas_call | solution.py:76
  36.8 0.0 copy-start.4
  36.8 1.0 copy-done.4
  37.8 0.0 all-to-all-done
  37.9 6.5 %collective-permute-start.3 = (f32[4,16,1024]{2,1,0:T(8,128)S(1)}, f32[4,16,1024]{2,1,0:T(8,128)S(1)}, u32[]{:S(2)}, u32[]{:S(2)}) collective-permute-start(f32[4,16,1024]{2,1,0:T(8,128)S(1)} %get-tuple-element.35), channel_id=1, source_target_pairs={{0,16},{16,256},{256,272},{272,0},{1,17},{17,257},{257,273},{273,1... | collective-permute-start | bytes 786440 | tf_op jit(solution)/shard_map/ppermute | solution.py:352
  44.4 3.2 %collective-permute-start.4 = (f32[4,16,1024]{2,1,0:T(8,128)S(1)}, f32[4,16,1024]{2,1,0:T(8,128)S(1)}, u32[]{:S(2)}, u32[]{:S(2)}) collective-permute-start(f32[4,16,1024]{2,1,0:T(8,128)S(1)} %get-tuple-element.34), channel_id=1, source_target_pairs={{0,272},{16,0},{256,16},{272,256},{1,273},{17,1},{257,17},{273,257... | collective-permute-start | bytes 786440 | tf_op jit(solution)/shard_map/ppermute | solution.py:352
  47.6 0.0 copy-start.5
  47.6 1.2 copy-done.5
  48.8 1.1 shard_map.79
  49.9 4.0 %collective-permute-start.2 = (f32[8,8,512]{2,1,0:T(8,128)S(1)}, f32[8,8,512]{2,1,0:T(8,128)S(1)}, u32[]{:S(2)}, u32[]{:S(2)}) collective-permute-start(f32[8,8,512]{2,1,0:T(8,128)S(1)} %get-tuple-element.24), channel_id=1, source_target_pairs={{0,1},{1,0},{2,3},{3,2},{4,5},{5,4},{6,7},{7,6},{8,9},{9,8},{10,11... | collective-permute-start | bytes 393224 | tf_op jit(solution)/shard_map/ppermute | solution.py:358
  53.9 0.0 collective-permute-done.3
  53.9 0.0 collective-permute-done.4
  53.9 1.1 shard_map.80
  55.1 3.0 %collective-permute-start.5 = (f32[8,8,512]{2,1,0:T(8,128)S(1)}, f32[8,8,512]{2,1,0:T(8,128)S(1)}, u32[]{:S(2)}, u32[]{:S(2)}) collective-permute-start(f32[8,8,512]{2,1,0:T(8,128)S(1)} %get-tuple-element.26), channel_id=1, source_target_pairs={{0,1},{1,0},{2,3},{3,2},{4,5},{5,4},{6,7},{7,6},{8,9},{9,8},{10,11... | collective-permute-start | bytes 393224 | tf_op jit(solution)/shard_map/ppermute | solution.py:358
  58.0 0.0 collective-permute-done.2
  58.1 0.9 collective-permute-done.5
  59.0 17.8 %all_to_all.15 = f32[8,16,512]{2,1,0:T(8,128)S(1)} all-to-all(f32[8,16,512]{2,1,0:T(8,128)S(1)} %pad_maximum_fusion), channel_id=1, replica_groups=mesh['child'=2,'z'=8,'xl'=2,'y'=8,'core'=2] {'y'}, dimensions={0} | all-to-all | bytes 524288 | tf_op jit(solution)/shard_map/all_to_all | solution.py:361
  76.8 0.1 broadcast_in_dim.6
  76.9 18.6 %all_to_all.16.mine = f32[16,16,512]{2,1,0:T(8,128)S(1)} all-to-all(f32[16,16,512]{2,1,0:T(8,128)S(1)} %broadcast_in_dim.6), channel_id=1, replica_groups=mesh['child'=2,'z'=8,'xl'=2,'y'=8,'core'=2] {'child','y'}, dimensions={0} | all-to-all | bytes 1048576 | tf_op jit(solution)/shard_map/all_to_all | solution.py:363
  95.5 4.9 %collective-permute-start.6 = (f32[16,16,512]{2,1,0:T(8,128)S(1)}, f32[16,16,512]{2,1,0:T(8,128)S(1)}, u32[]{:S(2)}, u32[]{:S(2)}) collective-permute-start(f32[16,16,512]{2,1,0:T(8,128)S(1)} %all_to_all.16.mine), channel_id=1, source_target_pairs={{0,1},{1,0},{2,3},{3,2},{4,5},{5,4},{6,7},{7,6},{8,9},{9,8},{10,11... | collective-permute-start | bytes 1572872 | tf_op jit(solution)/shard_map/ppermute | solution.py:366
  100.3 1.5 %collective-permute-done.6.theirs = f32[16,16,512]{2,1,0:T(8,128)S(1)} collective-permute-done((f32[16,16,512]{2,1,0:T(8,128)S(1)}, f32[16,16,512]{2,1,0:T(8,128)S(1)}, u32[]{:S(2)}, u32[]{:S(2)}) %collective-permute-start.6) | collective-permute-done | bytes 524320 | tf_op jit(solution)/shard_map/ppermute | solution.py:366
  101.8 7.0 %shard_map.81 = (f32[256,1024]{1,0:T(8,128)S(1)}, f32[2,128,256]{2,1,0:T(8,128)S(1)}, f32[2,128,128]{2,1,0:T(8,128)S(1)}, f32[2,128,256]{2,1,0:T(8,128)S(1)}) custom-call(s32[5]{0:T(128)S(1)} %stack.28.scalars, f32[16,16,512]{2,1,0:T(8,128)S(1)} %all_to_all.16.mine, f32[16,16,512]{2,1,0:T(8,128)S(1)} %collective-permute-done.6.theirs), custom_call_target="tpu_custom_call" | custom-call | tf_op jit(solution)/shard_map/pallas_call | solution.py:246
  108.8 2.7 %collective-permute-start.7 = (f32[2,128,256]{2,1,0:T(8,128)S(1)}, f32[2,128,256]{2,1,0:T(8,128)S(1)}, u32[]{:S(2)}, u32[]{:S(2)}) collective-permute-start(f32[2,128,256]{2,1,0:T(8,128)S(1)} %get-tuple-element.28.u_head), channel_id=1, source_target_pairs={{0,16},{16,0},{1,17},{17,1},{2,18},{18,2},{3,19},{19,3},{4,20},{20... | collective-permute-start | bytes 786440 | tf_op jit(solution)/shard_map/ppermute | solution.py:369
  111.5 5.0 %shard_map.82 = (f32[2,128,128]{2,1,0:T(8,128)S(1)}, f32[2,8,256]{2,1,0:T(8,128)S(1)}, f32[2,8,256]{2,1,0:T(8,128)S(1)}) custom-call(s32[5]{0:T(128)S(1)} %stack.28.scalars, f32[2,128,256]{2,1,0:T(8,128)S(1)} %get-tuple-element.28.u_head, f32[2,128,128]{2,1,0:T(8,128)S(1)} %get-tuple-element.29.x_head, f32[2,128,256]{2,1,0:T(8,128)S(1)} %get-tuple-element.30.rest), custom_call_target="tpu_custom_call" | custom-call | flops 8000000000 | bytes 1000000 | tf_op jit(solution)/shard_map/pallas_call | solution.py:287
  116.5 2.6 %collective-permute-start.8 = (f32[2,128,128]{2,1,0:T(8,128)S(1)}, f32[2,128,128]{2,1,0:T(8,128)S(1)}, u32[]{:S(2)}, u32[]{:S(2)}) collective-permute-start(f32[2,128,128]{2,1,0:T(8,128)S(1)} %get-tuple-element.33), channel_id=1, source_target_pairs={{0,16},{16,0},{1,17},{17,1},{2,18},{18,2},{3,19},{19,3},{4,20},{20... | collective-permute-start | bytes 393224 | tf_op jit(solution)/shard_map/ppermute | solution.py:371
  119.1 1.8 %shard_map.83 = f32[8,1024]{1,0:T(8,128)} custom-call(s32[5]{0:T(128)S(1)} %stack.28.scalars, f32[256,1024]{1,0:T(8,128)S(1)} %get-tuple-element.27.window, f32[2,8,256]{2,1,0:T(8,128)S(1)} %get-tuple-element.31.x_own), custom_call_target="tpu_custom_call" | custom-call | flops 1000000000 | bytes 1000000 | tf_op jit(solution)/shard_map/pallas_call | solution.py:372
  120.8 1.9 %collective-permute-done.8.sib_tail = f32[2,128,128]{2,1,0:T(8,128)S(1)} collective-permute-done((f32[2,128,128]{2,1,0:T(8,128)S(1)}, f32[2,128,128]{2,1,0:T(8,128)S(1)}, u32[]{:S(2)}, u32[]{:S(2)}) %collective-permute-start.8) | collective-permute-done | bytes 131104 | tf_op jit(solution)/shard_map/ppermute | solution.py:371
  122.8 0.0 collective-permute-done.7.sib_head
  122.8 1.1 shard_map.84
  (8 shorter events, 0.1 us)
Async XLA Ops:
  0.6 25.2 %collective-permute-start = (f32[512,512]{1,0:T(8,128)}, f32[512,512]{1,0:T(8,128)S(1)}, u32[]{:S(2)}, u32[]{:S(2)}) collective-permute-start(f32[512,512]{1,0:T(8,128)} %bitcast.23), channel_id=1, source_target_pairs={{0,256},{256,0},{1,257},{257,1},{2,258},{258,2},{3,259},{259,3},{4... | collective-permute-start | bytes 3145736 | tf_op jit(solution)/shard_map/ppermute | solution.py:322
  6.1 0.8 copy-start
  7.8 30.0 %all-to-all-start = ((f32[8,16,1024]{2,1,0:T(8,128)}), f32[8,16,1024]{2,1,0:T(8,128)S(1)}, u32[]{:S(2)}, u32[]{:S(2)}) async-start(f32[8,16,1024]{2,1,0:T(8,128)} %shard_map.77), calls=%async_computation | async-start | bytes 1048576 | tf_op jit(solution)/shard_map/all_to_all | solution.py:344
  18.5 7.3 %collective-permute-start.1 = (s32[2,1,512]{2,1,0:T(1,128)S(1)}, s32[2,1,512]{2,1,0:T(1,128)S(1)}, u32[]{:S(2)}, u32[]{:S(2)}) collective-permute-start(s32[2,1,512]{2,1,0:T(1,128)S(1)} %pad_add_fusion.1), channel_id=1, source_target_pairs={{0,256},{256,0},{1,257},{257,1},{2,258},{258,2},{3,259},{259,3},{4... | collective-permute-start | bytes 12296 | tf_op jit(solution)/shard_map/ppermute | solution.py:326
  25.9 1.6 %copy-start.1 = (f32[1,512,1024]{2,1,0:T(8,128)S(1)}, f32[1,512,1024]{2,1,0:T(8,128)}, u32[]{:S(2)}) copy-start(f32[1,512,1024]{2,1,0:T(8,128)} %param.7) | copy-start | bytes 6291460
  27.5 1.2 copy-start.2
  28.7 0.7 copy-start.3
  36.8 1.0 copy-start.4
  37.9 16.0 %collective-permute-start.3 = (f32[4,16,1024]{2,1,0:T(8,128)S(1)}, f32[4,16,1024]{2,1,0:T(8,128)S(1)}, u32[]{:S(2)}, u32[]{:S(2)}) collective-permute-start(f32[4,16,1024]{2,1,0:T(8,128)S(1)} %get-tuple-element.35), channel_id=1, source_target_pairs={{0,16},{16,256},{256,272},{272,0},{1,17},{17,257},{257,273},{273,1... | collective-permute-start | bytes 786440 | tf_op jit(solution)/shard_map/ppermute | solution.py:352
  44.4 9.6 %collective-permute-start.4 = (f32[4,16,1024]{2,1,0:T(8,128)S(1)}, f32[4,16,1024]{2,1,0:T(8,128)S(1)}, u32[]{:S(2)}, u32[]{:S(2)}) collective-permute-start(f32[4,16,1024]{2,1,0:T(8,128)S(1)} %get-tuple-element.34), channel_id=1, source_target_pairs={{0,272},{16,0},{256,16},{272,256},{1,273},{17,1},{257,17},{273,257... | collective-permute-start | bytes 786440 | tf_op jit(solution)/shard_map/ppermute | solution.py:352
  47.6 1.2 copy-start.5
  49.9 8.1 %collective-permute-start.2 = (f32[8,8,512]{2,1,0:T(8,128)S(1)}, f32[8,8,512]{2,1,0:T(8,128)S(1)}, u32[]{:S(2)}, u32[]{:S(2)}) collective-permute-start(f32[8,8,512]{2,1,0:T(8,128)S(1)} %get-tuple-element.24), channel_id=1, source_target_pairs={{0,1},{1,0},{2,3},{3,2},{4,5},{5,4},{6,7},{7,6},{8,9},{9,8},{10,11... | collective-permute-start | bytes 393224 | tf_op jit(solution)/shard_map/ppermute | solution.py:358
  55.1 3.9 %collective-permute-start.5 = (f32[8,8,512]{2,1,0:T(8,128)S(1)}, f32[8,8,512]{2,1,0:T(8,128)S(1)}, u32[]{:S(2)}, u32[]{:S(2)}) collective-permute-start(f32[8,8,512]{2,1,0:T(8,128)S(1)} %get-tuple-element.26), channel_id=1, source_target_pairs={{0,1},{1,0},{2,3},{3,2},{4,5},{5,4},{6,7},{7,6},{8,9},{9,8},{10,11... | collective-permute-start | bytes 393224 | tf_op jit(solution)/shard_map/ppermute | solution.py:358
  95.5 6.4 %collective-permute-start.6 = (f32[16,16,512]{2,1,0:T(8,128)S(1)}, f32[16,16,512]{2,1,0:T(8,128)S(1)}, u32[]{:S(2)}, u32[]{:S(2)}) collective-permute-start(f32[16,16,512]{2,1,0:T(8,128)S(1)} %all_to_all.16.mine), channel_id=1, source_target_pairs={{0,1},{1,0},{2,3},{3,2},{4,5},{5,4},{6,7},{7,6},{8,9},{9,8},{10,11... | collective-permute-start | bytes 1572872 | tf_op jit(solution)/shard_map/ppermute | solution.py:366
  108.8 14.0 %collective-permute-start.7 = (f32[2,128,256]{2,1,0:T(8,128)S(1)}, f32[2,128,256]{2,1,0:T(8,128)S(1)}, u32[]{:S(2)}, u32[]{:S(2)}) collective-permute-start(f32[2,128,256]{2,1,0:T(8,128)S(1)} %get-tuple-element.28.u_head), channel_id=1, source_target_pairs={{0,16},{16,0},{1,17},{17,1},{2,18},{18,2},{3,19},{19,3},{4,20},{20... | collective-permute-start | bytes 786440 | tf_op jit(solution)/shard_map/ppermute | solution.py:369
  116.5 6.3 %collective-permute-start.8 = (f32[2,128,128]{2,1,0:T(8,128)S(1)}, f32[2,128,128]{2,1,0:T(8,128)S(1)}, u32[]{:S(2)}, u32[]{:S(2)}) collective-permute-start(f32[2,128,128]{2,1,0:T(8,128)S(1)} %get-tuple-element.33), channel_id=1, source_target_pairs={{0,16},{16,0},{1,17},{17,1},{2,18},{18,2},{3,19},{19,3},{4,20},{20... | collective-permute-start | bytes 393224 | tf_op jit(solution)/shard_map/ppermute | solution.py:371

commit v5 on v4

--- a/solution.py
+++ b/solution.py
@@ -38,62 +38,74 @@
         out[copy] = lines[...]
 
 
-def operator_kernel(scalars, pattern, own, sibling, assembled, columns, targets, top, low, built, parts, spread):
-    step = pl.program_id(0)
+def child_terms(child, block, targets, spread_rows, half_rows):
+    places = lax.broadcasted_iota(jnp.int32, (half_rows, targets.shape[1]), 0) + child * half_rows
+    spread = (places == targets[...]).astype(f32).astype(bf16)
+    for part, piece in enumerate(two_parts(block[...])):
+        spread_rows[part] = dot(spread, piece, NN).astype(bf16)
+
+
+def picked_terms(columns, spread_rows, start, rows):
+    places = lax.broadcasted_iota(jnp.int32, (rows, columns.shape[1]), 0) + start
+    pick = (places == columns[...]).astype(f32).astype(bf16)
+    return dot(pick, spread_rows[0], NT) + dot(pick, spread_rows[1], NT)
+
+
+def own_kernel(scalars, pattern, block, assembled, columns, targets, total, built, spread_rows):
     child = scalars[0]
-    rows, half_rows = top.shape
-    tile_cols = own.shape[1]
-
-    @pl.when(step == 0)
-    def _():
-        places = lax.broadcasted_iota(jnp.int32, (half_rows, targets.shape[1]), 0) + child * half_rows
-        for source, block in enumerate((own, sibling)):
-            parts[source, 0], parts[source, 1] = two_parts(block[...])
-            spread[source] = (places == targets[source : source + 1, :]).astype(f32).astype(bf16)
-        built[...] = jnp.zeros_like(built)
-
-    places = lax.broadcasted_iota(jnp.int32, (rows, tile_cols), 0) + step * rows
-    total = jnp.zeros((rows, half_rows), f32)
-    for source in range(2):
-        pick = (places == columns[source : source + 1, :]).astype(f32).astype(bf16)
-        for part in range(2):
-            picked = dot(pick, parts[source, part], NT).astype(bf16)
-            total = total + dot(picked, spread[source], NT)
+    window_rows, half_rows = total.shape
+    child_terms(child, block, targets, spread_rows, half_rows)
     tiles = half_rows // BT
-    for tile in range(tiles):
-        keep = pattern[child * tiles + tile, step].astype(f32)
-        lanes = slice(tile * BT, (tile + 1) * BT)
-        entries = assembled[lanes, :].T
-        top[:, lanes], low[:, lanes] = two_parts(total[:, lanes] + entries * keep)
-
-
-def build_operator(scalars, pattern, own, sibling, assembled, columns, targets):
-    tile_rows, tile_cols = own.shape
-    window_rows = assembled.shape[1]
-    half_rows = assembled.shape[0]
-    block = pl.BlockSpec((BT, half_rows), lambda i: (i, 0))
-    whole = pl.BlockSpec((tile_rows, tile_cols), lambda i: (0, 0))
+    for step in range(window_rows // BT):
+        rows = slice(step * BT, (step + 1) * BT)
+        terms = picked_terms(columns, spread_rows, step * BT, BT)
+        for tile in range(tiles):
+            keep = pattern[child * tiles + tile, step].astype(f32)
+            lanes = slice(tile * BT, (tile + 1) * BT)
+            total[rows, lanes] = terms[:, lanes] + assembled[lanes, rows].T * keep
+    built[...] = jnp.zeros_like(built)
+
+
+def sibling_kernel(scalars, own_total, block, maps, top, low, spread_rows, total, arrived):
+    window_rows, half_rows = total.shape
+    fetch = pltpu.make_async_copy(own_total, total, arrived)
+    fetch.start()
+    child_terms(scalars[0], block, maps.at[1], spread_rows, half_rows)
+    fetch.wait()
+    for step in range(window_rows // BT):
+        rows = slice(step * BT, (step + 1) * BT)
+        terms = picked_terms(maps.at[0], spread_rows, step * BT, BT)
+        top[rows, :], low[rows, :] = two_parts(total[rows, :] + terms)
+
+
+def own_operator(scalars, pattern, block, assembled, columns, targets):
+    half_rows, window_rows = assembled.shape
     return pl.pallas_call(
-        operator_kernel,
-        grid=(window_rows // BT,),
-        in_specs=[
-            SMEM,
-            SMEM,
-            whole,
-            whole,
-            pl.BlockSpec((half_rows, BT), lambda i: (0, i)),
-            pl.BlockSpec((2, tile_cols), lambda i: (0, 0)),
-            pl.BlockSpec((2, tile_rows), lambda i: (0, 0)),
+        own_kernel,
+        in_specs=[SMEM, SMEM] + [VMEM] * 4,
+        out_specs=[VMEM, VMEM],
+        out_shape=[shape(window_rows, half_rows), shape(8, 128)],
+        scratch_shapes=[pltpu.VMEM((2, half_rows, block.shape[1]), bf16)],
+        compiler_params=PARAMS,
+        cost_estimate=pl.CostEstimate(flops=2 * 10**9, bytes_accessed=5 * 10**6, transcendentals=0),
+    )(scalars, pattern, block, assembled, columns, targets)
+
+
+def whole_operator(scalars, total, block, maps):
+    window_rows, half_rows = total.shape
+    return pl.pallas_call(
+        sibling_kernel,
+        in_specs=[SMEM, pl.BlockSpec(memory_space=pltpu.HBM)] + [VMEM] * 2,
+        out_specs=[VMEM, VMEM],
+        out_shape=[shape(window_rows, half_rows, dtype=bf16)] * 2,
+        scratch_shapes=[
+            pltpu.VMEM((2, half_rows, block.shape[1]), bf16),
+            pltpu.VMEM((window_rows, half_rows), f32),
+            pltpu.SemaphoreType.DMA,
         ],
-        out_specs=[block, block, pl.BlockSpec((8, 128), lambda i: (0, 0))],
-        out_shape=[shape(window_rows, half_rows, dtype=bf16)] * 2 + [shape(8, 128)],
-        scratch_shapes=[
-            pltpu.VMEM((2, 2, tile_rows, tile_cols), bf16),
-            pltpu.VMEM((2, half_rows, tile_rows), bf16),
-        ],
-        compiler_params=PARAMS,
-        cost_estimate=pl.CostEstimate(flops=4 * 10**9, bytes_accessed=8 * 10**6, transcendentals=0),
-    )(scalars, pattern, own, sibling, assembled, columns, targets)
+        compiler_params=PARAMS,
+        cost_estimate=pl.CostEstimate(flops=2 * 10**9, bytes_accessed=5 * 10**6, transcendentals=0),
+    )(scalars, total, block, maps)
 
 
 def apply_kernel(scalars, built, *refs):
@@ -219,8 +231,13 @@
     lane = lax.broadcasted_iota(jnp.int32, (R, edge), 1)
     head = window[:, :edge]
     tail = window[:, window_rows - edge :]
-    gram[0] = dot(jnp.where(lane < bound, head, 0.0), head, NT, highest)
-    gram[1] = dot(jnp.where(lane + (window_rows - edge) < bound, 0.0, tail), tail, NT, highest)
+    for leaf, (inside, leaf_rows) in enumerate(
+        ((lane < bound, head), (lane + (window_rows - edge) >= bound, tail))
+    ):
+        high_rows, low_rows = two_parts(leaf_rows)
+        masked = two_parts(jnp.where(inside, leaf_rows, 0.0))[0]
+        cross = dot(masked, low_rows, NT)
+        gram[leaf] = dot(masked, high_rows, NT) + cross + cross.T
     blocks = (s0, s1)
     for leaf in range(2):
         rows = jnp.where(leaf == 0, bound, window_rows - bound)
@@ -342,16 +359,16 @@
         compiler_params=PARAMS,
     )(omega.T)
     own = lax.all_to_all(copies, "z", 0, 0)
-    both_maps = jnp.concatenate([maps, sibling_maps], axis=1)
-    top, low, built = build_operator(
-        scalars, pattern, contrib[0], sibling_block, assembled[0], both_maps[0], both_maps[1]
-    )
+    total, built = own_operator(scalars, pattern, contrib[0], assembled[0], columns, targets)
     own, built = lax.optimization_barrier((own, built))
     ring = lax.axis_size("child") * lax.axis_size("xl")
     other = [
         lax.ppermute(piece, ("child", "xl"), [(i, (i + step) % ring) for i in range(ring)])
         for piece, step in ((own[: z_count // 2], 1), (own[z_count // 2 :], -1))
     ]
+
+    sibling_block, sibling_maps = lax.optimization_barrier((sibling_block, sibling_maps))
+    top, low = whole_operator(scalars, total, sibling_block, sibling_maps)
 
     def half(pieces):
         give, keep = apply_operator(scalars, built, pieces, top, low)

time: 125 us -> 122 us (0.976)
  starting transfers between devices: 44.4 us -> 41.5 us
  Pallas kernels: 25.3 us -> 22.5 us
  blocking collectives: 36.4 us -> 37.9 us
    ppermute x2, starting transfers between devices: 9.67 us -> 6.49 us  [local(): lax.ppermute(piece, ('child', 'xl'), [(i, (i + step) % ring) for i in ran...]
    all_to_all x1, waiting for transfers between devices: 0.01 us -> 2.33 us  [local(): own = lax.all_to_all(copies, 'z', 0, 0)]
    pallas_call x1 -> x2, Pallas kernels: 7.45 us -> 5.42 us  [the longest x1 2.88 us: whole_operator(): pl.pallas_call(sibling_kernel, in_specs=[SMEM, pl.BlockSpec(memory_space=...]
    ppermute x1, waiting for transfers between devices: 4.42 us -> 2.93 us  [local(): sibling_maps = lax.ppermute(maps, 'child', SWAP)]
  transfers between devices with their start and end apart: 10 -> 10, of which waited for: 4 -> 5; matrix products, arithmetic and copies ran while one was open for 1% -> 1% of each run, Pallas kernels for 14% -> 12%
where the time goes in v5:
time: 122 us; the launch traced here: 121 us
  starting transfers between devices  41.5 us (34%)
  blocking collectives  37.9 us (31%)
  Pallas kernels  22.5 us (18%)
  waiting for transfers between devices  9.5 us (8%)
  local copies, waits for them, and re-layouts  7.41 us (6%)
  between operations  1.5 us (1%)
    all_to_all x1, blocking collectives, local(): lax.all_to_all(jnp.broadcast_to(samples, (groups,) + samples.shape), ('ch...  19 us
    all_to_all x1, blocking collectives, local(): terms = lax.all_to_all(parts, 'y', 0, 0)  18.9 us
    all_to_all x1, starting transfers between devices, local(): own = lax.all_to_all(copies, 'z', 0, 0)  10.9 us
    unnamed x12, local copies, waits for them, and re-layouts  7.24 us
    ppermute x2, starting transfers between devices, half(): return keep + lax.ppermute(give, 'core', SWAP)  7.13 us
    ppermute x2, starting transfers between devices, local(): lax.ppermute(piece, ('child', 'xl'), [(i, (i + step) % ring) for i in ran...  6.49 us
    pallas_call x1, Pallas kernels, factor_head(): pl.pallas_call(head_kernel, in_specs=[SMEM, VMEM, VMEM], out_specs=[VMEM]...  6.18 us
    pallas_call x1, Pallas kernels, factor_tail(): pl.pallas_call(tail_kernel, in_specs=[SMEM] + [VMEM] * 3, out_specs=[VMEM...  4.98 us
  transfers between devices with their start and end apart: 10, of which 5 were waited for; matrix products, arithmetic and copies ran while one was open for 1% of the time, Pallas kernels for 12%

profile of v5, /device:TPU:1, one launch (start us, length us, event | category | flops | bytes accessed | tf_op | source)
XLA Modules:
  0.0 121.1 jit_solution(897217865365088760)
XLA Ops:
  0.6 0.0 copy-start
  0.6 0.8 copy-done
  1.5 0.8 shard_map.77
  2.3 10.9 %all-to-all-start = ((f32[8,16,1024]{2,1,0:T(8,128)}), f32[8,16,1024]{2,1,0:T(8,128)S(1)}, u32[]{:S(2)}, u32[]{:S(2)}) async-start(f32[8,16,1024]{2,1,0:T(8,128)} %shard_map.77), calls=%async_computation | async-start | bytes 1048576 | tf_op jit(solution)/shard_map/all_to_all | solution.py:361
  13.2 4.6 %collective-permute-start = (f32[512,512]{1,0:T(8,128)}, f32[512,512]{1,0:T(8,128)S(1)}, u32[]{:S(2)}, u32[]{:S(2)}) collective-permute-start(f32[512,512]{1,0:T(8,128)} %bitcast.19), channel_id=1, source_target_pairs={{0,256},{256,0},{1,257},{257,1},{2,258},{258,2},{3,259},{259,3},{4... | collective-permute-start | bytes 3145736 | tf_op jit(solution)/shard_map/ppermute | solution.py:339
  17.8 0.7 dynamic-slice_subtract_fusion
  18.5 2.1 %collective-permute-start.1 = (s32[2,1,512]{2,1,0:T(1,128)S(1)}, s32[2,1,512]{2,1,0:T(1,128)S(1)}, u32[]{:S(2)}, u32[]{:S(2)}) collective-permute-start(s32[2,1,512]{2,1,0:T(1,128)S(1)} %pad_add_fusion), channel_id=1, source_target_pairs={{0,256},{256,0},{1,257},{257,1},{2,258},{258,2},{3,259},{259,3},{4... | collective-permute-start | bytes 12296 | tf_op jit(solution)/shard_map/ppermute | solution.py:343
  21.3 0.1 stack.28.scalars
  21.4 0.0 copy-start.1
  21.4 1.6 %copy-done.1 = f32[1,512,1024]{2,1,0:T(8,128)S(1)} copy-done((f32[1,512,1024]{2,1,0:T(8,128)S(1)}, f32[1,512,1024]{2,1,0:T(8,128)}, u32[]{:S(2)}) %copy-start.1) | copy-done | bytes 2097176
  23.0 0.0 copy-start.2
  23.0 1.2 %copy-done.2 = f32[1,512,512]{2,1,0:T(8,128)S(1)} copy-done((f32[1,512,512]{2,1,0:T(8,128)S(1)}, f32[1,512,512]{2,1,0:T(8,128)}, u32[]{:S(2)}) %copy-start.2) | copy-done | bytes 1048600
  24.2 0.0 copy-start.3
  24.2 0.7 copy-done.3
  24.9 2.5 %shard_map.78 = (f32[1024,512]{1,0:T(8,128)S(1)}, f32[8,128]{1,0:T(8,128)S(1)}) custom-call(s32[5]{0:T(128)S(1)} %stack.28.scalars, s32[4,4]{1,0:T(4,128)S(1)} %copy-done.3, f32[512,512]{1,0:T(8,128)S(1)} %bitcast.20, f32[512,1024]{1,0:T(8,128)S(1)} %bitcast.18, s32[1,512]{1,0:T(1,128)S(1)} %get-tuple-element.43.columns, s32[1,512]{1,0:T(1,128)S(1)} %get-tuple-element.42.targets), custom_call_target="tpu_custom_call" | custom-call | flops 2000000000 | bytes 5000000 | tf_op jit(solution)/shard_map/pallas_call | solution.py:83
  27.5 0.0 copy-start.4
  27.5 1.3 %copy-done.4 = f32[1024,512]{1,0:T(8,128)} copy-done((f32[1024,512]{1,0:T(8,128)}, f32[1024,512]{1,0:T(8,128)S(1)}, u32[]{:S(2)}) %copy-start.4) | copy-done | bytes 2097176
  28.8 2.3 %all-to-all-done = f32[8,16,1024]{2,1,0:T(8,128)S(1)} async-done(((f32[8,16,1024]{2,1,0:T(8,128)}), f32[8,16,1024]{2,1,0:T(8,128)S(1)}, u32[]{:S(2)}, u32[]{:S(2)}) %all-to-all-start) | async-done | bytes 524320 | tf_op jit(solution)/shard_map/all_to_all | solution.py:361
  31.2 3.1 %collective-permute-start.3 = (f32[4,16,1024]{2,1,0:T(8,128)S(1)}, f32[4,16,1024]{2,1,0:T(8,128)S(1)}, u32[]{:S(2)}, u32[]{:S(2)}) collective-permute-start(f32[4,16,1024]{2,1,0:T(8,128)S(1)} %get-tuple-element.41), channel_id=1, source_target_pairs={{0,16},{16,256},{256,272},{272,0},{1,17},{17,257},{257,273},{273,1... | collective-permute-start | bytes 786440 | tf_op jit(solution)/shard_map/ppermute | solution.py:366
  34.3 3.4 %collective-permute-start.4 = (f32[4,16,1024]{2,1,0:T(8,128)S(1)}, f32[4,16,1024]{2,1,0:T(8,128)S(1)}, u32[]{:S(2)}, u32[]{:S(2)}) collective-permute-start(f32[4,16,1024]{2,1,0:T(8,128)S(1)} %get-tuple-element.40), channel_id=1, source_target_pairs={{0,272},{16,0},{256,16},{272,256},{1,273},{17,1},{257,17},{273,257... | collective-permute-start | bytes 786440 | tf_op jit(solution)/shard_map/ppermute | solution.py:366
  37.7 2.9 %collective-permute-done.1.maps = s32[2,1,512]{2,1,0:T(1,128)S(1)} collective-permute-done((s32[2,1,512]{2,1,0:T(1,128)S(1)}, s32[2,1,512]{2,1,0:T(1,128)S(1)}, u32[]{:S(2)}, u32[]{:S(2)}) %collective-permute-start.1) | collective-permute-done | bytes 4128 | tf_op jit(solution)/shard_map/ppermute | solution.py:343
  40.6 0.0 collective-permute-done.block
  40.6 0.0 copy-start.5
  40.6 1.6 %copy-done.5 = f32[1024,512]{1,0:T(8,128)S(1)} copy-done((f32[1024,512]{1,0:T(8,128)S(1)}, f32[1024,512]{1,0:T(8,128)}, u32[]{:S(2)}) %copy-start.5) | copy-done | bytes 2097176
  42.2 2.9 %shard_map.79 = (bf16[1024,512]{1,0:T(8,128)(2,1)S(1)}, bf16[1024,512]{1,0:T(8,128)(2,1)S(1)}) custom-call(s32[5]{0:T(128)S(1)} %stack.28.scalars, f32[1024,512]{1,0:T(8,128)S(1)} %copy-done.5, f32[512,512]{1,0:T(8,128)S(1)} %collective-permute-done.block, s32[2,1,512]{2,1,0:T(1,128)S(1)} %collective-permute-done.1.maps), custom_call_target="tpu_custom_call" | custom-call | flops 2000000000 | bytes 5000000 | tf_op jit(solution)/shard_map/pallas_call | solution.py:96
  45.1 1.1 shard_map.80
  46.2 5.2 %collective-permute-start.2 = (f32[8,8,512]{2,1,0:T(8,128)S(1)}, f32[8,8,512]{2,1,0:T(8,128)S(1)}, u32[]{:S(2)}, u32[]{:S(2)}) collective-permute-start(f32[8,8,512]{2,1,0:T(8,128)S(1)} %get-tuple-element.30), channel_id=1, source_target_pairs={{0,1},{1,0},{2,3},{3,2},{4,5},{5,4},{6,7},{7,6},{8,9},{9,8},{10,11... | collective-permute-start | bytes 393224 | tf_op jit(solution)/shard_map/ppermute | solution.py:375
  51.4 0.0 collective-permute-done.3
  51.4 0.0 collective-permute-done.4
  51.4 1.1 shard_map.81
  52.5 1.9 %collective-permute-start.5 = (f32[8,8,512]{2,1,0:T(8,128)S(1)}, f32[8,8,512]{2,1,0:T(8,128)S(1)}, u32[]{:S(2)}, u32[]{:S(2)}) collective-permute-start(f32[8,8,512]{2,1,0:T(8,128)S(1)} %get-tuple-element.32), channel_id=1, source_target_pairs={{0,1},{1,0},{2,3},{3,2},{4,5},{5,4},{6,7},{7,6},{8,9},{9,8},{10,11... | collective-permute-start | bytes 393224 | tf_op jit(solution)/shard_map/ppermute | solution.py:375
  54.5 0.0 collective-permute-done.2
  54.5 1.3 %collective-permute-done.5 = f32[8,8,512]{2,1,0:T(8,128)S(1)} collective-permute-done((f32[8,8,512]{2,1,0:T(8,128)S(1)}, f32[8,8,512]{2,1,0:T(8,128)S(1)}, u32[]{:S(2)}, u32[]{:S(2)}) %collective-permute-start.5) | collective-permute-done | bytes 131104 | tf_op jit(solution)/shard_map/ppermute | solution.py:375
  55.8 18.9 %all_to_all.15 = f32[8,16,512]{2,1,0:T(8,128)S(1)} all-to-all(f32[8,16,512]{2,1,0:T(8,128)S(1)} %pad_maximum_fusion), channel_id=1, replica_groups=mesh['child'=2,'z'=8,'xl'=2,'y'=8,'core'=2] {'y'}, dimensions={0} | all-to-all | bytes 524288 | tf_op jit(solution)/shard_map/all_to_all | solution.py:378
  74.8 0.1 broadcast_in_dim.6
  74.8 19.0 %all_to_all.16.mine = f32[16,16,512]{2,1,0:T(8,128)S(1)} all-to-all(f32[16,16,512]{2,1,0:T(8,128)S(1)} %broadcast_in_dim.6), channel_id=1, replica_groups=mesh['child'=2,'z'=8,'xl'=2,'y'=8,'core'=2] {'child','y'}, dimensions={0} | all-to-all | bytes 1048576 | tf_op jit(solution)/shard_map/all_to_all | solution.py:380
  93.8 4.7 %collective-permute-start.6 = (f32[16,16,512]{2,1,0:T(8,128)S(1)}, f32[16,16,512]{2,1,0:T(8,128)S(1)}, u32[]{:S(2)}, u32[]{:S(2)}) collective-permute-start(f32[16,16,512]{2,1,0:T(8,128)S(1)} %all_to_all.16.mine), channel_id=1, source_target_pairs={{0,1},{1,0},{2,3},{3,2},{4,5},{5,4},{6,7},{7,6},{8,9},{9,8},{10,11... | collective-permute-start | bytes 1572872 | tf_op jit(solution)/shard_map/ppermute | solution.py:383
  98.6 1.5 %collective-permute-done.6.theirs = f32[16,16,512]{2,1,0:T(8,128)S(1)} collective-permute-done((f32[16,16,512]{2,1,0:T(8,128)S(1)}, f32[16,16,512]{2,1,0:T(8,128)S(1)}, u32[]{:S(2)}, u32[]{:S(2)}) %collective-permute-start.6) | collective-permute-done | bytes 524320 | tf_op jit(solution)/shard_map/ppermute | solution.py:383
  100.1 6.2 %shard_map.82 = (f32[256,1024]{1,0:T(8,128)S(1)}, f32[2,128,256]{2,1,0:T(8,128)S(1)}, f32[2,128,128]{2,1,0:T(8,128)S(1)}, f32[2,128,256]{2,1,0:T(8,128)S(1)}) custom-call(s32[5]{0:T(128)S(1)} %stack.28.scalars, f32[16,16,512]{2,1,0:T(8,128)S(1)} %all_to_all.16.mine, f32[16,16,512]{2,1,0:T(8,128)S(1)} %collective-permute-done.6.theirs), custom_call_target="tpu_custom_call" | custom-call | tf_op jit(solution)/shard_map/pallas_call | solution.py:263
  106.3 2.4 %collective-permute-start.7 = (f32[2,128,256]{2,1,0:T(8,128)S(1)}, f32[2,128,256]{2,1,0:T(8,128)S(1)}, u32[]{:S(2)}, u32[]{:S(2)}) collective-permute-start(f32[2,128,256]{2,1,0:T(8,128)S(1)} %get-tuple-element.34.u_head), channel_id=1, source_target_pairs={{0,16},{16,0},{1,17},{17,1},{2,18},{18,2},{3,19},{19,3},{4,20},{20... | collective-permute-start | bytes 786440 | tf_op jit(solution)/shard_map/ppermute | solution.py:386
  108.7 5.0 %shard_map.83 = (f32[2,128,128]{2,1,0:T(8,128)S(1)}, f32[2,8,256]{2,1,0:T(8,128)S(1)}, f32[2,8,256]{2,1,0:T(8,128)S(1)}) custom-call(s32[5]{0:T(128)S(1)} %stack.28.scalars, f32[2,128,256]{2,1,0:T(8,128)S(1)} %get-tuple-element.34.u_head, f32[2,128,128]{2,1,0:T(8,128)S(1)} %get-tuple-element.35.x_head, f32[2,128,256]{2,1,0:T(8,128)S(1)} %get-tuple-element.36.rest), custom_call_target="tpu_custom_call" | custom-call | flops 8000000000 | bytes 1000000 | tf_op jit(solution)/shard_map/pallas_call | solution.py:304
  113.7 3.1 %collective-permute-start.8 = (f32[2,128,128]{2,1,0:T(8,128)S(1)}, f32[2,128,128]{2,1,0:T(8,128)S(1)}, u32[]{:S(2)}, u32[]{:S(2)}) collective-permute-start(f32[2,128,128]{2,1,0:T(8,128)S(1)} %get-tuple-element.39), channel_id=1, source_target_pairs={{0,16},{16,0},{1,17},{17,1},{2,18},{18,2},{3,19},{19,3},{4,20},{20... | collective-permute-start | bytes 393224 | tf_op jit(solution)/shard_map/ppermute | solution.py:388
  116.8 1.8 %shard_map.84 = f32[8,1024]{1,0:T(8,128)} custom-call(s32[5]{0:T(128)S(1)} %stack.28.scalars, f32[256,1024]{1,0:T(8,128)S(1)} %get-tuple-element.33.window, f32[2,8,256]{2,1,0:T(8,128)S(1)} %get-tuple-element.37.x_own), custom_call_target="tpu_custom_call" | custom-call | flops 1000000000 | bytes 1000000 | tf_op jit(solution)/shard_map/pallas_call | solution.py:389
  118.5 1.4 %collective-permute-done.8.sib_tail = f32[2,128,128]{2,1,0:T(8,128)S(1)} collective-permute-done((f32[2,128,128]{2,1,0:T(8,128)S(1)}, f32[2,128,128]{2,1,0:T(8,128)S(1)}, u32[]{:S(2)}, u32[]{:S(2)}) %collective-permute-start.8) | collective-permute-done | bytes 131104 | tf_op jit(solution)/shard_map/ppermute | solution.py:388
  119.9 0.0 collective-permute-done.7.sib_head
  119.9 1.1 shard_map.85
  (6 shorter events, 0.1 us)
Async XLA Ops:
  0.6 0.8 copy-start
  2.3 28.8 %all-to-all-start = ((f32[8,16,1024]{2,1,0:T(8,128)}), f32[8,16,1024]{2,1,0:T(8,128)S(1)}, u32[]{:S(2)}, u32[]{:S(2)}) async-start(f32[8,16,1024]{2,1,0:T(8,128)} %shard_map.77), calls=%async_computation | async-start | bytes 1048576 | tf_op jit(solution)/shard_map/all_to_all | solution.py:361
  13.2 27.4 %collective-permute-start = (f32[512,512]{1,0:T(8,128)}, f32[512,512]{1,0:T(8,128)S(1)}, u32[]{:S(2)}, u32[]{:S(2)}) collective-permute-start(f32[512,512]{1,0:T(8,128)} %bitcast.19), channel_id=1, source_target_pairs={{0,256},{256,0},{1,257},{257,1},{2,258},{258,2},{3,259},{259,3},{4... | collective-permute-start | bytes 3145736 | tf_op jit(solution)/shard_map/ppermute | solution.py:339
  18.5 22.1 %collective-permute-start.1 = (s32[2,1,512]{2,1,0:T(1,128)S(1)}, s32[2,1,512]{2,1,0:T(1,128)S(1)}, u32[]{:S(2)}, u32[]{:S(2)}) collective-permute-start(s32[2,1,512]{2,1,0:T(1,128)S(1)} %pad_add_fusion), channel_id=1, source_target_pairs={{0,256},{256,0},{1,257},{257,1},{2,258},{258,2},{3,259},{259,3},{4... | collective-permute-start | bytes 12296 | tf_op jit(solution)/shard_map/ppermute | solution.py:343
  21.4 1.6 %copy-start.1 = (f32[1,512,1024]{2,1,0:T(8,128)S(1)}, f32[1,512,1024]{2,1,0:T(8,128)}, u32[]{:S(2)}) copy-start(f32[1,512,1024]{2,1,0:T(8,128)} %param.7) | copy-start | bytes 6291460
  23.0 1.2 %copy-start.2 = (f32[1,512,512]{2,1,0:T(8,128)S(1)}, f32[1,512,512]{2,1,0:T(8,128)}, u32[]{:S(2)}) copy-start(f32[1,512,512]{2,1,0:T(8,128)} %param.6) | copy-start | bytes 3145732
  24.2 0.7 copy-start.3
  27.5 1.3 %copy-start.4 = (f32[1024,512]{1,0:T(8,128)}, f32[1024,512]{1,0:T(8,128)S(1)}, u32[]{:S(2)}) copy-start(f32[1024,512]{1,0:T(8,128)S(1)} %get-tuple-element.24.own_total) | copy-start | bytes 6291460
  31.2 20.3 %collective-permute-start.3 = (f32[4,16,1024]{2,1,0:T(8,128)S(1)}, f32[4,16,1024]{2,1,0:T(8,128)S(1)}, u32[]{:S(2)}, u32[]{:S(2)}) collective-permute-start(f32[4,16,1024]{2,1,0:T(8,128)S(1)} %get-tuple-element.41), channel_id=1, source_target_pairs={{0,16},{16,256},{256,272},{272,0},{1,17},{17,257},{257,273},{273,1... | collective-permute-start | bytes 786440 | tf_op jit(solution)/shard_map/ppermute | solution.py:366
  34.3 17.1 %collective-permute-start.4 = (f32[4,16,1024]{2,1,0:T(8,128)S(1)}, f32[4,16,1024]{2,1,0:T(8,128)S(1)}, u32[]{:S(2)}, u32[]{:S(2)}) collective-permute-start(f32[4,16,1024]{2,1,0:T(8,128)S(1)} %get-tuple-element.40), channel_id=1, source_target_pairs={{0,272},{16,0},{256,16},{272,256},{1,273},{17,1},{257,17},{273,257... | collective-permute-start | bytes 786440 | tf_op jit(solution)/shard_map/ppermute | solution.py:366
  40.6 1.6 %copy-start.5 = (f32[1024,512]{1,0:T(8,128)S(1)}, f32[1024,512]{1,0:T(8,128)}, u32[]{:S(2)}) copy-start(f32[1024,512]{1,0:T(8,128)} %copy-done.4) | copy-start | bytes 6291460
  46.2 8.3 %collective-permute-start.2 = (f32[8,8,512]{2,1,0:T(8,128)S(1)}, f32[8,8,512]{2,1,0:T(8,128)S(1)}, u32[]{:S(2)}, u32[]{:S(2)}) collective-permute-start(f32[8,8,512]{2,1,0:T(8,128)S(1)} %get-tuple-element.30), channel_id=1, source_target_pairs={{0,1},{1,0},{2,3},{3,2},{4,5},{5,4},{6,7},{7,6},{8,9},{9,8},{10,11... | collective-permute-start | bytes 393224 | tf_op jit(solution)/shard_map/ppermute | solution.py:375
  52.5 3.2 %collective-permute-start.5 = (f32[8,8,512]{2,1,0:T(8,128)S(1)}, f32[8,8,512]{2,1,0:T(8,128)S(1)}, u32[]{:S(2)}, u32[]{:S(2)}) collective-permute-start(f32[8,8,512]{2,1,0:T(8,128)S(1)} %get-tuple-element.32), channel_id=1, source_target_pairs={{0,1},{1,0},{2,3},{3,2},{4,5},{5,4},{6,7},{7,6},{8,9},{9,8},{10,11... | collective-permute-start | bytes 393224 | tf_op jit(solution)/shard_map/ppermute | solution.py:375
  93.8 6.3 %collective-permute-start.6 = (f32[16,16,512]{2,1,0:T(8,128)S(1)}, f32[16,16,512]{2,1,0:T(8,128)S(1)}, u32[]{:S(2)}, u32[]{:S(2)}) collective-permute-start(f32[16,16,512]{2,1,0:T(8,128)S(1)} %all_to_all.16.mine), channel_id=1, source_target_pairs={{0,1},{1,0},{2,3},{3,2},{4,5},{5,4},{6,7},{7,6},{8,9},{9,8},{10,11... | collective-permute-start | bytes 1572872 | tf_op jit(solution)/shard_map/ppermute | solution.py:383
  106.3 13.6 %collective-permute-start.7 = (f32[2,128,256]{2,1,0:T(8,128)S(1)}, f32[2,128,256]{2,1,0:T(8,128)S(1)}, u32[]{:S(2)}, u32[]{:S(2)}) collective-permute-start(f32[2,128,256]{2,1,0:T(8,128)S(1)} %get-tuple-element.34.u_head), channel_id=1, source_target_pairs={{0,16},{16,0},{1,17},{17,1},{2,18},{18,2},{3,19},{19,3},{4,20},{20... | collective-permute-start | bytes 786440 | tf_op jit(solution)/shard_map/ppermute | solution.py:386
  113.7 6.3 %collective-permute-start.8 = (f32[2,128,128]{2,1,0:T(8,128)S(1)}, f32[2,128,128]{2,1,0:T(8,128)S(1)}, u32[]{:S(2)}, u32[]{:S(2)}) collective-permute-start(f32[2,128,128]{2,1,0:T(8,128)S(1)} %get-tuple-element.39), channel_id=1, source_target_pairs={{0,16},{16,0},{1,17},{17,1},{2,18},{18,2},{3,19},{19,3},{4,20},{20... | collective-permute-start | bytes 393224 | tf_op jit(solution)/shard_map/ppermute | solution.py:388

commit v6 on v5

--- a/solution.py
+++ b/solution.py
@@ -51,7 +51,7 @@
     return dot(pick, spread_rows[0], NT) + dot(pick, spread_rows[1], NT)
 
 
-def own_kernel(scalars, pattern, block, assembled, columns, targets, total, built, spread_rows):
+def own_kernel(scalars, pattern, block, assembled, columns, targets, total, spread_rows):
     child = scalars[0]
     window_rows, half_rows = total.shape
     child_terms(child, block, targets, spread_rows, half_rows)
@@ -63,15 +63,11 @@
             keep = pattern[child * tiles + tile, step].astype(f32)
             lanes = slice(tile * BT, (tile + 1) * BT)
             total[rows, lanes] = terms[:, lanes] + assembled[lanes, rows].T * keep
-    built[...] = jnp.zeros_like(built)
-
-
-def sibling_kernel(scalars, own_total, block, maps, top, low, spread_rows, total, arrived):
+
+
+def sibling_kernel(scalars, total, block, maps, top, low, spread_rows):
     window_rows, half_rows = total.shape
-    fetch = pltpu.make_async_copy(own_total, total, arrived)
-    fetch.start()
     child_terms(scalars[0], block, maps.at[1], spread_rows, half_rows)
-    fetch.wait()
     for step in range(window_rows // BT):
         rows = slice(step * BT, (step + 1) * BT)
         terms = picked_terms(maps.at[0], spread_rows, step * BT, BT)
@@ -83,8 +79,8 @@
     return pl.pallas_call(
         own_kernel,
         in_specs=[SMEM, SMEM] + [VMEM] * 4,
-        out_specs=[VMEM, VMEM],
-        out_shape=[shape(window_rows, half_rows), shape(8, 128)],
+        out_specs=VMEM,
+        out_shape=shape(window_rows, half_rows),
         scratch_shapes=[pltpu.VMEM((2, half_rows, block.shape[1]), bf16)],
         compiler_params=PARAMS,
         cost_estimate=pl.CostEstimate(flops=2 * 10**9, bytes_accessed=5 * 10**6, transcendentals=0),
@@ -95,55 +91,56 @@
     window_rows, half_rows = total.shape
     return pl.pallas_call(
         sibling_kernel,
-        in_specs=[SMEM, pl.BlockSpec(memory_space=pltpu.HBM)] + [VMEM] * 2,
+        in_specs=[SMEM] + [VMEM] * 3,
         out_specs=[VMEM, VMEM],
         out_shape=[shape(window_rows, half_rows, dtype=bf16)] * 2,
         scratch_shapes=[
             pltpu.VMEM((2, half_rows, block.shape[1]), bf16),
-            pltpu.VMEM((window_rows, half_rows), f32),
-            pltpu.SemaphoreType.DMA,
         ],
         compiler_params=PARAMS,
         cost_estimate=pl.CostEstimate(flops=2 * 10**9, bytes_accessed=5 * 10**6, transcendentals=0),
     )(scalars, total, block, maps)
 
 
-def apply_kernel(scalars, built, *refs):
-    *pieces, top, low, give, keep = refs
+def apply_kernel(scalars, own, ahead, behind, top, low, give, keep):
     core = scalars[2]
-    count, width, _ = give.shape
+    count, width, half_rows = give.shape
     depth = top.shape[0]
     rows = count * width
     ordered = jnp.concatenate(
         [
             piece[:, pl.ds(side, 1)].reshape(-1, depth)
             for side in (1 - core, core)
-            for piece in pieces
+            for piece in (own, ahead, behind)
         ]
     )
     high_lines, low_lines = two_parts(ordered)
-    both = jnp.concatenate([high_lines, low_lines])
-    for tile in range(top.shape[1] // BT):
+    for tile in range(half_rows // BT):
         lanes = slice(tile * BT, (tile + 1) * BT)
-        wide = dot(both, top[:, lanes], NN)
-        out = wide[: 2 * rows] + wide[2 * rows :] + dot(high_lines, low[:, lanes], NN)
-        give[:, :, lanes] = out[:rows].reshape(count, width, BT)
-        keep[:, :, lanes] = out[rows:].reshape(count, width, BT)
-
-
-def apply_operator(scalars, built, pieces, top, low):
-    count = sum(piece.shape[0] for piece in pieces)
-    width = pieces[0].shape[1] // 2
-    depth, half_rows = top.shape
-    lines = [piece.reshape(piece.shape[0], 2, width, depth) for piece in pieces]
+        out = (
+            dot(high_lines, top[:, lanes], NN)
+            + dot(low_lines, top[:, lanes], NN)
+            + dot(high_lines, low[:, lanes], NN)
+        )
+        for target, start in ((give, 0), (keep, rows)):
+            for side in range(2):
+                part = out[start + side * rows // 2 : start + (side + 1) * rows // 2]
+                there = slice(side * width // 2, (side + 1) * width // 2)
+                target[:, there, lanes] = part.reshape(count, width // 2, BT)
+
+
+def apply_operator(scalars, own, ahead, behind, top, low):
+    count, width, depth = own.shape
+    half_rows = top.shape[1]
+    lines = [v.reshape(v.shape[0], 2, width // 2, depth) for v in (own, ahead, behind)]
     return pl.pallas_call(
         apply_kernel,
-        in_specs=[SMEM] + [VMEM] * (3 + len(lines)),
+        in_specs=[SMEM] + [VMEM] * 5,
         out_specs=[VMEM, VMEM],
         out_shape=[shape(count, width, half_rows)] * 2,
         compiler_params=PARAMS,
         cost_estimate=pl.CostEstimate(flops=10**9, bytes_accessed=6 * 10**6, transcendentals=0),
-    )(scalars, built, *lines, top, low)
+    )(scalars, *lines, top, low)
 
 
 def spread_out(row_or_column):
@@ -359,8 +356,7 @@
         compiler_params=PARAMS,
     )(omega.T)
     own = lax.all_to_all(copies, "z", 0, 0)
-    total, built = own_operator(scalars, pattern, contrib[0], assembled[0], columns, targets)
-    own, built = lax.optimization_barrier((own, built))
+    total = own_operator(scalars, pattern, contrib[0], assembled[0], columns, targets)
     ring = lax.axis_size("child") * lax.axis_size("xl")
     other = [
         lax.ppermute(piece, ("child", "xl"), [(i, (i + step) % ring) for i in range(ring)])
@@ -370,11 +366,8 @@
     sibling_block, sibling_maps = lax.optimization_barrier((sibling_block, sibling_maps))
     top, low = whole_operator(scalars, total, sibling_block, sibling_maps)
 
-    def half(pieces):
-        give, keep = apply_operator(scalars, built, pieces, top, low)
-        return keep + lax.ppermute(give, "core", SWAP)
-
-    parts = jnp.concatenate([half([own]), half(other)], axis=1)
+    give, keep = apply_operator(scalars, own, *other, top, low)
+    parts = keep + lax.ppermute(give, "core", SWAP)
     terms = lax.all_to_all(parts, "y", 0, 0)
     samples = jnp.sum(terms, axis=0)
     mine = lax.all_to_all(

time: 122 us -> 117 us (0.959)
  waiting for transfers between devices: 9.5 us -> 16.7 us
  local copies, waits for them, and re-layouts: 7.41 us -> 2.23 us
  starting transfers between devices: 41.5 us -> 36.7 us
  blocking collectives: 37.9 us -> 36.6 us
    all_to_all x1, waiting for transfers between devices: 2.33 us -> 9.71 us  [local(): own = lax.all_to_all(copies, 'z', 0, 0)]
    unnamed x12 -> x8, local copies, waits for them, and re-layouts: 7.24 us -> 2.06 us
    ppermute x2 -> x1, starting transfers between devices: 7.13 us -> 2.46 us  [local(): parts = keep + lax.ppermute(give, 'core', SWAP)]
    ppermute x1, waiting for transfers between devices: 2.93 us -> 0.01 us  [local(): sibling_maps = lax.ppermute(maps, 'child', SWAP)]
    ppermute x2, waiting for transfers between devices: 0.01 us -> 2.9 us  [local(): lax.ppermute(piece, ('child', 'xl'), [(i, (i + step) % ring) for i in ran...]
    pallas_call x3 -> x2, Pallas kernels: 5.09 us -> 4.74 us  [the longest x1 3.19 us: whole_operator(): pl.pallas_call(sibling_kernel, in_specs=[SMEM] + [VMEM] * 3, out_specs=[V...]
  transfers between devices with their start and end apart: 10 -> 9, of which waited for: 5 -> 5; matrix products, arithmetic and copies ran while one was open for 1% -> 1% of each run, Pallas kernels for 12% -> 11%
where the time goes in v6:
time: 117 us
  starting transfers between devices  36.7 us (31%)
  blocking collectives  36.6 us (31%)
  Pallas kernels  22.1 us (19%)
  waiting for transfers between devices  16.7 us (14%)
  local copies, waits for them, and re-layouts  2.23 us (2%)
  between operations  1.48 us (1%)
    all_to_all x1, blocking collectives, local(): lax.all_to_all(jnp.broadcast_to(samples, (groups,) + samples.shape), ('ch...  18.8 us
    all_to_all x1, blocking collectives, local(): terms = lax.all_to_all(parts, 'y', 0, 0)  17.7 us
    all_to_all x1, starting transfers between devices, local(): own = lax.all_to_all(copies, 'z', 0, 0)  10.9 us
    all_to_all x1, waiting for transfers between devices, local(): own = lax.all_to_all(copies, 'z', 0, 0)  9.71 us
    ppermute x2, starting transfers between devices, local(): lax.ppermute(piece, ('child', 'xl'), [(i, (i + step) % ring) for i in ran...  6.49 us
    pallas_call x1, Pallas kernels, factor_head(): pl.pallas_call(head_kernel, in_specs=[SMEM, VMEM, VMEM], out_specs=[VMEM]...  6.16 us
    pallas_call x1, Pallas kernels, factor_tail(): pl.pallas_call(tail_kernel, in_specs=[SMEM] + [VMEM] * 3, out_specs=[VMEM...  4.98 us
    ppermute x1, starting transfers between devices, local(): theirs = lax.ppermute(mine, 'core', SWAP)  4.86 us
  transfers between devices with their start and end apart: 9, of which 5 were waited for; matrix products, arithmetic and copies ran while one was open for 1% of the time, Pallas kernels for 11%

profile of v6, /device:TPU:1, one launch (start us, length us, event | category | flops | bytes accessed | tf_op | source)
XLA Modules:
  0.0 116.6 jit_solution(9363117824336121222)
XLA Ops:
  0.6 0.0 copy-start
  0.6 0.8 copy-done
  1.5 0.0 copy-start.1
  1.5 0.0 copy-start.3
  1.5 0.9 shard_map.77
  2.3 10.9 %all-to-all-start = ((f32[8,16,1024]{2,1,0:T(8,128)}), f32[8,16,1024]{2,1,0:T(8,128)S(1)}, u32[]{:S(2)}, u32[]{:S(2)}) async-start(f32[8,16,1024]{2,1,0:T(8,128)} %shard_map.77), calls=%async_computation | async-start | bytes 1048576 | tf_op jit(solution)/shard_map/all_to_all | solution.py:358
  13.2 4.6 %collective-permute-start.2 = (f32[512,512]{1,0:T(8,128)}, f32[512,512]{1,0:T(8,128)}, u32[]{:S(2)}, u32[]{:S(2)}) collective-permute-start(f32[512,512]{1,0:T(8,128)} %bitcast.19), channel_id=1, source_target_pairs={{0,256},{256,0},{1,257},{257,1},{2,258},{258,2},{3,259},{259,3},{4... | collective-permute-start | bytes 3145736 | tf_op jit(solution)/shard_map/ppermute | solution.py:336
  17.9 0.7 dynamic-slice_subtract_fusion
  18.6 2.1 %collective-permute-start.3 = (s32[2,1,512]{2,1,0:T(1,128)S(1)}, s32[2,1,512]{2,1,0:T(1,128)S(1)}, u32[]{:S(2)}, u32[]{:S(2)}) collective-permute-start(s32[2,1,512]{2,1,0:T(1,128)S(1)} %pad_add_fusion), channel_id=1, source_target_pairs={{0,256},{256,0},{1,257},{257,1},{2,258},{258,2},{3,259},{259,3},{4... | collective-permute-start | bytes 12296 | tf_op jit(solution)/shard_map/ppermute | solution.py:340
  21.4 0.1 stack.28.scalars
  21.4 9.7 %all-to-all-done = f32[8,16,1024]{2,1,0:T(8,128)S(1)} async-done(((f32[8,16,1024]{2,1,0:T(8,128)}), f32[8,16,1024]{2,1,0:T(8,128)S(1)}, u32[]{:S(2)}, u32[]{:S(2)}) %all-to-all-start) | async-done | bytes 524320 | tf_op jit(solution)/shard_map/all_to_all | solution.py:358
  31.2 3.1 %collective-permute-start = (f32[4,16,1024]{2,1,0:T(8,128)S(1)}, f32[4,16,1024]{2,1,0:T(8,128)S(1)}, u32[]{:S(2)}, u32[]{:S(2)}) collective-permute-start(f32[4,16,1024]{2,1,0:T(8,128)S(1)} %get-tuple-element.29), channel_id=1, source_target_pairs={{0,16},{16,256},{256,272},{272,0},{1,17},{17,257},{257,273},{273,1... | collective-permute-start | bytes 786440 | tf_op jit(solution)/shard_map/ppermute | solution.py:362
  34.3 3.4 %collective-permute-start.1 = (f32[4,16,1024]{2,1,0:T(8,128)S(1)}, f32[4,16,1024]{2,1,0:T(8,128)S(1)}, u32[]{:S(2)}, u32[]{:S(2)}) collective-permute-start(f32[4,16,1024]{2,1,0:T(8,128)S(1)} %get-tuple-element.28), channel_id=1, source_target_pairs={{0,272},{16,0},{256,16},{272,256},{1,273},{17,1},{257,17},{273,257... | collective-permute-start | bytes 786440 | tf_op jit(solution)/shard_map/ppermute | solution.py:362
  37.7 0.0 copy-done.1
  37.7 0.0 copy-done.3
  37.7 0.0 copy-start.2
  37.7 1.2 %copy-done.2 = f32[1,512,512]{2,1,0:T(8,128)S(1)} copy-done((f32[1,512,512]{2,1,0:T(8,128)S(1)}, f32[1,512,512]{2,1,0:T(8,128)}, u32[]{:S(2)}) %copy-start.2) | copy-done | bytes 1048600
  39.0 2.5 %shard_map.78.total = f32[1024,512]{1,0:T(8,128)S(1)} custom-call(s32[5]{0:T(128)S(1)} %stack.28.scalars, s32[4,4]{1,0:T(4,128)S(1)} %copy-done.3, f32[512,512]{1,0:T(8,128)S(1)} %bitcast.20, f32[512,1024]{1,0:T(8,128)S(1)} %bitcast.18, s32[1,512]{1,0:T(1,128)S(1)} %get-tuple-element.31.columns, s32[1,512]{1,0:T(1,128)S(1)} %get-tuple-element.30.targets), custom_call_target="tpu_custom_call" | custom-call | flops 2000000000 | bytes 5000000 | tf_op jit(solution)/shard_map/pallas_call | solution.py:79
  41.5 0.0 collective-permute-done.3.maps
  41.5 0.0 collective-permute-done.2.block
  41.5 3.2 %shard_map.79 = (bf16[1024,512]{1,0:T(8,128)(2,1)S(1)}, bf16[1024,512]{1,0:T(8,128)(2,1)S(1)}) custom-call(s32[5]{0:T(128)S(1)} %stack.28.scalars, f32[1024,512]{1,0:T(8,128)S(1)} %shard_map.78.total, f32[512,512]{1,0:T(8,128)} %collective-permute-done.2.block, s32[2,1,512]{2,1,0:T(1,128)S(1)} %collective-permute-done.3.maps), custom_call_target="tpu_custom_call" | custom-call | flops 2000000000 | bytes 5000000 | tf_op jit(solution)/shard_map/pallas_call | solution.py:92
  44.7 2.9 %collective-permute-done = f32[4,16,1024]{2,1,0:T(8,128)S(1)} collective-permute-done((f32[4,16,1024]{2,1,0:T(8,128)S(1)}, f32[4,16,1024]{2,1,0:T(8,128)S(1)}, u32[]{:S(2)}, u32[]{:S(2)}) %collective-permute-start) | collective-permute-done | bytes 262176 | tf_op jit(solution)/shard_map/ppermute | solution.py:362
  47.6 0.0 collective-permute-done.1
  47.6 1.5 %shard_map.80 = (f32[8,16,512]{2,1,0:T(8,128)S(1)}, f32[8,16,512]{2,1,0:T(8,128)S(1)}) custom-call(s32[5]{0:T(128)S(1)} %stack.28.scalars, f32[8,2,8,1024]{3,2,1,0:T(8,128)S(1)} %bitcast.14, f32[4,2,8,1024]{3,2,1,0:T(8,128)S(1)} %bitcast.21, f32[4,2,8,1024]{3,2,1,0:T(8,128)S(1)} %bitcast.22, bf16[1024,512]{1,0:T(8,128)(2,1)S(1)} %get-tuple-element.17.top, ...), custom_call_target="tpu_custom_call" | custom-call | flops 1000000000 | bytes 6000000 | tf_op jit(solution)/shard_map/pallas_call | solution.py:136
  49.1 2.5 %collective-permute-start.4 = (f32[8,16,512]{2,1,0:T(8,128)S(1)}, f32[8,16,512]{2,1,0:T(8,128)S(1)}, u32[]{:S(2)}, u32[]{:S(2)}) collective-permute-start(f32[8,16,512]{2,1,0:T(8,128)S(1)} %get-tuple-element.20), channel_id=1, source_target_pairs={{0,1},{1,0},{2,3},{3,2},{4,5},{5,4},{6,7},{7,6},{8,9},{9,8},{10,11... | collective-permute-start | bytes 786440 | tf_op jit(solution)/shard_map/ppermute | solution.py:370
  51.6 1.1 collective-permute-done.4
  52.8 17.7 %all_to_all.15 = f32[8,16,512]{2,1,0:T(8,128)S(1)} all-to-all(f32[8,16,512]{2,1,0:T(8,128)S(1)} %add.24), channel_id=1, replica_groups=mesh['child'=2,'z'=8,'xl'=2,'y'=8,'core'=2] {'y'}, dimensions={0} | all-to-all | bytes 524288 | tf_op jit(solution)/shard_map/all_to_all | solution.py:371
  70.5 0.1 broadcast_in_dim.6
  70.6 18.8 %all_to_all.16.mine = f32[16,16,512]{2,1,0:T(8,128)S(1)} all-to-all(f32[16,16,512]{2,1,0:T(8,128)S(1)} %broadcast_in_dim.6), channel_id=1, replica_groups=mesh['child'=2,'z'=8,'xl'=2,'y'=8,'core'=2] {'child','y'}, dimensions={0} | all-to-all | bytes 1048576 | tf_op jit(solution)/shard_map/all_to_all | solution.py:373
  89.4 4.9 %collective-permute-start.5 = (f32[16,16,512]{2,1,0:T(8,128)S(1)}, f32[16,16,512]{2,1,0:T(8,128)S(1)}, u32[]{:S(2)}, u32[]{:S(2)}) collective-permute-start(f32[16,16,512]{2,1,0:T(8,128)S(1)} %all_to_all.16.mine), channel_id=1, source_target_pairs={{0,1},{1,0},{2,3},{3,2},{4,5},{5,4},{6,7},{7,6},{8,9},{9,8},{10,11... | collective-permute-start | bytes 1572872 | tf_op jit(solution)/shard_map/ppermute | solution.py:376
  94.3 1.5 %collective-permute-done.5.theirs = f32[16,16,512]{2,1,0:T(8,128)S(1)} collective-permute-done((f32[16,16,512]{2,1,0:T(8,128)S(1)}, f32[16,16,512]{2,1,0:T(8,128)S(1)}, u32[]{:S(2)}, u32[]{:S(2)}) %collective-permute-start.5) | collective-permute-done | bytes 524320 | tf_op jit(solution)/shard_map/ppermute | solution.py:376
  95.8 6.2 %shard_map.81 = (f32[256,1024]{1,0:T(8,128)S(1)}, f32[2,128,256]{2,1,0:T(8,128)S(1)}, f32[2,128,128]{2,1,0:T(8,128)S(1)}, f32[2,128,256]{2,1,0:T(8,128)S(1)}) custom-call(s32[5]{0:T(128)S(1)} %stack.28.scalars, f32[16,16,512]{2,1,0:T(8,128)S(1)} %all_to_all.16.mine, f32[16,16,512]{2,1,0:T(8,128)S(1)} %collective-permute-done.5.theirs), custom_call_target="tpu_custom_call" | custom-call | tf_op jit(solution)/shard_map/pallas_call | solution.py:260
  102.0 2.2 %collective-permute-start.6 = (f32[2,128,256]{2,1,0:T(8,128)S(1)}, f32[2,128,256]{2,1,0:T(8,128)S(1)}, u32[]{:S(2)}, u32[]{:S(2)}) collective-permute-start(f32[2,128,256]{2,1,0:T(8,128)S(1)} %get-tuple-element.22.u_head), channel_id=1, source_target_pairs={{0,16},{16,0},{1,17},{17,1},{2,18},{18,2},{3,19},{19,3},{4,20},{20... | collective-permute-start | bytes 786440 | tf_op jit(solution)/shard_map/ppermute | solution.py:379
  104.2 5.0 %shard_map.82 = (f32[2,128,128]{2,1,0:T(8,128)S(1)}, f32[2,8,256]{2,1,0:T(8,128)S(1)}, f32[2,8,256]{2,1,0:T(8,128)S(1)}) custom-call(s32[5]{0:T(128)S(1)} %stack.28.scalars, f32[2,128,256]{2,1,0:T(8,128)S(1)} %get-tuple-element.22.u_head, f32[2,128,128]{2,1,0:T(8,128)S(1)} %get-tuple-element.23.x_head, f32[2,128,256]{2,1,0:T(8,128)S(1)} %get-tuple-element.24.rest), custom_call_target="tpu_custom_call" | custom-call | flops 8000000000 | bytes 1000000 | tf_op jit(solution)/shard_map/pallas_call | solution.py:301
  109.2 3.1 %collective-permute-start.7 = (f32[2,128,128]{2,1,0:T(8,128)S(1)}, f32[2,128,128]{2,1,0:T(8,128)S(1)}, u32[]{:S(2)}, u32[]{:S(2)}) collective-permute-start(f32[2,128,128]{2,1,0:T(8,128)S(1)} %get-tuple-element.27), channel_id=1, source_target_pairs={{0,16},{16,0},{1,17},{17,1},{2,18},{18,2},{3,19},{19,3},{4,20},{20... | collective-permute-start | bytes 393224 | tf_op jit(solution)/shard_map/ppermute | solution.py:381
  112.3 1.7 %shard_map.83 = f32[8,1024]{1,0:T(8,128)} custom-call(s32[5]{0:T(128)S(1)} %stack.28.scalars, f32[256,1024]{1,0:T(8,128)S(1)} %get-tuple-element.21.window, f32[2,8,256]{2,1,0:T(8,128)S(1)} %get-tuple-element.25.x_own), custom_call_target="tpu_custom_call" | custom-call | flops 1000000000 | bytes 1000000 | tf_op jit(solution)/shard_map/pallas_call | solution.py:382
  114.0 1.4 %collective-permute-done.7.sib_tail = f32[2,128,128]{2,1,0:T(8,128)S(1)} collective-permute-done((f32[2,128,128]{2,1,0:T(8,128)S(1)}, f32[2,128,128]{2,1,0:T(8,128)S(1)}, u32[]{:S(2)}, u32[]{:S(2)}) %collective-permute-start.7) | collective-permute-done | bytes 131104 | tf_op jit(solution)/shard_map/ppermute | solution.py:381
  115.5 0.0 collective-permute-done.6.sib_head
  115.5 1.1 shard_map.84
  (4 shorter events, 0.1 us)
Async XLA Ops:
  0.6 0.8 copy-start
  1.5 36.2 %copy-start.1 = (f32[1,512,1024]{2,1,0:T(8,128)S(1)}, f32[1,512,1024]{2,1,0:T(8,128)}, u32[]{:S(2)}) copy-start(f32[1,512,1024]{2,1,0:T(8,128)} %param.7) | copy-start | bytes 6291460
  1.5 36.2 %copy-start.3 = (s32[4,4]{1,0:T(4,128)S(1)}, s32[4,4]{1,0:T(4,128)}, u32[]{:S(2)}) copy-start(s32[4,4]{1,0:T(4,128)} %pattern.1) | copy-start | bytes 196
  2.3 28.8 %all-to-all-start = ((f32[8,16,1024]{2,1,0:T(8,128)}), f32[8,16,1024]{2,1,0:T(8,128)S(1)}, u32[]{:S(2)}, u32[]{:S(2)}) async-start(f32[8,16,1024]{2,1,0:T(8,128)} %shard_map.77), calls=%async_computation | async-start | bytes 1048576 | tf_op jit(solution)/shard_map/all_to_all | solution.py:358
  13.2 28.3 %collective-permute-start.2 = (f32[512,512]{1,0:T(8,128)}, f32[512,512]{1,0:T(8,128)}, u32[]{:S(2)}, u32[]{:S(2)}) collective-permute-start(f32[512,512]{1,0:T(8,128)} %bitcast.19), channel_id=1, source_target_pairs={{0,256},{256,0},{1,257},{257,1},{2,258},{258,2},{3,259},{259,3},{4... | collective-permute-start | bytes 3145736 | tf_op jit(solution)/shard_map/ppermute | solution.py:336
  18.6 22.9 %collective-permute-start.3 = (s32[2,1,512]{2,1,0:T(1,128)S(1)}, s32[2,1,512]{2,1,0:T(1,128)S(1)}, u32[]{:S(2)}, u32[]{:S(2)}) collective-permute-start(s32[2,1,512]{2,1,0:T(1,128)S(1)} %pad_add_fusion), channel_id=1, source_target_pairs={{0,256},{256,0},{1,257},{257,1},{2,258},{258,2},{3,259},{259,3},{4... | collective-permute-start | bytes 12296 | tf_op jit(solution)/shard_map/ppermute | solution.py:340
  31.2 16.4 %collective-permute-start = (f32[4,16,1024]{2,1,0:T(8,128)S(1)}, f32[4,16,1024]{2,1,0:T(8,128)S(1)}, u32[]{:S(2)}, u32[]{:S(2)}) collective-permute-start(f32[4,16,1024]{2,1,0:T(8,128)S(1)} %get-tuple-element.29), channel_id=1, source_target_pairs={{0,16},{16,256},{256,272},{272,0},{1,17},{17,257},{257,273},{273,1... | collective-permute-start | bytes 786440 | tf_op jit(solution)/shard_map/ppermute | solution.py:362
  34.3 13.3 %collective-permute-start.1 = (f32[4,16,1024]{2,1,0:T(8,128)S(1)}, f32[4,16,1024]{2,1,0:T(8,128)S(1)}, u32[]{:S(2)}, u32[]{:S(2)}) collective-permute-start(f32[4,16,1024]{2,1,0:T(8,128)S(1)} %get-tuple-element.28), channel_id=1, source_target_pairs={{0,272},{16,0},{256,16},{272,256},{1,273},{17,1},{257,17},{273,257... | collective-permute-start | bytes 786440 | tf_op jit(solution)/shard_map/ppermute | solution.py:362
  37.7 1.2 %copy-start.2 = (f32[1,512,512]{2,1,0:T(8,128)S(1)}, f32[1,512,512]{2,1,0:T(8,128)}, u32[]{:S(2)}) copy-start(f32[1,512,512]{2,1,0:T(8,128)} %param.6) | copy-start | bytes 3145732
  49.1 3.6 %collective-permute-start.4 = (f32[8,16,512]{2,1,0:T(8,128)S(1)}, f32[8,16,512]{2,1,0:T(8,128)S(1)}, u32[]{:S(2)}, u32[]{:S(2)}) collective-permute-start(f32[8,16,512]{2,1,0:T(8,128)S(1)} %get-tuple-element.20), channel_id=1, source_target_pairs={{0,1},{1,0},{2,3},{3,2},{4,5},{5,4},{6,7},{7,6},{8,9},{9,8},{10,11... | collective-permute-start | bytes 786440 | tf_op jit(solution)/shard_map/ppermute | solution.py:370
  89.4 6.4 %collective-permute-start.5 = (f32[16,16,512]{2,1,0:T(8,128)S(1)}, f32[16,16,512]{2,1,0:T(8,128)S(1)}, u32[]{:S(2)}, u32[]{:S(2)}) collective-permute-start(f32[16,16,512]{2,1,0:T(8,128)S(1)} %all_to_all.16.mine), channel_id=1, source_target_pairs={{0,1},{1,0},{2,3},{3,2},{4,5},{5,4},{6,7},{7,6},{8,9},{9,8},{10,11... | collective-permute-start | bytes 1572872 | tf_op jit(solution)/shard_map/ppermute | solution.py:376
  102.0 13.5 %collective-permute-start.6 = (f32[2,128,256]{2,1,0:T(8,128)S(1)}, f32[2,128,256]{2,1,0:T(8,128)S(1)}, u32[]{:S(2)}, u32[]{:S(2)}) collective-permute-start(f32[2,128,256]{2,1,0:T(8,128)S(1)} %get-tuple-element.22.u_head), channel_id=1, source_target_pairs={{0,16},{16,0},{1,17},{17,1},{2,18},{18,2},{3,19},{19,3},{4,20},{20... | collective-permute-start | bytes 786440 | tf_op jit(solution)/shard_map/ppermute | solution.py:379
  109.2 6.3 %collective-permute-start.7 = (f32[2,128,128]{2,1,0:T(8,128)S(1)}, f32[2,128,128]{2,1,0:T(8,128)S(1)}, u32[]{:S(2)}, u32[]{:S(2)}) collective-permute-start(f32[2,128,128]{2,1,0:T(8,128)S(1)} %get-tuple-element.27), channel_id=1, source_target_pairs={{0,16},{16,0},{1,17},{17,1},{2,18},{18,2},{3,19},{19,3},{4,20},{20... | collective-permute-start | bytes 393224 | tf_op jit(solution)/shard_map/ppermute | solution.py:381

commit v7 on v6

--- a/solution.py
+++ b/solution.py
@@ -102,15 +102,14 @@
     )(scalars, total, block, maps)
 
 
-def apply_kernel(scalars, own, ahead, behind, top, low, give, keep):
-    core = scalars[2]
-    count, width, half_rows = give.shape
+def apply_kernel(own, ahead, behind, top, low, parts):
+    count, sides, width, half_rows = parts.shape
     depth = top.shape[0]
     rows = count * width
     ordered = jnp.concatenate(
         [
-            piece[:, pl.ds(side, 1)].reshape(-1, depth)
-            for side in (1 - core, core)
+            piece[:, side].reshape(-1, depth)
+            for side in range(sides)
             for piece in (own, ahead, behind)
         ]
     )
@@ -122,25 +121,27 @@
             + dot(low_lines, top[:, lanes], NN)
             + dot(high_lines, low[:, lanes], NN)
         )
-        for target, start in ((give, 0), (keep, rows)):
-            for side in range(2):
-                part = out[start + side * rows // 2 : start + (side + 1) * rows // 2]
-                there = slice(side * width // 2, (side + 1) * width // 2)
-                target[:, there, lanes] = part.reshape(count, width // 2, BT)
-
-
-def apply_operator(scalars, own, ahead, behind, top, low):
+        for side in range(sides):
+            for piece in range(2):
+                start = side * rows + piece * rows // 2
+                there = slice(piece * width // 2, (piece + 1) * width // 2)
+                parts[:, side, there, lanes] = out[start : start + rows // 2].reshape(
+                    count, width // 2, BT
+                )
+
+
+def apply_operator(own, ahead, behind, top, low):
     count, width, depth = own.shape
     half_rows = top.shape[1]
     lines = [v.reshape(v.shape[0], 2, width // 2, depth) for v in (own, ahead, behind)]
     return pl.pallas_call(
         apply_kernel,
-        in_specs=[SMEM] + [VMEM] * 5,
-        out_specs=[VMEM, VMEM],
-        out_shape=[shape(count, width, half_rows)] * 2,
+        in_specs=[VMEM] * 5,
+        out_specs=VMEM,
+        out_shape=shape(count, 2, width, half_rows),
         compiler_params=PARAMS,
         cost_estimate=pl.CostEstimate(flops=10**9, bytes_accessed=6 * 10**6, transcendentals=0),
-    )(scalars, *lines, top, low)
+    )(*lines, top, low)
 
 
 def spread_out(row_or_column):
@@ -272,7 +273,7 @@
     )(scalars, mine, theirs)
 
 
-def tail_kernel(scalars, u_head, x_head, rest, u_tail, u_own, x_own, x_tail, s0, s1):
+def tail_kernel(scalars, u_head, x_head, rest, packed, u_own, x_own, u_tail, x_tail, s0, s1):
     group = scalars[4]
     blocks = (s0, s1)
     for leaf in range(2):
@@ -284,6 +285,11 @@
         x_tail[leaf, r : r + 8, :] = u[:, HALF:]
 
     factor_block(blocks, store)
+    row = lax.broadcasted_iota(jnp.int32, (HALF, HALF), 0)
+    column = lax.broadcasted_iota(jnp.int32, (HALF, HALF), 1)
+    packed[:HALF, :] = jnp.where(row <= column, u_tail[0], u_tail[1].T)
+    diagonal = jnp.sum(jnp.where(row == column, u_tail[1], 0.0), axis=0, keepdims=True)
+    packed[HALF:, :] = jnp.broadcast_to(diagonal, (8, HALF))
     start = pl.multiple_of(group % (HALF // 8) * 8, 8)
     in_head = group < HALF // 8
     for leaf in range(2):
@@ -302,8 +308,9 @@
         tail_kernel,
         in_specs=[SMEM] + [VMEM] * 3,
         out_specs=[VMEM] * 3,
-        out_shape=[shape(2, HALF, HALF), shape(2, 8, R), shape(2, 8, R)],
-        scratch_shapes=[pltpu.VMEM((2, HALF, R), f32)] + [pltpu.VMEM((HALF, R + HALF), f32)] * 2,
+        out_shape=[shape(HALF + 8, HALF), shape(2, 8, R), shape(2, 8, R)],
+        scratch_shapes=[pltpu.VMEM((2, HALF, HALF), f32), pltpu.VMEM((2, HALF, R), f32)]
+        + [pltpu.VMEM((HALF, R + HALF), f32)] * 2,
         compiler_params=PARAMS,
         cost_estimate=pl.CostEstimate(flops=8 * 10**9, bytes_accessed=10**6, transcendentals=0),
     )(scalars, u_head, x_head, rest)
@@ -316,7 +323,15 @@
     out[...] = jnp.where(lane < scalars[3], solved[:8], solved[8:])
 
 
-def coupling_kernel(u_own, sib_head, sib_tail, out):
+def coupling_kernel(u_own, sib_head, packed, out):
+    row = lax.broadcasted_iota(jnp.int32, (HALF, HALF), 0)
+    column = lax.broadcasted_iota(jnp.int32, (HALF, HALF), 1)
+    square = packed[:HALF, :]
+    second = jnp.where(row > column, square, 0.0).T
+    sib_tail = [
+        jnp.where(row <= column, square, 0.0),
+        jnp.where(row == column, packed[HALF : HALF + 1, :], second),
+    ]
     for leaf in range(2):
         own = u_own[leaf]
         out[leaf, :, :HALF] = dot(own, sib_head[leaf], NT, highest)
@@ -366,9 +381,8 @@
     sibling_block, sibling_maps = lax.optimization_barrier((sibling_block, sibling_maps))
     top, low = whole_operator(scalars, total, sibling_block, sibling_maps)
 
-    give, keep = apply_operator(scalars, own, *other, top, low)
-    parts = keep + lax.ppermute(give, "core", SWAP)
-    terms = lax.all_to_all(parts, "y", 0, 0)
+    parts = apply_operator(own, *other, top, low)
+    terms = lax.all_to_all(parts.reshape((-1,) + parts.shape[2:]), ("y", "core"), 0, 0)
     samples = jnp.sum(terms, axis=0)
     mine = lax.all_to_all(
         jnp.broadcast_to(samples, (groups,) + samples.shape), ("child", "y"), 0, 0

time: 117 us -> 120 us (1.026)
  blocking collectives: 36.6 us -> 44 us
  waiting for transfers between devices: 16.7 us -> 14.4 us
  starting transfers between devices: 36.7 us -> 34.5 us
    all_to_all x1, blocking collectives: 17.7 us -> 24.8 us  [local(): lax.all_to_all(parts.reshape((-1,) + parts.shape[2:]), ('y', 'core'), 0, 0)]
    ppermute x1 -> x0, starting transfers between devices: 2.46 us -> none  [local(): parts = keep + lax.ppermute(give, 'core', SWAP)]
    ppermute x1, waiting for transfers between devices: 1.45 us -> 0.23 us  [local(): sib_tail = lax.ppermute(u_tail, 'xl', SWAP)]
  transfers between devices with their start and end apart: 9 -> 8, of which waited for: 5 -> 4; matrix products, arithmetic and copies ran while one was open for 1% -> 1% of each run, Pallas kernels for 11% -> 10%
where the time goes in v7:
time: 120 us; the launch traced here: 119 us
  blocking collectives  44 us (37%)
  starting transfers between devices  34.5 us (29%)
  Pallas kernels  21.6 us (18%)
  waiting for transfers between devices  14.4 us (12%)
  local copies, waits for them, and re-layouts  2.24 us (2%)
  between operations  1.46 us (1%)
    all_to_all x1, blocking collectives, local(): lax.all_to_all(parts.reshape((-1,) + parts.shape[2:]), ('y', 'core'), 0, 0)  24.8 us
    all_to_all x1, blocking collectives, local(): lax.all_to_all(jnp.broadcast_to(samples, (groups,) + samples.shape), ('ch...  19.2 us
    all_to_all x1, starting transfers between devices, local(): own = lax.all_to_all(copies, 'z', 0, 0)  10.9 us
    all_to_all x1, waiting for transfers between devices, local(): own = lax.all_to_all(copies, 'z', 0, 0)  9.71 us
    ppermute x2, starting transfers between devices, local(): lax.ppermute(piece, ('child', 'xl'), [(i, (i + step) % ring) for i in ran...  6.49 us
    pallas_call x1, Pallas kernels, factor_head(): pl.pallas_call(head_kernel, in_specs=[SMEM, VMEM, VMEM], out_specs=[VMEM]...  6.16 us
    ppermute x1, starting transfers between devices, local(): theirs = lax.ppermute(mine, 'core', SWAP)  5.05 us
    pallas_call x1, Pallas kernels, factor_tail(): pl.pallas_call(tail_kernel, in_specs=[SMEM] + [VMEM] * 3, out_specs=[VMEM...  5.04 us
  transfers between devices with their start and end apart: 8, of which 4 were waited for; matrix products, arithmetic and copies ran while one was open for 1% of the time, Pallas kernels for 10%

profile of v7, /device:TPU:1, one launch (start us, length us, event | category | flops | bytes accessed | tf_op | source)
XLA Modules:
  0.0 118.9 jit_solution(10251652141908791631)
XLA Ops:
  0.6 0.0 copy-start
  0.6 0.8 copy-done
  1.5 0.0 copy-start.1
  1.5 0.0 copy-start.3
  1.5 0.9 shard_map.77
  2.3 10.9 %all-to-all-start = ((f32[8,16,1024]{2,1,0:T(8,128)}), f32[8,16,1024]{2,1,0:T(8,128)S(1)}, u32[]{:S(2)}, u32[]{:S(2)}) async-start(f32[8,16,1024]{2,1,0:T(8,128)} %shard_map.77), calls=%async_computation | async-start | bytes 1048576 | tf_op jit(solution)/shard_map/all_to_all | solution.py:373
  13.2 4.6 %collective-permute-start.2 = (f32[512,512]{1,0:T(8,128)}, f32[512,512]{1,0:T(8,128)}, u32[]{:S(2)}, u32[]{:S(2)}) collective-permute-start(f32[512,512]{1,0:T(8,128)} %bitcast.21), channel_id=1, source_target_pairs={{0,256},{256,0},{1,257},{257,1},{2,258},{258,2},{3,259},{259,3},{4... | collective-permute-start | bytes 3145736 | tf_op jit(solution)/shard_map/ppermute | solution.py:351
  17.9 0.7 dynamic-slice_subtract_fusion
  18.6 2.1 %collective-permute-start.3 = (s32[2,1,512]{2,1,0:T(1,128)S(1)}, s32[2,1,512]{2,1,0:T(1,128)S(1)}, u32[]{:S(2)}, u32[]{:S(2)}) collective-permute-start(s32[2,1,512]{2,1,0:T(1,128)S(1)} %pad_add_fusion), channel_id=1, source_target_pairs={{0,256},{256,0},{1,257},{257,1},{2,258},{258,2},{3,259},{259,3},{4... | collective-permute-start | bytes 12296 | tf_op jit(solution)/shard_map/ppermute | solution.py:355
  21.4 0.1 stack.28.scalars
  21.5 9.7 %all-to-all-done = f32[8,16,1024]{2,1,0:T(8,128)S(1)} async-done(((f32[8,16,1024]{2,1,0:T(8,128)}), f32[8,16,1024]{2,1,0:T(8,128)S(1)}, u32[]{:S(2)}, u32[]{:S(2)}) %all-to-all-start) | async-done | bytes 524320 | tf_op jit(solution)/shard_map/all_to_all | solution.py:373
  31.2 3.1 %collective-permute-start = (f32[4,16,1024]{2,1,0:T(8,128)S(1)}, f32[4,16,1024]{2,1,0:T(8,128)S(1)}, u32[]{:S(2)}, u32[]{:S(2)}) collective-permute-start(f32[4,16,1024]{2,1,0:T(8,128)S(1)} %get-tuple-element.25), channel_id=1, source_target_pairs={{0,16},{16,256},{256,272},{272,0},{1,17},{17,257},{257,273},{273,1... | collective-permute-start | bytes 786440 | tf_op jit(solution)/shard_map/ppermute | solution.py:377
  34.3 3.4 %collective-permute-start.1 = (f32[4,16,1024]{2,1,0:T(8,128)S(1)}, f32[4,16,1024]{2,1,0:T(8,128)S(1)}, u32[]{:S(2)}, u32[]{:S(2)}) collective-permute-start(f32[4,16,1024]{2,1,0:T(8,128)S(1)} %get-tuple-element.24), channel_id=1, source_target_pairs={{0,272},{16,0},{256,16},{272,256},{1,273},{17,1},{257,17},{273,257... | collective-permute-start | bytes 786440 | tf_op jit(solution)/shard_map/ppermute | solution.py:377
  37.7 0.0 copy-done.1
  37.7 0.0 copy-done.3
  37.7 0.0 copy-start.2
  37.8 1.2 %copy-done.2 = f32[1,512,512]{2,1,0:T(8,128)S(1)} copy-done((f32[1,512,512]{2,1,0:T(8,128)S(1)}, f32[1,512,512]{2,1,0:T(8,128)}, u32[]{:S(2)}) %copy-start.2) | copy-done | bytes 1048600
  39.0 2.5 %shard_map.78.total = f32[1024,512]{1,0:T(8,128)S(1)} custom-call(s32[5]{0:T(128)S(1)} %stack.28.scalars, s32[4,4]{1,0:T(4,128)S(1)} %copy-done.3, f32[512,512]{1,0:T(8,128)S(1)} %bitcast.22, f32[512,1024]{1,0:T(8,128)S(1)} %bitcast.20, s32[1,512]{1,0:T(1,128)S(1)} %get-tuple-element.27.columns, s32[1,512]{1,0:T(1,128)S(1)} %get-tuple-element.26.targets), custom_call_target="tpu_custom_call" | custom-call | flops 2000000000 | bytes 5000000 | tf_op jit(solution)/shard_map/pallas_call | solution.py:79
  41.5 0.0 collective-permute-done.3.maps
  41.5 0.0 collective-permute-done.2.block
  41.5 3.2 %shard_map.79 = (bf16[1024,512]{1,0:T(8,128)(2,1)S(1)}, bf16[1024,512]{1,0:T(8,128)(2,1)S(1)}) custom-call(s32[5]{0:T(128)S(1)} %stack.28.scalars, f32[1024,512]{1,0:T(8,128)S(1)} %shard_map.78.total, f32[512,512]{1,0:T(8,128)} %collective-permute-done.2.block, s32[2,1,512]{2,1,0:T(1,128)S(1)} %collective-permute-done.3.maps), custom_call_target="tpu_custom_call" | custom-call | flops 2000000000 | bytes 5000000 | tf_op jit(solution)/shard_map/pallas_call | solution.py:92
  44.7 2.9 %collective-permute-done = f32[4,16,1024]{2,1,0:T(8,128)S(1)} collective-permute-done((f32[4,16,1024]{2,1,0:T(8,128)S(1)}, f32[4,16,1024]{2,1,0:T(8,128)S(1)}, u32[]{:S(2)}, u32[]{:S(2)}) %collective-permute-start) | collective-permute-done | bytes 262176 | tf_op jit(solution)/shard_map/ppermute | solution.py:377
  47.6 0.0 collective-permute-done.1
  47.6 1.0 shard_map.80
  48.6 24.8 %all_to_all.15 = f32[16,16,512]{2,1,0:T(8,128)S(1)} all-to-all(f32[16,16,512]{2,1,0:T(8,128)S(1)} %bitcast.16), channel_id=1, replica_groups=mesh['child'=2,'z'=8,'xl'=2,'y'=8,'core'=2] {'y','core'}, dimensions={0} | all-to-all | bytes 1048576 | tf_op jit(solution)/shard_map/all_to_all | solution.py:385
  73.4 0.1 broadcast_in_dim.6
  73.5 19.2 %all_to_all.16.mine = f32[16,16,512]{2,1,0:T(8,128)S(1)} all-to-all(f32[16,16,512]{2,1,0:T(8,128)S(1)} %broadcast_in_dim.6), channel_id=1, replica_groups=mesh['child'=2,'z'=8,'xl'=2,'y'=8,'core'=2] {'child','y'}, dimensions={0} | all-to-all | bytes 1048576 | tf_op jit(solution)/shard_map/all_to_all | solution.py:387
  92.7 5.0 %collective-permute-start.4 = (f32[16,16,512]{2,1,0:T(8,128)S(1)}, f32[16,16,512]{2,1,0:T(8,128)S(1)}, u32[]{:S(2)}, u32[]{:S(2)}) collective-permute-start(f32[16,16,512]{2,1,0:T(8,128)S(1)} %all_to_all.16.mine), channel_id=1, source_target_pairs={{0,1},{1,0},{2,3},{3,2},{4,5},{5,4},{6,7},{7,6},{8,9},{9,8},{10,11... | collective-permute-start | bytes 1572872 | tf_op jit(solution)/shard_map/ppermute | solution.py:390
  97.8 1.5 %collective-permute-done.4.theirs = f32[16,16,512]{2,1,0:T(8,128)S(1)} collective-permute-done((f32[16,16,512]{2,1,0:T(8,128)S(1)}, f32[16,16,512]{2,1,0:T(8,128)S(1)}, u32[]{:S(2)}, u32[]{:S(2)}) %collective-permute-start.4) | collective-permute-done | bytes 524320 | tf_op jit(solution)/shard_map/ppermute | solution.py:390
  99.3 6.2 %shard_map.81 = (f32[256,1024]{1,0:T(8,128)S(1)}, f32[2,128,256]{2,1,0:T(8,128)S(1)}, f32[2,128,128]{2,1,0:T(8,128)S(1)}, f32[2,128,256]{2,1,0:T(8,128)S(1)}) custom-call(s32[5]{0:T(128)S(1)} %stack.28.scalars, f32[16,16,512]{2,1,0:T(8,128)S(1)} %all_to_all.16.mine, f32[16,16,512]{2,1,0:T(8,128)S(1)} %collective-permute-done.4.theirs), custom_call_target="tpu_custom_call" | custom-call | tf_op jit(solution)/shard_map/pallas_call | solution.py:261
  105.5 2.2 %collective-permute-start.5 = (f32[2,128,256]{2,1,0:T(8,128)S(1)}, f32[2,128,256]{2,1,0:T(8,128)S(1)}, u32[]{:S(2)}, u32[]{:S(2)}) collective-permute-start(f32[2,128,256]{2,1,0:T(8,128)S(1)} %get-tuple-element.18.u_head), channel_id=1, source_target_pairs={{0,16},{16,0},{1,17},{17,1},{2,18},{18,2},{3,19},{19,3},{4,20},{20... | collective-permute-start | bytes 786440 | tf_op jit(solution)/shard_map/ppermute | solution.py:393
  107.7 5.0 %shard_map.82 = (f32[136,128]{1,0:T(8,128)S(1)}, f32[2,8,256]{2,1,0:T(8,128)S(1)}, f32[2,8,256]{2,1,0:T(8,128)S(1)}) custom-call(s32[5]{0:T(128)S(1)} %stack.28.scalars, f32[2,128,256]{2,1,0:T(8,128)S(1)} %get-tuple-element.18.u_head, f32[2,128,128]{2,1,0:T(8,128)S(1)} %get-tuple-element.19.x_head, f32[2,128,256]{2,1,0:T(8,128)S(1)} %get-tuple-element.20.rest), custom_call_target="tpu_custom_call" | custom-call | flops 8000000000 | bytes 1000000 | tf_op jit(solution)/shard_map/pallas_call | solution.py:307
  112.7 3.1 %collective-permute-start.6 = (f32[136,128]{1,0:T(8,128)S(1)}, f32[136,128]{1,0:T(8,128)S(1)}, u32[]{:S(2)}, u32[]{:S(2)}) collective-permute-start(f32[136,128]{1,0:T(8,128)S(1)} %get-tuple-element.23), channel_id=1, source_target_pairs={{0,16},{16,0},{1,17},{17,1},{2,18},{18,2},{3,19},{19,3},{4,20},{20... | collective-permute-start | bytes 208904 | tf_op jit(solution)/shard_map/ppermute | solution.py:395
  115.8 1.7 %shard_map.83 = f32[8,1024]{1,0:T(8,128)} custom-call(s32[5]{0:T(128)S(1)} %stack.28.scalars, f32[256,1024]{1,0:T(8,128)S(1)} %get-tuple-element.17.window, f32[2,8,256]{2,1,0:T(8,128)S(1)} %get-tuple-element.21.x_own), custom_call_target="tpu_custom_call" | custom-call | flops 1000000000 | bytes 1000000 | tf_op jit(solution)/shard_map/pallas_call | solution.py:396
  117.6 0.2 collective-permute-done.6.packed
  117.8 0.0 collective-permute-done.5.sib_head
  117.8 1.1 shard_map.84
  (3 shorter events, 0.1 us)
Async XLA Ops:
  0.6 0.8 copy-start
  1.5 36.2 %copy-start.1 = (f32[1,512,1024]{2,1,0:T(8,128)S(1)}, f32[1,512,1024]{2,1,0:T(8,128)}, u32[]{:S(2)}) copy-start(f32[1,512,1024]{2,1,0:T(8,128)} %param.7) | copy-start | bytes 6291460
  1.5 36.3 %copy-start.3 = (s32[4,4]{1,0:T(4,128)S(1)}, s32[4,4]{1,0:T(4,128)}, u32[]{:S(2)}) copy-start(s32[4,4]{1,0:T(4,128)} %pattern.1) | copy-start | bytes 196
  2.3 28.8 %all-to-all-start = ((f32[8,16,1024]{2,1,0:T(8,128)}), f32[8,16,1024]{2,1,0:T(8,128)S(1)}, u32[]{:S(2)}, u32[]{:S(2)}) async-start(f32[8,16,1024]{2,1,0:T(8,128)} %shard_map.77), calls=%async_computation | async-start | bytes 1048576 | tf_op jit(solution)/shard_map/all_to_all | solution.py:373
  13.2 28.3 %collective-permute-start.2 = (f32[512,512]{1,0:T(8,128)}, f32[512,512]{1,0:T(8,128)}, u32[]{:S(2)}, u32[]{:S(2)}) collective-permute-start(f32[512,512]{1,0:T(8,128)} %bitcast.21), channel_id=1, source_target_pairs={{0,256},{256,0},{1,257},{257,1},{2,258},{258,2},{3,259},{259,3},{4... | collective-permute-start | bytes 3145736 | tf_op jit(solution)/shard_map/ppermute | solution.py:351
  18.6 22.9 %collective-permute-start.3 = (s32[2,1,512]{2,1,0:T(1,128)S(1)}, s32[2,1,512]{2,1,0:T(1,128)S(1)}, u32[]{:S(2)}, u32[]{:S(2)}) collective-permute-start(s32[2,1,512]{2,1,0:T(1,128)S(1)} %pad_add_fusion), channel_id=1, source_target_pairs={{0,256},{256,0},{1,257},{257,1},{2,258},{258,2},{3,259},{259,3},{4... | collective-permute-start | bytes 12296 | tf_op jit(solution)/shard_map/ppermute | solution.py:355
  31.2 16.4 %collective-permute-start = (f32[4,16,1024]{2,1,0:T(8,128)S(1)}, f32[4,16,1024]{2,1,0:T(8,128)S(1)}, u32[]{:S(2)}, u32[]{:S(2)}) collective-permute-start(f32[4,16,1024]{2,1,0:T(8,128)S(1)} %get-tuple-element.25), channel_id=1, source_target_pairs={{0,16},{16,256},{256,272},{272,0},{1,17},{17,257},{257,273},{273,1... | collective-permute-start | bytes 786440 | tf_op jit(solution)/shard_map/ppermute | solution.py:377
  34.3 13.3 %collective-permute-start.1 = (f32[4,16,1024]{2,1,0:T(8,128)S(1)}, f32[4,16,1024]{2,1,0:T(8,128)S(1)}, u32[]{:S(2)}, u32[]{:S(2)}) collective-permute-start(f32[4,16,1024]{2,1,0:T(8,128)S(1)} %get-tuple-element.24), channel_id=1, source_target_pairs={{0,272},{16,0},{256,16},{272,256},{1,273},{17,1},{257,17},{273,257... | collective-permute-start | bytes 786440 | tf_op jit(solution)/shard_map/ppermute | solution.py:377
  37.7 1.2 %copy-start.2 = (f32[1,512,512]{2,1,0:T(8,128)S(1)}, f32[1,512,512]{2,1,0:T(8,128)}, u32[]{:S(2)}) copy-start(f32[1,512,512]{2,1,0:T(8,128)} %param.6) | copy-start | bytes 3145732
  92.7 6.6 %collective-permute-start.4 = (f32[16,16,512]{2,1,0:T(8,128)S(1)}, f32[16,16,512]{2,1,0:T(8,128)S(1)}, u32[]{:S(2)}, u32[]{:S(2)}) collective-permute-start(f32[16,16,512]{2,1,0:T(8,128)S(1)} %all_to_all.16.mine), channel_id=1, source_target_pairs={{0,1},{1,0},{2,3},{3,2},{4,5},{5,4},{6,7},{7,6},{8,9},{9,8},{10,11... | collective-permute-start | bytes 1572872 | tf_op jit(solution)/shard_map/ppermute | solution.py:390
  105.5 12.3 %collective-permute-start.5 = (f32[2,128,256]{2,1,0:T(8,128)S(1)}, f32[2,128,256]{2,1,0:T(8,128)S(1)}, u32[]{:S(2)}, u32[]{:S(2)}) collective-permute-start(f32[2,128,256]{2,1,0:T(8,128)S(1)} %get-tuple-element.18.u_head), channel_id=1, source_target_pairs={{0,16},{16,0},{1,17},{17,1},{2,18},{18,2},{3,19},{19,3},{4,20},{20... | collective-permute-start | bytes 786440 | tf_op jit(solution)/shard_map/ppermute | solution.py:393
  112.7 5.1 %collective-permute-start.6 = (f32[136,128]{1,0:T(8,128)S(1)}, f32[136,128]{1,0:T(8,128)S(1)}, u32[]{:S(2)}, u32[]{:S(2)}) collective-permute-start(f32[136,128]{1,0:T(8,128)S(1)} %get-tuple-element.23), channel_id=1, source_target_pairs={{0,16},{16,0},{1,17},{17,1},{2,18},{18,2},{3,19},{19,3},{4,20},{20... | collective-permute-start | bytes 208904 | tf_op jit(solution)/shard_map/ppermute | solution.py:395

commit v8 on v7

--- a/solution.py
+++ b/solution.py
@@ -102,16 +102,13 @@
     )(scalars, total, block, maps)
 
 
-def apply_kernel(own, ahead, behind, top, low, parts):
-    count, sides, width, half_rows = parts.shape
+def apply_kernel(scalars, own, ahead, behind, top, low, give, keep):
+    core = scalars[2]
+    count, width, half_rows = give.shape
     depth = top.shape[0]
     rows = count * width
     ordered = jnp.concatenate(
-        [
-            piece[:, side].reshape(-1, depth)
-            for side in range(sides)
-            for piece in (own, ahead, behind)
-        ]
+        [piece[:, side].reshape(-1, depth) for side in range(2) for piece in (own, ahead, behind)]
     )
     high_lines, low_lines = two_parts(ordered)
     for tile in range(half_rows // BT):
@@ -121,27 +118,29 @@
             + dot(low_lines, top[:, lanes], NN)
             + dot(high_lines, low[:, lanes], NN)
         )
-        for side in range(sides):
+        first, second = out[:rows], out[rows:]
+        for target, value in (
+            (give, jnp.where(core == 0, second, first)),
+            (keep, jnp.where(core == 0, first, second)),
+        ):
             for piece in range(2):
-                start = side * rows + piece * rows // 2
                 there = slice(piece * width // 2, (piece + 1) * width // 2)
-                parts[:, side, there, lanes] = out[start : start + rows // 2].reshape(
-                    count, width // 2, BT
-                )
-
-
-def apply_operator(own, ahead, behind, top, low):
+                part = value[piece * rows // 2 : (piece + 1) * rows // 2]
+                target[:, there, lanes] = part.reshape(count, width // 2, BT)
+
+
+def apply_operator(scalars, own, ahead, behind, top, low):
     count, width, depth = own.shape
     half_rows = top.shape[1]
     lines = [v.reshape(v.shape[0], 2, width // 2, depth) for v in (own, ahead, behind)]
     return pl.pallas_call(
         apply_kernel,
-        in_specs=[VMEM] * 5,
-        out_specs=VMEM,
-        out_shape=shape(count, 2, width, half_rows),
+        in_specs=[SMEM] + [VMEM] * 5,
+        out_specs=[VMEM, VMEM],
+        out_shape=[shape(count, width, half_rows)] * 2,
         compiler_params=PARAMS,
         cost_estimate=pl.CostEstimate(flops=10**9, bytes_accessed=6 * 10**6, transcendentals=0),
-    )(*lines, top, low)
+    )(scalars, *lines, top, low)
 
 
 def spread_out(row_or_column):
@@ -316,14 +315,18 @@
     )(scalars, u_head, x_head, rest)
 
 
-def bases_kernel(scalars, window, x_own, out):
-    both = jnp.concatenate([x_own[0], x_own[1]], 0)
-    solved = dot(both, window[...], NN, highest)
+def bases_kernel(scalars, window, x_own, u_own, sib_head, out, head_part):
+    high_x, low_x = two_parts(jnp.concatenate([x_own[0], x_own[1]], 0))
+    high_w, low_w = two_parts(window[...])
+    wide = dot(jnp.concatenate([high_x, low_x], 0), high_w, NN)
+    solved = wide[:16] + wide[16:] + dot(high_x, low_w, NN)
     lane = lax.broadcasted_iota(jnp.int32, out.shape, 1)
     out[...] = jnp.where(lane < scalars[3], solved[:8], solved[8:])
-
-
-def coupling_kernel(u_own, sib_head, packed, out):
+    for leaf in range(2):
+        head_part[leaf] = dot(u_own[leaf], sib_head[leaf], NT, highest)
+
+
+def coupling_kernel(u_own, head_part, packed, out):
     row = lax.broadcasted_iota(jnp.int32, (HALF, HALF), 0)
     column = lax.broadcasted_iota(jnp.int32, (HALF, HALF), 1)
     square = packed[:HALF, :]
@@ -333,9 +336,8 @@
         jnp.where(row == column, packed[HALF : HALF + 1, :], second),
     ]
     for leaf in range(2):
-        own = u_own[leaf]
-        out[leaf, :, :HALF] = dot(own, sib_head[leaf], NT, highest)
-        out[leaf, :, HALF:] = dot(own[:, HALF:], sib_tail[leaf], NT, highest)
+        out[leaf, :, :HALF] = head_part[leaf]
+        out[leaf, :, HALF:] = dot(u_own[leaf, :, HALF:], sib_tail[leaf], NT, highest)
 
 
 def local(contrib, assembled, pattern, omega, row_maps, leaf_bounds):
@@ -381,8 +383,9 @@
     sibling_block, sibling_maps = lax.optimization_barrier((sibling_block, sibling_maps))
     top, low = whole_operator(scalars, total, sibling_block, sibling_maps)
 
-    parts = apply_operator(own, *other, top, low)
-    terms = lax.all_to_all(parts.reshape((-1,) + parts.shape[2:]), ("y", "core"), 0, 0)
+    give, keep = apply_operator(scalars, own, *other, top, low)
+    parts = keep + lax.ppermute(give, "core", SWAP)
+    terms = lax.all_to_all(parts, "y", 0, 0)
     samples = jnp.sum(terms, axis=0)
     mine = lax.all_to_all(
         jnp.broadcast_to(samples, (groups,) + samples.shape), ("child", "y"), 0, 0
@@ -393,21 +396,21 @@
     sib_head = lax.ppermute(u_head, "xl", SWAP)
     u_tail, u_own, x_own = factor_tail(scalars, u_head, x_head, rest)
     sib_tail = lax.ppermute(u_tail, "xl", SWAP)
-    bases = pl.pallas_call(
+    bases, head_part = pl.pallas_call(
         bases_kernel,
-        in_specs=[SMEM, VMEM, VMEM],
-        out_specs=VMEM,
-        out_shape=shape(width, window_rows),
+        in_specs=[SMEM] + [VMEM] * 4,
+        out_specs=[VMEM, VMEM],
+        out_shape=[shape(width, window_rows), shape(2, width, HALF)],
         compiler_params=PARAMS,
         cost_estimate=pl.CostEstimate(flops=10**9, bytes_accessed=10**6, transcendentals=0),
-    )(scalars, window, x_own)
+    )(scalars, window, x_own, u_own, sib_head)
     coupling = pl.pallas_call(
         coupling_kernel,
         in_specs=[VMEM] * 3,
         out_specs=VMEM,
         out_shape=shape(2, width, R),
         compiler_params=PARAMS,
-    )(u_own, sib_head, sib_tail)
+    )(u_own, head_part, sib_tail)
     return (bases.T, coupling[None])
 
 

time: 120 us -> 116 us (0.967)
  blocking collectives: 44 us -> 36.6 us
  starting transfers between devices: 34.5 us -> 36.7 us
  waiting for transfers between devices: 14.4 us -> 15.8 us
    all_to_all x1, blocking collectives: 24.8 us -> 17.7 us  [local(): terms = lax.all_to_all(parts, 'y', 0, 0)]
    ppermute x0 -> x1, starting transfers between devices: none -> 2.47 us  [local(): parts = keep + lax.ppermute(give, 'core', SWAP)]
  transfers between devices with their start and end apart: 8 -> 9, of which waited for: 4 -> 5; matrix products, arithmetic and copies ran while one was open for 1% -> 1% of each run, Pallas kernels for 10% -> 11%
where the time goes in v8:
time: 116 us; the launch traced here: 115 us
  starting transfers between devices  36.7 us (32%)
  blocking collectives  36.6 us (32%)
  Pallas kernels  21.7 us (19%)
  waiting for transfers between devices  15.8 us (14%)
  local copies, waits for them, and re-layouts  2.23 us (2%)
  between operations  1.48 us (1%)
    all_to_all x1, blocking collectives, local(): lax.all_to_all(jnp.broadcast_to(samples, (groups,) + samples.shape), ('ch...  18.9 us
    all_to_all x1, blocking collectives, local(): terms = lax.all_to_all(parts, 'y', 0, 0)  17.7 us
    all_to_all x1, starting transfers between devices, local(): own = lax.all_to_all(copies, 'z', 0, 0)  10.9 us
    all_to_all x1, waiting for transfers between devices, local(): own = lax.all_to_all(copies, 'z', 0, 0)  9.71 us
    ppermute x2, starting transfers between devices, local(): lax.ppermute(piece, ('child', 'xl'), [(i, (i + step) % ring) for i in ran...  6.49 us
    pallas_call x1, Pallas kernels, factor_head(): pl.pallas_call(head_kernel, in_specs=[SMEM, VMEM, VMEM], out_specs=[VMEM]...  6.17 us
    pallas_call x1, Pallas kernels, factor_tail(): pl.pallas_call(tail_kernel, in_specs=[SMEM] + [VMEM] * 3, out_specs=[VMEM...  5.04 us
    ppermute x1, starting transfers between devices, local(): theirs = lax.ppermute(mine, 'core', SWAP)  4.86 us
  transfers between devices with their start and end apart: 9, of which 5 were waited for; matrix products, arithmetic and copies ran while one was open for 1% of the time, Pallas kernels for 11%

profile of v8, /device:TPU:1, one launch (start us, length us, event | category | flops | bytes accessed | tf_op | source)
XLA Modules:
  0.0 115.3 jit_solution(7866200774652662134)
XLA Ops:
  0.6 0.0 copy-start
  0.6 0.8 copy-done
  1.5 0.0 copy-start.1
  1.5 0.0 copy-start.3
  1.5 0.9 shard_map.77
  2.3 10.9 %all-to-all-start = ((f32[8,16,1024]{2,1,0:T(8,128)}), f32[8,16,1024]{2,1,0:T(8,128)S(1)}, u32[]{:S(2)}, u32[]{:S(2)}) async-start(f32[8,16,1024]{2,1,0:T(8,128)} %shard_map.77), calls=%async_computation | async-start | bytes 1048576 | tf_op jit(solution)/shard_map/all_to_all | solution.py:375
  13.2 4.6 %collective-permute-start.2 = (f32[512,512]{1,0:T(8,128)}, f32[512,512]{1,0:T(8,128)}, u32[]{:S(2)}, u32[]{:S(2)}) collective-permute-start(f32[512,512]{1,0:T(8,128)} %bitcast.19), channel_id=1, source_target_pairs={{0,256},{256,0},{1,257},{257,1},{2,258},{258,2},{3,259},{259,3},{4... | collective-permute-start | bytes 3145736 | tf_op jit(solution)/shard_map/ppermute | solution.py:353
  17.9 0.7 dynamic-slice_subtract_fusion
  18.6 2.1 %collective-permute-start.3 = (s32[2,1,512]{2,1,0:T(1,128)S(1)}, s32[2,1,512]{2,1,0:T(1,128)S(1)}, u32[]{:S(2)}, u32[]{:S(2)}) collective-permute-start(s32[2,1,512]{2,1,0:T(1,128)S(1)} %pad_add_fusion), channel_id=1, source_target_pairs={{0,256},{256,0},{1,257},{257,1},{2,258},{258,2},{3,259},{259,3},{4... | collective-permute-start | bytes 12296 | tf_op jit(solution)/shard_map/ppermute | solution.py:357
  21.4 0.1 stack.28.scalars
  21.4 9.7 %all-to-all-done = f32[8,16,1024]{2,1,0:T(8,128)S(1)} async-done(((f32[8,16,1024]{2,1,0:T(8,128)}), f32[8,16,1024]{2,1,0:T(8,128)S(1)}, u32[]{:S(2)}, u32[]{:S(2)}) %all-to-all-start) | async-done | bytes 524320 | tf_op jit(solution)/shard_map/all_to_all | solution.py:375
  31.2 3.1 %collective-permute-start = (f32[4,16,1024]{2,1,0:T(8,128)S(1)}, f32[4,16,1024]{2,1,0:T(8,128)S(1)}, u32[]{:S(2)}, u32[]{:S(2)}) collective-permute-start(f32[4,16,1024]{2,1,0:T(8,128)S(1)} %get-tuple-element.33), channel_id=1, source_target_pairs={{0,16},{16,256},{256,272},{272,0},{1,17},{17,257},{257,273},{273,1... | collective-permute-start | bytes 786440 | tf_op jit(solution)/shard_map/ppermute | solution.py:379
  34.3 3.4 %collective-permute-start.1 = (f32[4,16,1024]{2,1,0:T(8,128)S(1)}, f32[4,16,1024]{2,1,0:T(8,128)S(1)}, u32[]{:S(2)}, u32[]{:S(2)}) collective-permute-start(f32[4,16,1024]{2,1,0:T(8,128)S(1)} %get-tuple-element.32), channel_id=1, source_target_pairs={{0,272},{16,0},{256,16},{272,256},{1,273},{17,1},{257,17},{273,257... | collective-permute-start | bytes 786440 | tf_op jit(solution)/shard_map/ppermute | solution.py:379
  37.7 0.0 copy-done.1
  37.7 0.0 copy-done.3
  37.7 0.0 copy-start.2
  37.7 1.2 %copy-done.2 = f32[1,512,512]{2,1,0:T(8,128)S(1)} copy-done((f32[1,512,512]{2,1,0:T(8,128)S(1)}, f32[1,512,512]{2,1,0:T(8,128)}, u32[]{:S(2)}) %copy-start.2) | copy-done | bytes 1048600
  39.0 2.5 %shard_map.78.total = f32[1024,512]{1,0:T(8,128)S(1)} custom-call(s32[5]{0:T(128)S(1)} %stack.28.scalars, s32[4,4]{1,0:T(4,128)S(1)} %copy-done.3, f32[512,512]{1,0:T(8,128)S(1)} %bitcast.20, f32[512,1024]{1,0:T(8,128)S(1)} %bitcast.18, s32[1,512]{1,0:T(1,128)S(1)} %get-tuple-element.35.columns, s32[1,512]{1,0:T(1,128)S(1)} %get-tuple-element.34.targets), custom_call_target="tpu_custom_call" | custom-call | flops 2000000000 | bytes 5000000 | tf_op jit(solution)/shard_map/pallas_call | solution.py:79
  41.5 0.0 collective-permute-done.3.maps
  41.5 0.0 collective-permute-done.2.block
  41.5 3.2 %shard_map.79 = (bf16[1024,512]{1,0:T(8,128)(2,1)S(1)}, bf16[1024,512]{1,0:T(8,128)(2,1)S(1)}) custom-call(s32[5]{0:T(128)S(1)} %stack.28.scalars, f32[1024,512]{1,0:T(8,128)S(1)} %shard_map.78.total, f32[512,512]{1,0:T(8,128)} %collective-permute-done.2.block, s32[2,1,512]{2,1,0:T(1,128)S(1)} %collective-permute-done.3.maps), custom_call_target="tpu_custom_call" | custom-call | flops 2000000000 | bytes 5000000 | tf_op jit(solution)/shard_map/pallas_call | solution.py:92
  44.7 2.9 %collective-permute-done = f32[4,16,1024]{2,1,0:T(8,128)S(1)} collective-permute-done((f32[4,16,1024]{2,1,0:T(8,128)S(1)}, f32[4,16,1024]{2,1,0:T(8,128)S(1)}, u32[]{:S(2)}, u32[]{:S(2)}) %collective-permute-start) | collective-permute-done | bytes 262176 | tf_op jit(solution)/shard_map/ppermute | solution.py:379
  47.6 0.0 collective-permute-done.1
  47.6 1.5 %shard_map.80 = (f32[8,16,512]{2,1,0:T(8,128)S(1)}, f32[8,16,512]{2,1,0:T(8,128)S(1)}) custom-call(s32[5]{0:T(128)S(1)} %stack.28.scalars, f32[8,2,8,1024]{3,2,1,0:T(8,128)S(1)} %bitcast.14, f32[4,2,8,1024]{3,2,1,0:T(8,128)S(1)} %bitcast.21, f32[4,2,8,1024]{3,2,1,0:T(8,128)S(1)} %bitcast.22, bf16[1024,512]{1,0:T(8,128)(2,1)S(1)} %get-tuple-element.19.top, ...), custom_call_target="tpu_custom_call" | custom-call | flops 1000000000 | bytes 6000000 | tf_op jit(solution)/shard_map/pallas_call | solution.py:136
  49.1 2.5 %collective-permute-start.4 = (f32[8,16,512]{2,1,0:T(8,128)S(1)}, f32[8,16,512]{2,1,0:T(8,128)S(1)}, u32[]{:S(2)}, u32[]{:S(2)}) collective-permute-start(f32[8,16,512]{2,1,0:T(8,128)S(1)} %get-tuple-element.22), channel_id=1, source_target_pairs={{0,1},{1,0},{2,3},{3,2},{4,5},{5,4},{6,7},{7,6},{8,9},{9,8},{10,11... | collective-permute-start | bytes 786440 | tf_op jit(solution)/shard_map/ppermute | solution.py:387
  51.6 1.1 collective-permute-done.4
  52.8 17.7 %all_to_all.15 = f32[8,16,512]{2,1,0:T(8,128)S(1)} all-to-all(f32[8,16,512]{2,1,0:T(8,128)S(1)} %add.24), channel_id=1, replica_groups=mesh['child'=2,'z'=8,'xl'=2,'y'=8,'core'=2] {'y'}, dimensions={0} | all-to-all | bytes 524288 | tf_op jit(solution)/shard_map/all_to_all | solution.py:388
  70.5 0.1 broadcast_in_dim.6
  70.6 18.9 %all_to_all.16.mine = f32[16,16,512]{2,1,0:T(8,128)S(1)} all-to-all(f32[16,16,512]{2,1,0:T(8,128)S(1)} %broadcast_in_dim.6), channel_id=1, replica_groups=mesh['child'=2,'z'=8,'xl'=2,'y'=8,'core'=2] {'child','y'}, dimensions={0} | all-to-all | bytes 1048576 | tf_op jit(solution)/shard_map/all_to_all | solution.py:390
  89.4 4.9 %collective-permute-start.5 = (f32[16,16,512]{2,1,0:T(8,128)S(1)}, f32[16,16,512]{2,1,0:T(8,128)S(1)}, u32[]{:S(2)}, u32[]{:S(2)}) collective-permute-start(f32[16,16,512]{2,1,0:T(8,128)S(1)} %all_to_all.16.mine), channel_id=1, source_target_pairs={{0,1},{1,0},{2,3},{3,2},{4,5},{5,4},{6,7},{7,6},{8,9},{9,8},{10,11... | collective-permute-start | bytes 1572872 | tf_op jit(solution)/shard_map/ppermute | solution.py:393
  94.3 1.5 %collective-permute-done.5.theirs = f32[16,16,512]{2,1,0:T(8,128)S(1)} collective-permute-done((f32[16,16,512]{2,1,0:T(8,128)S(1)}, f32[16,16,512]{2,1,0:T(8,128)S(1)}, u32[]{:S(2)}, u32[]{:S(2)}) %collective-permute-start.5) | collective-permute-done | bytes 524320 | tf_op jit(solution)/shard_map/ppermute | solution.py:393
  95.8 6.2 %shard_map.81 = (f32[256,1024]{1,0:T(8,128)S(1)}, f32[2,128,256]{2,1,0:T(8,128)S(1)}, f32[2,128,128]{2,1,0:T(8,128)S(1)}, f32[2,128,256]{2,1,0:T(8,128)S(1)}) custom-call(s32[5]{0:T(128)S(1)} %stack.28.scalars, f32[16,16,512]{2,1,0:T(8,128)S(1)} %all_to_all.16.mine, f32[16,16,512]{2,1,0:T(8,128)S(1)} %collective-permute-done.5.theirs), custom_call_target="tpu_custom_call" | custom-call | tf_op jit(solution)/shard_map/pallas_call | solution.py:260
  102.0 2.2 %collective-permute-start.6 = (f32[2,128,256]{2,1,0:T(8,128)S(1)}, f32[2,128,256]{2,1,0:T(8,128)S(1)}, u32[]{:S(2)}, u32[]{:S(2)}) collective-permute-start(f32[2,128,256]{2,1,0:T(8,128)S(1)} %get-tuple-element.24.u_head), channel_id=1, source_target_pairs={{0,16},{16,0},{1,17},{17,1},{2,18},{18,2},{3,19},{19,3},{4,20},{20... | collective-permute-start | bytes 786440 | tf_op jit(solution)/shard_map/ppermute | solution.py:396
  104.2 5.0 %shard_map.82 = (f32[136,128]{1,0:T(8,128)S(1)}, f32[2,8,256]{2,1,0:T(8,128)S(1)}, f32[2,8,256]{2,1,0:T(8,128)S(1)}) custom-call(s32[5]{0:T(128)S(1)} %stack.28.scalars, f32[2,128,256]{2,1,0:T(8,128)S(1)} %get-tuple-element.24.u_head, f32[2,128,128]{2,1,0:T(8,128)S(1)} %get-tuple-element.25.x_head, f32[2,128,256]{2,1,0:T(8,128)S(1)} %get-tuple-element.26.rest), custom_call_target="tpu_custom_call" | custom-call | flops 8000000000 | bytes 1000000 | tf_op jit(solution)/shard_map/pallas_call | solution.py:306
  109.3 3.1 %collective-permute-start.7 = (f32[136,128]{1,0:T(8,128)S(1)}, f32[136,128]{1,0:T(8,128)S(1)}, u32[]{:S(2)}, u32[]{:S(2)}) collective-permute-start(f32[136,128]{1,0:T(8,128)S(1)} %get-tuple-element.31), channel_id=1, source_target_pairs={{0,16},{16,0},{1,17},{17,1},{2,18},{18,2},{3,19},{19,3},{4,20},{20... | collective-permute-start | bytes 208904 | tf_op jit(solution)/shard_map/ppermute | solution.py:398
  112.3 0.0 collective-permute-done.6.sib_head
  112.4 1.4 %shard_map.83 = (f32[8,1024]{1,0:T(8,128)}, f32[2,8,128]{2,1,0:T(8,128)S(1)}) custom-call(s32[5]{0:T(128)S(1)} %stack.28.scalars, f32[256,1024]{1,0:T(8,128)S(1)} %get-tuple-element.23.window, f32[2,8,256]{2,1,0:T(8,128)S(1)} %get-tuple-element.27.x_own, f32[2,8,256]{2,1,0:T(8,128)S(1)} %get-tuple-element.28.u_own, ...), custom_call_target="tpu_custom_call" | custom-call | flops 1000000000 | bytes 1000000 | tf_op jit(solution)/shard_map/pallas_call | solution.py:399
  113.8 0.5 collective-permute-done.7.packed
  114.3 1.0 shard_map.84
  (4 shorter events, 0.1 us)
Async XLA Ops:
  0.6 0.8 copy-start
  1.5 36.2 %copy-start.1 = (f32[1,512,1024]{2,1,0:T(8,128)S(1)}, f32[1,512,1024]{2,1,0:T(8,128)}, u32[]{:S(2)}) copy-start(f32[1,512,1024]{2,1,0:T(8,128)} %param.7) | copy-start | bytes 6291460
  1.5 36.2 %copy-start.3 = (s32[4,4]{1,0:T(4,128)S(1)}, s32[4,4]{1,0:T(4,128)}, u32[]{:S(2)}) copy-start(s32[4,4]{1,0:T(4,128)} %pattern.1) | copy-start | bytes 196
  2.3 28.8 %all-to-all-start = ((f32[8,16,1024]{2,1,0:T(8,128)}), f32[8,16,1024]{2,1,0:T(8,128)S(1)}, u32[]{:S(2)}, u32[]{:S(2)}) async-start(f32[8,16,1024]{2,1,0:T(8,128)} %shard_map.77), calls=%async_computation | async-start | bytes 1048576 | tf_op jit(solution)/shard_map/all_to_all | solution.py:375
  13.2 28.3 %collective-permute-start.2 = (f32[512,512]{1,0:T(8,128)}, f32[512,512]{1,0:T(8,128)}, u32[]{:S(2)}, u32[]{:S(2)}) collective-permute-start(f32[512,512]{1,0:T(8,128)} %bitcast.19), channel_id=1, source_target_pairs={{0,256},{256,0},{1,257},{257,1},{2,258},{258,2},{3,259},{259,3},{4... | collective-permute-start | bytes 3145736 | tf_op jit(solution)/shard_map/ppermute | solution.py:353
  18.6 22.9 %collective-permute-start.3 = (s32[2,1,512]{2,1,0:T(1,128)S(1)}, s32[2,1,512]{2,1,0:T(1,128)S(1)}, u32[]{:S(2)}, u32[]{:S(2)}) collective-permute-start(s32[2,1,512]{2,1,0:T(1,128)S(1)} %pad_add_fusion), channel_id=1, source_target_pairs={{0,256},{256,0},{1,257},{257,1},{2,258},{258,2},{3,259},{259,3},{4... | collective-permute-start | bytes 12296 | tf_op jit(solution)/shard_map/ppermute | solution.py:357
  31.2 16.4 %collective-permute-start = (f32[4,16,1024]{2,1,0:T(8,128)S(1)}, f32[4,16,1024]{2,1,0:T(8,128)S(1)}, u32[]{:S(2)}, u32[]{:S(2)}) collective-permute-start(f32[4,16,1024]{2,1,0:T(8,128)S(1)} %get-tuple-element.33), channel_id=1, source_target_pairs={{0,16},{16,256},{256,272},{272,0},{1,17},{17,257},{257,273},{273,1... | collective-permute-start | bytes 786440 | tf_op jit(solution)/shard_map/ppermute | solution.py:379
  34.3 13.3 %collective-permute-start.1 = (f32[4,16,1024]{2,1,0:T(8,128)S(1)}, f32[4,16,1024]{2,1,0:T(8,128)S(1)}, u32[]{:S(2)}, u32[]{:S(2)}) collective-permute-start(f32[4,16,1024]{2,1,0:T(8,128)S(1)} %get-tuple-element.32), channel_id=1, source_target_pairs={{0,272},{16,0},{256,16},{272,256},{1,273},{17,1},{257,17},{273,257... | collective-permute-start | bytes 786440 | tf_op jit(solution)/shard_map/ppermute | solution.py:379
  37.7 1.2 %copy-start.2 = (f32[1,512,512]{2,1,0:T(8,128)S(1)}, f32[1,512,512]{2,1,0:T(8,128)}, u32[]{:S(2)}) copy-start(f32[1,512,512]{2,1,0:T(8,128)} %param.6) | copy-start | bytes 3145732
  49.1 3.6 %collective-permute-start.4 = (f32[8,16,512]{2,1,0:T(8,128)S(1)}, f32[8,16,512]{2,1,0:T(8,128)S(1)}, u32[]{:S(2)}, u32[]{:S(2)}) collective-permute-start(f32[8,16,512]{2,1,0:T(8,128)S(1)} %get-tuple-element.22), channel_id=1, source_target_pairs={{0,1},{1,0},{2,3},{3,2},{4,5},{5,4},{6,7},{7,6},{8,9},{9,8},{10,11... | collective-permute-start | bytes 786440 | tf_op jit(solution)/shard_map/ppermute | solution.py:387
  89.4 6.4 %collective-permute-start.5 = (f32[16,16,512]{2,1,0:T(8,128)S(1)}, f32[16,16,512]{2,1,0:T(8,128)S(1)}, u32[]{:S(2)}, u32[]{:S(2)}) collective-permute-start(f32[16,16,512]{2,1,0:T(8,128)S(1)} %all_to_all.16.mine), channel_id=1, source_target_pairs={{0,1},{1,0},{2,3},{3,2},{4,5},{5,4},{6,7},{7,6},{8,9},{9,8},{10,11... | collective-permute-start | bytes 1572872 | tf_op jit(solution)/shard_map/ppermute | solution.py:393
  102.0 10.3 %collective-permute-start.6 = (f32[2,128,256]{2,1,0:T(8,128)S(1)}, f32[2,128,256]{2,1,0:T(8,128)S(1)}, u32[]{:S(2)}, u32[]{:S(2)}) collective-permute-start(f32[2,128,256]{2,1,0:T(8,128)S(1)} %get-tuple-element.24.u_head), channel_id=1, source_target_pairs={{0,16},{16,0},{1,17},{17,1},{2,18},{18,2},{3,19},{19,3},{4,20},{20... | collective-permute-start | bytes 786440 | tf_op jit(solution)/shard_map/ppermute | solution.py:396
  109.3 5.1 %collective-permute-start.7 = (f32[136,128]{1,0:T(8,128)S(1)}, f32[136,128]{1,0:T(8,128)S(1)}, u32[]{:S(2)}, u32[]{:S(2)}) collective-permute-start(f32[136,128]{1,0:T(8,128)S(1)} %get-tuple-element.31), channel_id=1, source_target_pairs={{0,16},{16,0},{1,17},{17,1},{2,18},{18,2},{3,19},{19,3},{4,20},{20... | collective-permute-start | bytes 208904 | tf_op jit(solution)/shard_map/ppermute | solution.py:398

commit v9 on v8

--- a/solution.py
+++ b/solution.py
@@ -1,3 +1,5 @@
+import functools
+
 import jax
 import jax.numpy as jnp
 from jax import lax
@@ -102,15 +104,11 @@
     )(scalars, total, block, maps)
 
 
-def apply_kernel(scalars, own, ahead, behind, top, low, give, keep):
-    core = scalars[2]
-    count, width, half_rows = give.shape
-    depth = top.shape[0]
-    rows = count * width
-    ordered = jnp.concatenate(
-        [piece[:, side].reshape(-1, depth) for side in range(2) for piece in (own, ahead, behind)]
-    )
-    high_lines, low_lines = two_parts(ordered)
+def mapped(pieces, side, top, low, targets):
+    depth, half_rows = top.shape
+    lines = jnp.concatenate([piece[:, side].reshape(-1, depth) for piece in pieces])
+    high_lines, low_lines = two_parts(lines)
+    count, width, _ = targets.shape
     for tile in range(half_rows // BT):
         lanes = slice(tile * BT, (tile + 1) * BT)
         out = (
@@ -118,29 +116,59 @@
             + dot(low_lines, top[:, lanes], NN)
             + dot(high_lines, low[:, lanes], NN)
         )
-        first, second = out[:rows], out[rows:]
-        for target, value in (
-            (give, jnp.where(core == 0, second, first)),
-            (keep, jnp.where(core == 0, first, second)),
-        ):
-            for piece in range(2):
-                there = slice(piece * width // 2, (piece + 1) * width // 2)
-                part = value[piece * rows // 2 : (piece + 1) * rows // 2]
-                target[:, there, lanes] = part.reshape(count, width // 2, BT)
-
-
-def apply_operator(scalars, own, ahead, behind, top, low):
-    count, width, depth = own.shape
-    half_rows = top.shape[1]
-    lines = [v.reshape(v.shape[0], 2, width // 2, depth) for v in (own, ahead, behind)]
-    return pl.pallas_call(
-        apply_kernel,
+        targets[:, :, lanes] = out.reshape(count, width, BT)
+
+
+def on_each_core(core, body):
+    for value in range(2):
+        pl.when(core == value)(lambda value=value: body(value))
+
+
+def own_columns_kernel(scalars, own, top, low, give, keep):
+    def body(core):
+        mapped([own], 1 - core, top, low, give)
+        mapped([own], core, top, low, keep)
+
+    on_each_core(scalars[2], body)
+
+
+def other_columns_kernel(given, scalars, first, ahead, behind, top, low, out):
+    width = first.shape[1]
+    out[:, :width, :] = first[...]
+
+    def body(core):
+        mapped([ahead, behind], 1 - core if given else core, top, low, out.at[:, width:, :])
+
+    on_each_core(scalars[2], body)
+
+
+def sides(gathered):
+    count, both, depth = gathered.shape
+    return gathered.reshape(count, 2, both // 2, depth)
+
+
+def own_columns(scalars, own, top, low):
+    lines = sides(own)
+    return pl.pallas_call(
+        own_columns_kernel,
+        in_specs=[SMEM] + [VMEM] * 3,
+        out_specs=[VMEM, VMEM],
+        out_shape=[shape(lines.shape[0], lines.shape[2], top.shape[1])] * 2,
+        compiler_params=PARAMS,
+        cost_estimate=pl.CostEstimate(flops=5 * 10**8, bytes_accessed=10**6, transcendentals=0),
+    )(scalars, lines, top, low)
+
+
+def other_columns(given, scalars, first, ahead, behind, top, low):
+    count, width, half_rows = first.shape
+    return pl.pallas_call(
+        functools.partial(other_columns_kernel, given),
         in_specs=[SMEM] + [VMEM] * 5,
-        out_specs=[VMEM, VMEM],
-        out_shape=[shape(count, width, half_rows)] * 2,
-        compiler_params=PARAMS,
-        cost_estimate=pl.CostEstimate(flops=10**9, bytes_accessed=6 * 10**6, transcendentals=0),
-    )(scalars, *lines, top, low)
+        out_specs=VMEM,
+        out_shape=shape(count, 2 * width, half_rows),
+        compiler_params=PARAMS,
+        cost_estimate=pl.CostEstimate(flops=5 * 10**8, bytes_accessed=10**6, transcendentals=0),
+    )(scalars, first, sides(ahead), sides(behind), top, low)
 
 
 def spread_out(row_or_column):
@@ -383,8 +411,10 @@
     sibling_block, sibling_maps = lax.optimization_barrier((sibling_block, sibling_maps))
     top, low = whole_operator(scalars, total, sibling_block, sibling_maps)
 
-    give, keep = apply_operator(scalars, own, *other, top, low)
-    parts = keep + lax.ppermute(give, "core", SWAP)
+    give, keep = own_columns(scalars, own, top, low)
+    give = other_columns(True, scalars, give, *other, top, low)
+    arrived = lax.ppermute(give, "core", SWAP)
+    parts = other_columns(False, scalars, keep, *other, top, low) + arrived
     terms = lax.all_to_all(parts, "y", 0, 0)
     samples = jnp.sum(terms, axis=0)
     mine = lax.all_to_all(

time: 116 us -> 118 us (1.017)
  waiting for transfers between devices: 15.8 us -> 12.9 us
  Pallas kernels: 21.7 us -> 24.3 us
  starting transfers between devices: 36.7 us -> 38.2 us
    pallas_call x1 -> x3, Pallas kernels: 1.54 us -> 4.13 us  [the longest x2 2.4 us: other_columns(): pl.pallas_call(functools.partial(other_columns_kernel, given), in_specs=[...]
    ppermute x2, waiting for transfers between devices: 2.9 us -> 1.18 us  [local(): lax.ppermute(piece, ('child', 'xl'), [(i, (i + step) % ring) for i in ran...]
  transfers between devices with their start and end apart: 9 -> 9, of which waited for: 5 -> 4; matrix products, arithmetic and copies ran while one was open for 1% -> 1% of each run, Pallas kernels for 11% -> 13%
where the time goes in v9:
time: 118 us; the launch traced here: 116 us
  starting transfers between devices  38.2 us (32%)
  blocking collectives  36.5 us (31%)
  Pallas kernels  24.3 us (21%)
  waiting for transfers between devices  12.9 us (11%)
  local copies, waits for them, and re-layouts  2.24 us (2%)
  between operations  1.51 us (1%)
    all_to_all x1, blocking collectives, local(): terms = lax.all_to_all(parts, 'y', 0, 0)  18.4 us
    all_to_all x1, blocking collectives, local(): lax.all_to_all(jnp.broadcast_to(samples, (groups,) + samples.shape), ('ch...  18.1 us
    all_to_all x1, starting transfers between devices, local(): own = lax.all_to_all(copies, 'z', 0, 0)  10.9 us
    all_to_all x1, waiting for transfers between devices, local(): own = lax.all_to_all(copies, 'z', 0, 0)  9.71 us
    ppermute x2, starting transfers between devices, local(): lax.ppermute(piece, ('child', 'xl'), [(i, (i + step) % ring) for i in ran...  6.49 us
    pallas_call x1, Pallas kernels, factor_head(): pl.pallas_call(head_kernel, in_specs=[SMEM, VMEM, VMEM], out_specs=[VMEM]...  6.16 us
    ppermute x1, starting transfers between devices, local(): theirs = lax.ppermute(mine, 'core', SWAP)  5.38 us
    pallas_call x1, Pallas kernels, factor_tail(): pl.pallas_call(tail_kernel, in_specs=[SMEM] + [VMEM] * 3, out_specs=[VMEM...  5.04 us
  transfers between devices with their start and end apart: 9, of which 4 were waited for; matrix products, arithmetic and copies ran while one was open for 1% of the time, Pallas kernels for 13%

profile of v9, /device:TPU:1, one launch (start us, length us, event | category | flops | bytes accessed | tf_op | source)
XLA Modules:
  0.0 116.4 jit_solution(3842552626632571562)
XLA Ops:
  0.6 0.0 copy-start
  0.6 0.8 copy-done
  1.5 0.0 copy-start.1
  1.5 0.0 copy-start.3
  1.5 0.9 shard_map.77
  2.3 10.9 %all-to-all-start = ((f32[8,16,1024]{2,1,0:T(8,128)}), f32[8,16,1024]{2,1,0:T(8,128)S(1)}, u32[]{:S(2)}, u32[]{:S(2)}) async-start(f32[8,16,1024]{2,1,0:T(8,128)} %shard_map.77), calls=%async_computation | async-start | bytes 1048576 | tf_op jit(solution)/shard_map/all_to_all | solution.py:403
  13.2 4.6 %collective-permute-start = (f32[512,512]{1,0:T(8,128)}, f32[512,512]{1,0:T(8,128)}, u32[]{:S(2)}, u32[]{:S(2)}) collective-permute-start(f32[512,512]{1,0:T(8,128)} %bitcast.23), channel_id=1, source_target_pairs={{0,256},{256,0},{1,257},{257,1},{2,258},{258,2},{3,259},{259,3},{4... | collective-permute-start | bytes 3145736 | tf_op jit(solution)/shard_map/ppermute | solution.py:381
  17.9 0.7 dynamic-slice_subtract_fusion
  18.6 2.1 %collective-permute-start.1 = (s32[2,1,512]{2,1,0:T(1,128)S(1)}, s32[2,1,512]{2,1,0:T(1,128)S(1)}, u32[]{:S(2)}, u32[]{:S(2)}) collective-permute-start(s32[2,1,512]{2,1,0:T(1,128)S(1)} %pad_add_fusion), channel_id=1, source_target_pairs={{0,256},{256,0},{1,257},{257,1},{2,258},{258,2},{3,259},{259,3},{4... | collective-permute-start | bytes 12296 | tf_op jit(solution)/shard_map/ppermute | solution.py:385
  21.4 0.1 stack.28.scalars
  21.4 9.7 %all-to-all-done = f32[8,16,1024]{2,1,0:T(8,128)S(1)} async-done(((f32[8,16,1024]{2,1,0:T(8,128)}), f32[8,16,1024]{2,1,0:T(8,128)S(1)}, u32[]{:S(2)}, u32[]{:S(2)}) %all-to-all-start) | async-done | bytes 524320 | tf_op jit(solution)/shard_map/all_to_all | solution.py:403
  31.2 3.1 %collective-permute-start.2 = (f32[4,16,1024]{2,1,0:T(8,128)S(1)}, f32[4,16,1024]{2,1,0:T(8,128)S(1)}, u32[]{:S(2)}, u32[]{:S(2)}) collective-permute-start(f32[4,16,1024]{2,1,0:T(8,128)S(1)} %get-tuple-element.33), channel_id=1, source_target_pairs={{0,16},{16,256},{256,272},{272,0},{1,17},{17,257},{257,273},{273,1... | collective-permute-start | bytes 786440 | tf_op jit(solution)/shard_map/ppermute | solution.py:407
  34.3 3.4 %collective-permute-start.3 = (f32[4,16,1024]{2,1,0:T(8,128)S(1)}, f32[4,16,1024]{2,1,0:T(8,128)S(1)}, u32[]{:S(2)}, u32[]{:S(2)}) collective-permute-start(f32[4,16,1024]{2,1,0:T(8,128)S(1)} %get-tuple-element.32), channel_id=1, source_target_pairs={{0,272},{16,0},{256,16},{272,256},{1,273},{17,1},{257,17},{273,257... | collective-permute-start | bytes 786440 | tf_op jit(solution)/shard_map/ppermute | solution.py:407
  37.7 0.0 copy-done.1
  37.7 0.0 copy-done.3
  37.7 0.0 copy-start.2
  37.7 1.2 %copy-done.2 = f32[1,512,512]{2,1,0:T(8,128)S(1)} copy-done((f32[1,512,512]{2,1,0:T(8,128)S(1)}, f32[1,512,512]{2,1,0:T(8,128)}, u32[]{:S(2)}) %copy-start.2) | copy-done | bytes 1048600
  39.0 2.5 %shard_map.78.total = f32[1024,512]{1,0:T(8,128)S(1)} custom-call(s32[5]{0:T(128)S(1)} %stack.28.scalars, s32[4,4]{1,0:T(4,128)S(1)} %copy-done.3, f32[512,512]{1,0:T(8,128)S(1)} %bitcast.24, f32[512,1024]{1,0:T(8,128)S(1)} %bitcast.22, s32[1,512]{1,0:T(1,128)S(1)} %get-tuple-element.35.columns, s32[1,512]{1,0:T(1,128)S(1)} %get-tuple-element.34.targets), custom_call_target="tpu_custom_call" | custom-call | flops 2000000000 | bytes 5000000 | tf_op jit(solution)/shard_map/pallas_call | solution.py:81
  41.5 0.0 collective-permute-done.1.maps
  41.5 0.0 collective-permute-done.block
  41.5 3.2 %shard_map.79 = (bf16[1024,512]{1,0:T(8,128)(2,1)S(1)}, bf16[1024,512]{1,0:T(8,128)(2,1)S(1)}) custom-call(s32[5]{0:T(128)S(1)} %stack.28.scalars, f32[1024,512]{1,0:T(8,128)S(1)} %shard_map.78.total, f32[512,512]{1,0:T(8,128)} %collective-permute-done.block, s32[2,1,512]{2,1,0:T(1,128)S(1)} %collective-permute-done.1.maps), custom_call_target="tpu_custom_call" | custom-call | flops 2000000000 | bytes 5000000 | tf_op jit(solution)/shard_map/pallas_call | solution.py:94
  44.7 1.7 %shard_map.80 = (f32[8,8,512]{2,1,0:T(8,128)S(1)}, f32[8,8,512]{2,1,0:T(8,128)S(1)}) custom-call(s32[5]{0:T(128)S(1)} %stack.28.scalars, f32[8,2,8,1024]{3,2,1,0:T(8,128)S(1)} %bitcast.14, bf16[1024,512]{1,0:T(8,128)(2,1)S(1)} %get-tuple-element.19.top, bf16[1024,512]{1,0:T(8,128)(2,1)S(1)} %get-tuple-element.20.low), custom_call_target="tpu_custom_call" | custom-call | flops 500000000 | bytes 1000000 | tf_op jit(solution)/shard_map/pallas_call | solution.py:152
  46.4 1.2 %collective-permute-done.2 = f32[4,16,1024]{2,1,0:T(8,128)S(1)} collective-permute-done((f32[4,16,1024]{2,1,0:T(8,128)S(1)}, f32[4,16,1024]{2,1,0:T(8,128)S(1)}, u32[]{:S(2)}, u32[]{:S(2)}) %collective-permute-start.2) | collective-permute-done | bytes 262176 | tf_op jit(solution)/shard_map/ppermute | solution.py:407
  47.6 0.0 collective-permute-done.3
  47.6 1.2 %shard_map.82 = f32[8,16,512]{2,1,0:T(8,128)S(1)} custom-call(s32[5]{0:T(128)S(1)} %stack.28.scalars, f32[8,8,512]{2,1,0:T(8,128)S(1)} %get-tuple-element.22.first, f32[4,2,8,1024]{3,2,1,0:T(8,128)S(1)} %bitcast.15, f32[4,2,8,1024]{3,2,1,0:T(8,128)S(1)} %bitcast.17, bf16[1024,512]{1,0:T(8,128)(2,1)S(1)} %get-tuple-element.19.top, ...), custom_call_target="tpu_custom_call" | custom-call | flops 500000000 | bytes 1000000 | tf_op jit(solution)/shard_map/pallas_call | solution.py:164
  48.8 3.3 %collective-permute-start.4 = (f32[8,16,512]{2,1,0:T(8,128)S(1)}, f32[8,16,512]{2,1,0:T(8,128)S(1)}, u32[]{:S(2)}, u32[]{:S(2)}) collective-permute-start(f32[8,16,512]{2,1,0:T(8,128)S(1)} %shard_map.82), channel_id=1, source_target_pairs={{0,1},{1,0},{2,3},{3,2},{4,5},{5,4},{6,7},{7,6},{8,9},{9,8},{10,11... | collective-permute-start | bytes 786440 | tf_op jit(solution)/shard_map/ppermute | solution.py:416
  52.1 1.2 %shard_map.81 = f32[8,16,512]{2,1,0:T(8,128)S(1)} custom-call(s32[5]{0:T(128)S(1)} %stack.28.scalars, f32[8,8,512]{2,1,0:T(8,128)S(1)} %get-tuple-element.21.first, f32[4,2,8,1024]{3,2,1,0:T(8,128)S(1)} %bitcast.16, f32[4,2,8,1024]{3,2,1,0:T(8,128)S(1)} %bitcast.18, bf16[1024,512]{1,0:T(8,128)(2,1)S(1)} %get-tuple-element.19.top, ...), custom_call_target="tpu_custom_call" | custom-call | flops 500000000 | bytes 1000000 | tf_op jit(solution)/shard_map/pallas_call | solution.py:164
  53.3 0.0 collective-permute-done.4
  53.3 18.4 %all_to_all.15 = f32[8,16,512]{2,1,0:T(8,128)S(1)} all-to-all(f32[8,16,512]{2,1,0:T(8,128)S(1)} %add.24), channel_id=1, replica_groups=mesh['child'=2,'z'=8,'xl'=2,'y'=8,'core'=2] {'y'}, dimensions={0} | all-to-all | bytes 524288 | tf_op jit(solution)/shard_map/all_to_all | solution.py:418
  71.7 0.1 broadcast_in_dim.6
  71.8 18.1 %all_to_all.16.mine = f32[16,16,512]{2,1,0:T(8,128)S(1)} all-to-all(f32[16,16,512]{2,1,0:T(8,128)S(1)} %broadcast_in_dim.6), channel_id=1, replica_groups=mesh['child'=2,'z'=8,'xl'=2,'y'=8,'core'=2] {'child','y'}, dimensions={0} | all-to-all | bytes 1048576 | tf_op jit(solution)/shard_map/all_to_all | solution.py:420
  89.9 5.4 %collective-permute-start.5 = (f32[16,16,512]{2,1,0:T(8,128)S(1)}, f32[16,16,512]{2,1,0:T(8,128)S(1)}, u32[]{:S(2)}, u32[]{:S(2)}) collective-permute-start(f32[16,16,512]{2,1,0:T(8,128)S(1)} %all_to_all.16.mine), channel_id=1, source_target_pairs={{0,1},{1,0},{2,3},{3,2},{4,5},{5,4},{6,7},{7,6},{8,9},{9,8},{10,11... | collective-permute-start | bytes 1572872 | tf_op jit(solution)/shard_map/ppermute | solution.py:423
  95.2 1.5 %collective-permute-done.5.theirs = f32[16,16,512]{2,1,0:T(8,128)S(1)} collective-permute-done((f32[16,16,512]{2,1,0:T(8,128)S(1)}, f32[16,16,512]{2,1,0:T(8,128)S(1)}, u32[]{:S(2)}, u32[]{:S(2)}) %collective-permute-start.5) | collective-permute-done | bytes 524320 | tf_op jit(solution)/shard_map/ppermute | solution.py:423
  96.8 6.2 %shard_map.83 = (f32[256,1024]{1,0:T(8,128)S(1)}, f32[2,128,256]{2,1,0:T(8,128)S(1)}, f32[2,128,128]{2,1,0:T(8,128)S(1)}, f32[2,128,256]{2,1,0:T(8,128)S(1)}) custom-call(s32[5]{0:T(128)S(1)} %stack.28.scalars, f32[16,16,512]{2,1,0:T(8,128)S(1)} %all_to_all.16.mine, f32[16,16,512]{2,1,0:T(8,128)S(1)} %collective-permute-done.5.theirs), custom_call_target="tpu_custom_call" | custom-call | tf_op jit(solution)/shard_map/pallas_call | solution.py:288
  102.9 2.4 %collective-permute-start.6 = (f32[2,128,256]{2,1,0:T(8,128)S(1)}, f32[2,128,256]{2,1,0:T(8,128)S(1)}, u32[]{:S(2)}, u32[]{:S(2)}) collective-permute-start(f32[2,128,256]{2,1,0:T(8,128)S(1)} %get-tuple-element.24.u_head), channel_id=1, source_target_pairs={{0,16},{16,0},{1,17},{17,1},{2,18},{18,2},{3,19},{19,3},{4,20},{20... | collective-permute-start | bytes 786440 | tf_op jit(solution)/shard_map/ppermute | solution.py:426
  105.3 5.0 %shard_map.84 = (f32[136,128]{1,0:T(8,128)S(1)}, f32[2,8,256]{2,1,0:T(8,128)S(1)}, f32[2,8,256]{2,1,0:T(8,128)S(1)}) custom-call(s32[5]{0:T(128)S(1)} %stack.28.scalars, f32[2,128,256]{2,1,0:T(8,128)S(1)} %get-tuple-element.24.u_head, f32[2,128,128]{2,1,0:T(8,128)S(1)} %get-tuple-element.25.x_head, f32[2,128,256]{2,1,0:T(8,128)S(1)} %get-tuple-element.26.rest), custom_call_target="tpu_custom_call" | custom-call | flops 8000000000 | bytes 1000000 | tf_op jit(solution)/shard_map/pallas_call | solution.py:334
  110.3 3.1 %collective-permute-start.7 = (f32[136,128]{1,0:T(8,128)S(1)}, f32[136,128]{1,0:T(8,128)S(1)}, u32[]{:S(2)}, u32[]{:S(2)}) collective-permute-start(f32[136,128]{1,0:T(8,128)S(1)} %get-tuple-element.31), channel_id=1, source_target_pairs={{0,16},{16,0},{1,17},{17,1},{2,18},{18,2},{3,19},{19,3},{4,20},{20... | collective-permute-start | bytes 208904 | tf_op jit(solution)/shard_map/ppermute | solution.py:428
  113.5 0.0 collective-permute-done.6.sib_head
  113.5 1.4 %shard_map.85 = (f32[8,1024]{1,0:T(8,128)}, f32[2,8,128]{2,1,0:T(8,128)S(1)}) custom-call(s32[5]{0:T(128)S(1)} %stack.28.scalars, f32[256,1024]{1,0:T(8,128)S(1)} %get-tuple-element.23.window, f32[2,8,256]{2,1,0:T(8,128)S(1)} %get-tuple-element.27.x_own, f32[2,8,256]{2,1,0:T(8,128)S(1)} %get-tuple-element.28.u_own, ...), custom_call_target="tpu_custom_call" | custom-call | flops 1000000000 | bytes 1000000 | tf_op jit(solution)/shard_map/pallas_call | solution.py:429
  114.9 0.5 collective-permute-done.7.packed
  115.4 1.0 shard_map.86
  (4 shorter events, 0.1 us)
Async XLA Ops:
  0.6 0.8 copy-start
  1.5 36.2 %copy-start.1 = (f32[1,512,1024]{2,1,0:T(8,128)S(1)}, f32[1,512,1024]{2,1,0:T(8,128)}, u32[]{:S(2)}) copy-start(f32[1,512,1024]{2,1,0:T(8,128)} %param.7) | copy-start | bytes 6291460
  1.5 36.2 %copy-start.3 = (s32[4,4]{1,0:T(4,128)S(1)}, s32[4,4]{1,0:T(4,128)}, u32[]{:S(2)}) copy-start(s32[4,4]{1,0:T(4,128)} %pattern.1) | copy-start | bytes 196
  2.3 28.8 %all-to-all-start = ((f32[8,16,1024]{2,1,0:T(8,128)}), f32[8,16,1024]{2,1,0:T(8,128)S(1)}, u32[]{:S(2)}, u32[]{:S(2)}) async-start(f32[8,16,1024]{2,1,0:T(8,128)} %shard_map.77), calls=%async_computation | async-start | bytes 1048576 | tf_op jit(solution)/shard_map/all_to_all | solution.py:403
  13.2 28.3 %collective-permute-start = (f32[512,512]{1,0:T(8,128)}, f32[512,512]{1,0:T(8,128)}, u32[]{:S(2)}, u32[]{:S(2)}) collective-permute-start(f32[512,512]{1,0:T(8,128)} %bitcast.23), channel_id=1, source_target_pairs={{0,256},{256,0},{1,257},{257,1},{2,258},{258,2},{3,259},{259,3},{4... | collective-permute-start | bytes 3145736 | tf_op jit(solution)/shard_map/ppermute | solution.py:381
  18.6 22.9 %collective-permute-start.1 = (s32[2,1,512]{2,1,0:T(1,128)S(1)}, s32[2,1,512]{2,1,0:T(1,128)S(1)}, u32[]{:S(2)}, u32[]{:S(2)}) collective-permute-start(s32[2,1,512]{2,1,0:T(1,128)S(1)} %pad_add_fusion), channel_id=1, source_target_pairs={{0,256},{256,0},{1,257},{257,1},{2,258},{258,2},{3,259},{259,3},{4... | collective-permute-start | bytes 12296 | tf_op jit(solution)/shard_map/ppermute | solution.py:385
  31.2 16.4 %collective-permute-start.2 = (f32[4,16,1024]{2,1,0:T(8,128)S(1)}, f32[4,16,1024]{2,1,0:T(8,128)S(1)}, u32[]{:S(2)}, u32[]{:S(2)}) collective-permute-start(f32[4,16,1024]{2,1,0:T(8,128)S(1)} %get-tuple-element.33), channel_id=1, source_target_pairs={{0,16},{16,256},{256,272},{272,0},{1,17},{17,257},{257,273},{273,1... | collective-permute-start | bytes 786440 | tf_op jit(solution)/shard_map/ppermute | solution.py:407
  34.3 13.3 %collective-permute-start.3 = (f32[4,16,1024]{2,1,0:T(8,128)S(1)}, f32[4,16,1024]{2,1,0:T(8,128)S(1)}, u32[]{:S(2)}, u32[]{:S(2)}) collective-permute-start(f32[4,16,1024]{2,1,0:T(8,128)S(1)} %get-tuple-element.32), channel_id=1, source_target_pairs={{0,272},{16,0},{256,16},{272,256},{1,273},{17,1},{257,17},{273,257... | collective-permute-start | bytes 786440 | tf_op jit(solution)/shard_map/ppermute | solution.py:407
  37.7 1.2 %copy-start.2 = (f32[1,512,512]{2,1,0:T(8,128)S(1)}, f32[1,512,512]{2,1,0:T(8,128)}, u32[]{:S(2)}) copy-start(f32[1,512,512]{2,1,0:T(8,128)} %param.6) | copy-start | bytes 3145732
  48.8 4.5 %collective-permute-start.4 = (f32[8,16,512]{2,1,0:T(8,128)S(1)}, f32[8,16,512]{2,1,0:T(8,128)S(1)}, u32[]{:S(2)}, u32[]{:S(2)}) collective-permute-start(f32[8,16,512]{2,1,0:T(8,128)S(1)} %shard_map.82), channel_id=1, source_target_pairs={{0,1},{1,0},{2,3},{3,2},{4,5},{5,4},{6,7},{7,6},{8,9},{9,8},{10,11... | collective-permute-start | bytes 786440 | tf_op jit(solution)/shard_map/ppermute | solution.py:416
  89.9 6.9 %collective-permute-start.5 = (f32[16,16,512]{2,1,0:T(8,128)S(1)}, f32[16,16,512]{2,1,0:T(8,128)S(1)}, u32[]{:S(2)}, u32[]{:S(2)}) collective-permute-start(f32[16,16,512]{2,1,0:T(8,128)S(1)} %all_to_all.16.mine), channel_id=1, source_target_pairs={{0,1},{1,0},{2,3},{3,2},{4,5},{5,4},{6,7},{7,6},{8,9},{9,8},{10,11... | collective-permute-start | bytes 1572872 | tf_op jit(solution)/shard_map/ppermute | solution.py:423
  102.9 10.5 %collective-permute-start.6 = (f32[2,128,256]{2,1,0:T(8,128)S(1)}, f32[2,128,256]{2,1,0:T(8,128)S(1)}, u32[]{:S(2)}, u32[]{:S(2)}) collective-permute-start(f32[2,128,256]{2,1,0:T(8,128)S(1)} %get-tuple-element.24.u_head), channel_id=1, source_target_pairs={{0,16},{16,0},{1,17},{17,1},{2,18},{18,2},{3,19},{19,3},{4,20},{20... | collective-permute-start | bytes 786440 | tf_op jit(solution)/shard_map/ppermute | solution.py:426
  110.3 5.1 %collective-permute-start.7 = (f32[136,128]{1,0:T(8,128)S(1)}, f32[136,128]{1,0:T(8,128)S(1)}, u32[]{:S(2)}, u32[]{:S(2)}) collective-permute-start(f32[136,128]{1,0:T(8,128)S(1)} %get-tuple-element.31), channel_id=1, source_target_pairs={{0,16},{16,0},{1,17},{17,1},{2,18},{18,2},{3,19},{19,3},{4,20},{20... | collective-permute-start | bytes 208904 | tf_op jit(solution)/shard_map/ppermute | solution.py:428

commit v10 on v8

--- a/solution.py
+++ b/solution.py
@@ -103,30 +103,34 @@
 
 
 def apply_kernel(scalars, own, ahead, behind, top, low, give, keep):
-    core = scalars[2]
-    count, width, half_rows = give.shape
-    depth = top.shape[0]
-    rows = count * width
-    ordered = jnp.concatenate(
-        [piece[:, side].reshape(-1, depth) for side in range(2) for piece in (own, ahead, behind)]
-    )
-    high_lines, low_lines = two_parts(ordered)
-    for tile in range(half_rows // BT):
-        lanes = slice(tile * BT, (tile + 1) * BT)
-        out = (
-            dot(high_lines, top[:, lanes], NN)
-            + dot(low_lines, top[:, lanes], NN)
-            + dot(high_lines, low[:, lanes], NN)
+    depth, half_rows = top.shape
+    count, width, _ = give.shape
+    rows = count * width // 2
+
+    def body(core):
+        lines = jnp.concatenate(
+            [
+                piece[:, side].reshape(-1, depth)
+                for side in (1 - core, core)
+                for piece in (own, ahead, behind)
+            ]
         )
-        first, second = out[:rows], out[rows:]
-        for target, value in (
-            (give, jnp.where(core == 0, second, first)),
-            (keep, jnp.where(core == 0, first, second)),
-        ):
-            for piece in range(2):
-                there = slice(piece * width // 2, (piece + 1) * width // 2)
-                part = value[piece * rows // 2 : (piece + 1) * rows // 2]
+        high_lines, low_lines = two_parts(lines)
+        for tile in range(half_rows // BT):
+            lanes = slice(tile * BT, (tile + 1) * BT)
+            out = (
+                dot(high_lines, top[:, lanes], NN)
+                + dot(low_lines, top[:, lanes], NN)
+                + dot(high_lines, low[:, lanes], NN)
+            )
+            for block in range(4):
+                target = (give, keep)[block // 2]
+                there = slice(block % 2 * width // 2, (block % 2 + 1) * width // 2)
+                part = out[block * rows : (block + 1) * rows]
                 target[:, there, lanes] = part.reshape(count, width // 2, BT)
+
+    for value in range(2):
+        pl.when(scalars[2] == value)(lambda value=value: body(value))
 
 
 def apply_operator(scalars, own, ahead, behind, top, low):

time: 116 us -> 117 us (level)
  no operation moved by 1% of the time
where the time goes in v10:
time: 117 us; the launch traced here: 116 us
  starting transfers between devices  36.9 us (32%)
  blocking collectives  36.6 us (31%)
  Pallas kernels  21.7 us (19%)
  waiting for transfers between devices  15.8 us (14%)
  local copies, waits for them, and re-layouts  2.23 us (2%)
  between operations  1.48 us (1%)
    all_to_all x1, blocking collectives, local(): lax.all_to_all(jnp.broadcast_to(samples, (groups,) + samples.shape), ('ch...  18.9 us
    all_to_all x1, blocking collectives, local(): terms = lax.all_to_all(parts, 'y', 0, 0)  17.7 us
    all_to_all x1, starting transfers between devices, local(): own = lax.all_to_all(copies, 'z', 0, 0)  10.9 us
    all_to_all x1, waiting for transfers between devices, local(): own = lax.all_to_all(copies, 'z', 0, 0)  9.71 us
    ppermute x2, starting transfers between devices, local(): lax.ppermute(piece, ('child', 'xl'), [(i, (i + step) % ring) for i in ran...  6.49 us
    pallas_call x1, Pallas kernels, factor_head(): pl.pallas_call(head_kernel, in_specs=[SMEM, VMEM, VMEM], out_specs=[VMEM]...  6.17 us
    pallas_call x1, Pallas kernels, factor_tail(): pl.pallas_call(tail_kernel, in_specs=[SMEM] + [VMEM] * 3, out_specs=[VMEM...  5.04 us
    ppermute x1, starting transfers between devices, local(): theirs = lax.ppermute(mine, 'core', SWAP)  4.86 us
  transfers between devices with their start and end apart: 9, of which 5 were waited for; matrix products, arithmetic and copies ran while one was open for 1% of the time, Pallas kernels for 11%

profile of v10, /device:TPU:1, one launch (start us, length us, event | category | flops | bytes accessed | tf_op | source)
XLA Modules:
  0.0 115.5 jit_solution(6746824006506053838)
XLA Ops:
  0.6 0.0 copy-start
  0.6 0.8 copy-done
  1.5 0.0 copy-start.1
  1.5 0.0 copy-start.3
  1.5 0.9 shard_map.77
  2.3 10.9 %all-to-all-start = ((f32[8,16,1024]{2,1,0:T(8,128)}), f32[8,16,1024]{2,1,0:T(8,128)S(1)}, u32[]{:S(2)}, u32[]{:S(2)}) async-start(f32[8,16,1024]{2,1,0:T(8,128)} %shard_map.77), calls=%async_computation | async-start | bytes 1048576 | tf_op jit(solution)/shard_map/all_to_all | solution.py:379
  13.2 4.6 %collective-permute-start.2 = (f32[512,512]{1,0:T(8,128)}, f32[512,512]{1,0:T(8,128)}, u32[]{:S(2)}, u32[]{:S(2)}) collective-permute-start(f32[512,512]{1,0:T(8,128)} %bitcast.19), channel_id=1, source_target_pairs={{0,256},{256,0},{1,257},{257,1},{2,258},{258,2},{3,259},{259,3},{4... | collective-permute-start | bytes 3145736 | tf_op jit(solution)/shard_map/ppermute | solution.py:357
  17.9 0.7 dynamic-slice_subtract_fusion
  18.6 2.1 %collective-permute-start.3 = (s32[2,1,512]{2,1,0:T(1,128)S(1)}, s32[2,1,512]{2,1,0:T(1,128)S(1)}, u32[]{:S(2)}, u32[]{:S(2)}) collective-permute-start(s32[2,1,512]{2,1,0:T(1,128)S(1)} %pad_add_fusion), channel_id=1, source_target_pairs={{0,256},{256,0},{1,257},{257,1},{2,258},{258,2},{3,259},{259,3},{4... | collective-permute-start | bytes 12296 | tf_op jit(solution)/shard_map/ppermute | solution.py:361
  21.4 0.1 stack.28.scalars
  21.4 9.7 %all-to-all-done = f32[8,16,1024]{2,1,0:T(8,128)S(1)} async-done(((f32[8,16,1024]{2,1,0:T(8,128)}), f32[8,16,1024]{2,1,0:T(8,128)S(1)}, u32[]{:S(2)}, u32[]{:S(2)}) %all-to-all-start) | async-done | bytes 524320 | tf_op jit(solution)/shard_map/all_to_all | solution.py:379
  31.2 3.1 %collective-permute-start = (f32[4,16,1024]{2,1,0:T(8,128)S(1)}, f32[4,16,1024]{2,1,0:T(8,128)S(1)}, u32[]{:S(2)}, u32[]{:S(2)}) collective-permute-start(f32[4,16,1024]{2,1,0:T(8,128)S(1)} %get-tuple-element.33), channel_id=1, source_target_pairs={{0,16},{16,256},{256,272},{272,0},{1,17},{17,257},{257,273},{273,1... | collective-permute-start | bytes 786440 | tf_op jit(solution)/shard_map/ppermute | solution.py:383
  34.3 3.4 %collective-permute-start.1 = (f32[4,16,1024]{2,1,0:T(8,128)S(1)}, f32[4,16,1024]{2,1,0:T(8,128)S(1)}, u32[]{:S(2)}, u32[]{:S(2)}) collective-permute-start(f32[4,16,1024]{2,1,0:T(8,128)S(1)} %get-tuple-element.32), channel_id=1, source_target_pairs={{0,272},{16,0},{256,16},{272,256},{1,273},{17,1},{257,17},{273,257... | collective-permute-start | bytes 786440 | tf_op jit(solution)/shard_map/ppermute | solution.py:383
  37.7 0.0 copy-done.1
  37.7 0.0 copy-done.3
  37.7 0.0 copy-start.2
  37.7 1.2 %copy-done.2 = f32[1,512,512]{2,1,0:T(8,128)S(1)} copy-done((f32[1,512,512]{2,1,0:T(8,128)S(1)}, f32[1,512,512]{2,1,0:T(8,128)}, u32[]{:S(2)}) %copy-start.2) | copy-done | bytes 1048600
  39.0 2.5 %shard_map.78.total = f32[1024,512]{1,0:T(8,128)S(1)} custom-call(s32[5]{0:T(128)S(1)} %stack.28.scalars, s32[4,4]{1,0:T(4,128)S(1)} %copy-done.3, f32[512,512]{1,0:T(8,128)S(1)} %bitcast.20, f32[512,1024]{1,0:T(8,128)S(1)} %bitcast.18, s32[1,512]{1,0:T(1,128)S(1)} %get-tuple-element.35.columns, s32[1,512]{1,0:T(1,128)S(1)} %get-tuple-element.34.targets), custom_call_target="tpu_custom_call" | custom-call | flops 2000000000 | bytes 5000000 | tf_op jit(solution)/shard_map/pallas_call | solution.py:79
  41.5 0.0 collective-permute-done.3.maps
  41.5 0.0 collective-permute-done.2.block
  41.5 3.2 %shard_map.79 = (bf16[1024,512]{1,0:T(8,128)(2,1)S(1)}, bf16[1024,512]{1,0:T(8,128)(2,1)S(1)}) custom-call(s32[5]{0:T(128)S(1)} %stack.28.scalars, f32[1024,512]{1,0:T(8,128)S(1)} %shard_map.78.total, f32[512,512]{1,0:T(8,128)} %collective-permute-done.2.block, s32[2,1,512]{2,1,0:T(1,128)S(1)} %collective-permute-done.3.maps), custom_call_target="tpu_custom_call" | custom-call | flops 2000000000 | bytes 5000000 | tf_op jit(solution)/shard_map/pallas_call | solution.py:92
  44.7 2.9 %collective-permute-done = f32[4,16,1024]{2,1,0:T(8,128)S(1)} collective-permute-done((f32[4,16,1024]{2,1,0:T(8,128)S(1)}, f32[4,16,1024]{2,1,0:T(8,128)S(1)}, u32[]{:S(2)}, u32[]{:S(2)}) %collective-permute-start) | collective-permute-done | bytes 262176 | tf_op jit(solution)/shard_map/ppermute | solution.py:383
  47.6 0.0 collective-permute-done.1
  47.6 1.5 %shard_map.80 = (f32[8,16,512]{2,1,0:T(8,128)S(1)}, f32[8,16,512]{2,1,0:T(8,128)S(1)}) custom-call(s32[5]{0:T(128)S(1)} %stack.28.scalars, f32[8,2,8,1024]{3,2,1,0:T(8,128)S(1)} %bitcast.14, f32[4,2,8,1024]{3,2,1,0:T(8,128)S(1)} %bitcast.21, f32[4,2,8,1024]{3,2,1,0:T(8,128)S(1)} %bitcast.22, bf16[1024,512]{1,0:T(8,128)(2,1)S(1)} %get-tuple-element.19.top, ...), custom_call_target="tpu_custom_call" | custom-call | flops 1000000000 | bytes 6000000 | tf_op jit(solution)/shard_map/pallas_call | solution.py:140
  49.1 2.5 %collective-permute-start.4 = (f32[8,16,512]{2,1,0:T(8,128)S(1)}, f32[8,16,512]{2,1,0:T(8,128)S(1)}, u32[]{:S(2)}, u32[]{:S(2)}) collective-permute-start(f32[8,16,512]{2,1,0:T(8,128)S(1)} %get-tuple-element.22), channel_id=1, source_target_pairs={{0,1},{1,0},{2,3},{3,2},{4,5},{5,4},{6,7},{7,6},{8,9},{9,8},{10,11... | collective-permute-start | bytes 786440 | tf_op jit(solution)/shard_map/ppermute | solution.py:391
  51.6 1.1 collective-permute-done.4
  52.8 17.7 %all_to_all.15 = f32[8,16,512]{2,1,0:T(8,128)S(1)} all-to-all(f32[8,16,512]{2,1,0:T(8,128)S(1)} %add.24), channel_id=1, replica_groups=mesh['child'=2,'z'=8,'xl'=2,'y'=8,'core'=2] {'y'}, dimensions={0} | all-to-all | bytes 524288 | tf_op jit(solution)/shard_map/all_to_all | solution.py:392
  70.5 0.1 broadcast_in_dim.6
  70.6 18.9 %all_to_all.16.mine = f32[16,16,512]{2,1,0:T(8,128)S(1)} all-to-all(f32[16,16,512]{2,1,0:T(8,128)S(1)} %broadcast_in_dim.6), channel_id=1, replica_groups=mesh['child'=2,'z'=8,'xl'=2,'y'=8,'core'=2] {'child','y'}, dimensions={0} | all-to-all | bytes 1048576 | tf_op jit(solution)/shard_map/all_to_all | solution.py:394
  89.4 4.9 %collective-permute-start.5 = (f32[16,16,512]{2,1,0:T(8,128)S(1)}, f32[16,16,512]{2,1,0:T(8,128)S(1)}, u32[]{:S(2)}, u32[]{:S(2)}) collective-permute-start(f32[16,16,512]{2,1,0:T(8,128)S(1)} %all_to_all.16.mine), channel_id=1, source_target_pairs={{0,1},{1,0},{2,3},{3,2},{4,5},{5,4},{6,7},{7,6},{8,9},{9,8},{10,11... | collective-permute-start | bytes 1572872 | tf_op jit(solution)/shard_map/ppermute | solution.py:397
  94.3 1.5 %collective-permute-done.5.theirs = f32[16,16,512]{2,1,0:T(8,128)S(1)} collective-permute-done((f32[16,16,512]{2,1,0:T(8,128)S(1)}, f32[16,16,512]{2,1,0:T(8,128)S(1)}, u32[]{:S(2)}, u32[]{:S(2)}) %collective-permute-start.5) | collective-permute-done | bytes 524320 | tf_op jit(solution)/shard_map/ppermute | solution.py:397
  95.8 6.2 %shard_map.81 = (f32[256,1024]{1,0:T(8,128)S(1)}, f32[2,128,256]{2,1,0:T(8,128)S(1)}, f32[2,128,128]{2,1,0:T(8,128)S(1)}, f32[2,128,256]{2,1,0:T(8,128)S(1)}) custom-call(s32[5]{0:T(128)S(1)} %stack.28.scalars, f32[16,16,512]{2,1,0:T(8,128)S(1)} %all_to_all.16.mine, f32[16,16,512]{2,1,0:T(8,128)S(1)} %collective-permute-done.5.theirs), custom_call_target="tpu_custom_call" | custom-call | tf_op jit(solution)/shard_map/pallas_call | solution.py:264
  102.0 2.4 %collective-permute-start.6 = (f32[2,128,256]{2,1,0:T(8,128)S(1)}, f32[2,128,256]{2,1,0:T(8,128)S(1)}, u32[]{:S(2)}, u32[]{:S(2)}) collective-permute-start(f32[2,128,256]{2,1,0:T(8,128)S(1)} %get-tuple-element.24.u_head), channel_id=1, source_target_pairs={{0,16},{16,0},{1,17},{17,1},{2,18},{18,2},{3,19},{19,3},{4,20},{20... | collective-permute-start | bytes 786440 | tf_op jit(solution)/shard_map/ppermute | solution.py:400
  104.4 5.0 %shard_map.82 = (f32[136,128]{1,0:T(8,128)S(1)}, f32[2,8,256]{2,1,0:T(8,128)S(1)}, f32[2,8,256]{2,1,0:T(8,128)S(1)}) custom-call(s32[5]{0:T(128)S(1)} %stack.28.scalars, f32[2,128,256]{2,1,0:T(8,128)S(1)} %get-tuple-element.24.u_head, f32[2,128,128]{2,1,0:T(8,128)S(1)} %get-tuple-element.25.x_head, f32[2,128,256]{2,1,0:T(8,128)S(1)} %get-tuple-element.26.rest), custom_call_target="tpu_custom_call" | custom-call | flops 8000000000 | bytes 1000000 | tf_op jit(solution)/shard_map/pallas_call | solution.py:310
  109.5 3.1 %collective-permute-start.7 = (f32[136,128]{1,0:T(8,128)S(1)}, f32[136,128]{1,0:T(8,128)S(1)}, u32[]{:S(2)}, u32[]{:S(2)}) collective-permute-start(f32[136,128]{1,0:T(8,128)S(1)} %get-tuple-element.31), channel_id=1, source_target_pairs={{0,16},{16,0},{1,17},{17,1},{2,18},{18,2},{3,19},{19,3},{4,20},{20... | collective-permute-start | bytes 208904 | tf_op jit(solution)/shard_map/ppermute | solution.py:402
  112.5 0.0 collective-permute-done.6.sib_head
  112.5 1.4 %shard_map.83 = (f32[8,1024]{1,0:T(8,128)}, f32[2,8,128]{2,1,0:T(8,128)S(1)}) custom-call(s32[5]{0:T(128)S(1)} %stack.28.scalars, f32[256,1024]{1,0:T(8,128)S(1)} %get-tuple-element.23.window, f32[2,8,256]{2,1,0:T(8,128)S(1)} %get-tuple-element.27.x_own, f32[2,8,256]{2,1,0:T(8,128)S(1)} %get-tuple-element.28.u_own, ...), custom_call_target="tpu_custom_call" | custom-call | flops 1000000000 | bytes 1000000 | tf_op jit(solution)/shard_map/pallas_call | solution.py:403
  114.0 0.5 collective-permute-done.7.packed
  114.5 1.0 shard_map.84
  (4 shorter events, 0.1 us)
Async XLA Ops:
  0.6 0.8 copy-start
  1.5 36.2 %copy-start.1 = (f32[1,512,1024]{2,1,0:T(8,128)S(1)}, f32[1,512,1024]{2,1,0:T(8,128)}, u32[]{:S(2)}) copy-start(f32[1,512,1024]{2,1,0:T(8,128)} %param.7) | copy-start | bytes 6291460
  1.5 36.2 %copy-start.3 = (s32[4,4]{1,0:T(4,128)S(1)}, s32[4,4]{1,0:T(4,128)}, u32[]{:S(2)}) copy-start(s32[4,4]{1,0:T(4,128)} %pattern.1) | copy-start | bytes 196
  2.3 28.8 %all-to-all-start = ((f32[8,16,1024]{2,1,0:T(8,128)}), f32[8,16,1024]{2,1,0:T(8,128)S(1)}, u32[]{:S(2)}, u32[]{:S(2)}) async-start(f32[8,16,1024]{2,1,0:T(8,128)} %shard_map.77), calls=%async_computation | async-start | bytes 1048576 | tf_op jit(solution)/shard_map/all_to_all | solution.py:379
  13.2 28.3 %collective-permute-start.2 = (f32[512,512]{1,0:T(8,128)}, f32[512,512]{1,0:T(8,128)}, u32[]{:S(2)}, u32[]{:S(2)}) collective-permute-start(f32[512,512]{1,0:T(8,128)} %bitcast.19), channel_id=1, source_target_pairs={{0,256},{256,0},{1,257},{257,1},{2,258},{258,2},{3,259},{259,3},{4... | collective-permute-start | bytes 3145736 | tf_op jit(solution)/shard_map/ppermute | solution.py:357
  18.6 22.9 %collective-permute-start.3 = (s32[2,1,512]{2,1,0:T(1,128)S(1)}, s32[2,1,512]{2,1,0:T(1,128)S(1)}, u32[]{:S(2)}, u32[]{:S(2)}) collective-permute-start(s32[2,1,512]{2,1,0:T(1,128)S(1)} %pad_add_fusion), channel_id=1, source_target_pairs={{0,256},{256,0},{1,257},{257,1},{2,258},{258,2},{3,259},{259,3},{4... | collective-permute-start | bytes 12296 | tf_op jit(solution)/shard_map/ppermute | solution.py:361
  31.2 16.4 %collective-permute-start = (f32[4,16,1024]{2,1,0:T(8,128)S(1)}, f32[4,16,1024]{2,1,0:T(8,128)S(1)}, u32[]{:S(2)}, u32[]{:S(2)}) collective-permute-start(f32[4,16,1024]{2,1,0:T(8,128)S(1)} %get-tuple-element.33), channel_id=1, source_target_pairs={{0,16},{16,256},{256,272},{272,0},{1,17},{17,257},{257,273},{273,1... | collective-permute-start | bytes 786440 | tf_op jit(solution)/shard_map/ppermute | solution.py:383
  34.3 13.3 %collective-permute-start.1 = (f32[4,16,1024]{2,1,0:T(8,128)S(1)}, f32[4,16,1024]{2,1,0:T(8,128)S(1)}, u32[]{:S(2)}, u32[]{:S(2)}) collective-permute-start(f32[4,16,1024]{2,1,0:T(8,128)S(1)} %get-tuple-element.32), channel_id=1, source_target_pairs={{0,272},{16,0},{256,16},{272,256},{1,273},{17,1},{257,17},{273,257... | collective-permute-start | bytes 786440 | tf_op jit(solution)/shard_map/ppermute | solution.py:383
  37.7 1.2 %copy-start.2 = (f32[1,512,512]{2,1,0:T(8,128)S(1)}, f32[1,512,512]{2,1,0:T(8,128)}, u32[]{:S(2)}) copy-start(f32[1,512,512]{2,1,0:T(8,128)} %param.6) | copy-start | bytes 3145732
  49.1 3.6 %collective-permute-start.4 = (f32[8,16,512]{2,1,0:T(8,128)S(1)}, f32[8,16,512]{2,1,0:T(8,128)S(1)}, u32[]{:S(2)}, u32[]{:S(2)}) collective-permute-start(f32[8,16,512]{2,1,0:T(8,128)S(1)} %get-tuple-element.22), channel_id=1, source_target_pairs={{0,1},{1,0},{2,3},{3,2},{4,5},{5,4},{6,7},{7,6},{8,9},{9,8},{10,11... | collective-permute-start | bytes 786440 | tf_op jit(solution)/shard_map/ppermute | solution.py:391
  89.4 6.4 %collective-permute-start.5 = (f32[16,16,512]{2,1,0:T(8,128)S(1)}, f32[16,16,512]{2,1,0:T(8,128)S(1)}, u32[]{:S(2)}, u32[]{:S(2)}) collective-permute-start(f32[16,16,512]{2,1,0:T(8,128)S(1)} %all_to_all.16.mine), channel_id=1, source_target_pairs={{0,1},{1,0},{2,3},{3,2},{4,5},{5,4},{6,7},{7,6},{8,9},{9,8},{10,11... | collective-permute-start | bytes 1572872 | tf_op jit(solution)/shard_map/ppermute | solution.py:397
  102.0 10.5 %collective-permute-start.6 = (f32[2,128,256]{2,1,0:T(8,128)S(1)}, f32[2,128,256]{2,1,0:T(8,128)S(1)}, u32[]{:S(2)}, u32[]{:S(2)}) collective-permute-start(f32[2,128,256]{2,1,0:T(8,128)S(1)} %get-tuple-element.24.u_head), channel_id=1, source_target_pairs={{0,16},{16,0},{1,17},{17,1},{2,18},{18,2},{3,19},{19,3},{4,20},{20... | collective-permute-start | bytes 786440 | tf_op jit(solution)/shard_map/ppermute | solution.py:400
  109.5 5.1 %collective-permute-start.7 = (f32[136,128]{1,0:T(8,128)S(1)}, f32[136,128]{1,0:T(8,128)S(1)}, u32[]{:S(2)}, u32[]{:S(2)}) collective-permute-start(f32[136,128]{1,0:T(8,128)S(1)} %get-tuple-element.31), channel_id=1, source_target_pairs={{0,16},{16,0},{1,17},{17,1},{2,18},{18,2},{3,19},{19,3},{4,20},{20... | collective-permute-start | bytes 208904 | tf_op jit(solution)/shard_map/ppermute | solution.py:402

commit v11 on v8

--- a/solution.py
+++ b/solution.py
@@ -102,13 +102,13 @@
     )(scalars, total, block, maps)
 
 
-def apply_kernel(scalars, own, ahead, behind, top, low, give, keep):
+def apply_kernel(scalars, own, other, top, low, give, keep):
     core = scalars[2]
     count, width, half_rows = give.shape
     depth = top.shape[0]
     rows = count * width
     ordered = jnp.concatenate(
-        [piece[:, side].reshape(-1, depth) for side in range(2) for piece in (own, ahead, behind)]
+        [piece[:, side].reshape(-1, depth) for side in range(2) for piece in (own, other)]
     )
     high_lines, low_lines = two_parts(ordered)
     for tile in range(half_rows // BT):
@@ -129,13 +129,13 @@
                 target[:, there, lanes] = part.reshape(count, width // 2, BT)
 
 
-def apply_operator(scalars, own, ahead, behind, top, low):
+def apply_operator(scalars, own, other, top, low):
     count, width, depth = own.shape
     half_rows = top.shape[1]
-    lines = [v.reshape(v.shape[0], 2, width // 2, depth) for v in (own, ahead, behind)]
+    lines = [v.reshape(v.shape[0], 2, width // 2, depth) for v in (own, other)]
     return pl.pallas_call(
         apply_kernel,
-        in_specs=[SMEM] + [VMEM] * 5,
+        in_specs=[SMEM] + [VMEM] * 4,
         out_specs=[VMEM, VMEM],
         out_shape=[shape(count, width, half_rows)] * 2,
         compiler_params=PARAMS,
@@ -374,16 +374,12 @@
     )(omega.T)
     own = lax.all_to_all(copies, "z", 0, 0)
     total = own_operator(scalars, pattern, contrib[0], assembled[0], columns, targets)
-    ring = lax.axis_size("child") * lax.axis_size("xl")
-    other = [
-        lax.ppermute(piece, ("child", "xl"), [(i, (i + step) % ring) for i in range(ring)])
-        for piece, step in ((own[: z_count // 2], 1), (own[z_count // 2 :], -1))
-    ]
+    other = lax.ppermute(own, "xl", SWAP)
 
     sibling_block, sibling_maps = lax.optimization_barrier((sibling_block, sibling_maps))
     top, low = whole_operator(scalars, total, sibling_block, sibling_maps)
 
-    give, keep = apply_operator(scalars, own, *other, top, low)
+    give, keep = apply_operator(scalars, own, other, top, low)
     parts = keep + lax.ppermute(give, "core", SWAP)
     terms = lax.all_to_all(parts, "y", 0, 0)
     samples = jnp.sum(terms, axis=0)

time: 116 us -> 124 us (1.069)
  waiting for transfers between devices: 15.8 us -> 21.9 us
  local copies, waits for them, and re-layouts: 2.23 us -> 4.46 us
    ppermute x1, waiting for transfers between devices: 0.01 us -> 5.41 us  [local(): sibling_maps = lax.ppermute(maps, 'child', SWAP)]
    all_to_all x1, waiting for transfers between devices: 9.71 us -> 13.3 us  [local(): own = lax.all_to_all(copies, 'z', 0, 0)]
    ppermute x2 -> x1, starting transfers between devices: 6.49 us -> 3.11 us  [local(): other = lax.ppermute(own, 'xl', SWAP)]
    ppermute x2 -> x1, waiting for transfers between devices: 2.9 us -> 0.01 us  [local(): other = lax.ppermute(own, 'xl', SWAP)]
    unnamed x8, local copies, waits for them, and re-layouts: 2.06 us -> 4.33 us
    ppermute x1, starting transfers between devices: 2.12 us -> 4.35 us  [local(): sibling_maps = lax.ppermute(maps, 'child', SWAP)]
    ppermute x1, starting transfers between devices: 2.47 us -> 4.07 us  [local(): parts = keep + lax.ppermute(give, 'core', SWAP)]
  transfers between devices with their start and end apart: 9 -> 8, of which waited for: 5 -> 5; matrix products, arithmetic and copies ran while one was open for 1% -> 1% of each run, Pallas kernels for 11% -> 9%
where the time goes in v11:
time: 124 us; the launch traced here: 123 us
  starting transfers between devices  37.2 us (30%)
  blocking collectives  36.6 us (30%)
  waiting for transfers between devices  21.9 us (18%)
  Pallas kernels  21.1 us (17%)
  local copies, waits for them, and re-layouts  4.46 us (4%)
  between operations  1.44 us (1%)
    all_to_all x1, blocking collectives, local(): lax.all_to_all(jnp.broadcast_to(samples, (groups,) + samples.shape), ('ch...  18.9 us
    all_to_all x1, blocking collectives, local(): terms = lax.all_to_all(parts, 'y', 0, 0)  17.7 us
    all_to_all x1, waiting for transfers between devices, local(): own = lax.all_to_all(copies, 'z', 0, 0)  13.3 us
    all_to_all x1, starting transfers between devices, local(): own = lax.all_to_all(copies, 'z', 0, 0)  10.9 us
    pallas_call x1, Pallas kernels, factor_head(): pl.pallas_call(head_kernel, in_specs=[SMEM, VMEM, VMEM], out_specs=[VMEM]...  6.17 us
    ppermute x1, waiting for transfers between devices, local(): sibling_maps = lax.ppermute(maps, 'child', SWAP)  5.41 us
    pallas_call x1, Pallas kernels, factor_tail(): pl.pallas_call(tail_kernel, in_specs=[SMEM] + [VMEM] * 3, out_specs=[VMEM...  5.04 us
    ppermute x1, starting transfers between devices, local(): theirs = lax.ppermute(mine, 'core', SWAP)  4.86 us
  transfers between devices with their start and end apart: 8, of which 5 were waited for; matrix products, arithmetic and copies ran while one was open for 1% of the time, Pallas kernels for 9%

profile of v11, /device:TPU:1, one launch (start us, length us, event | category | flops | bytes accessed | tf_op | source)
XLA Modules:
  0.0 123.5 jit_solution(16695712481541907386)
XLA Ops:
  0.6 0.0 copy-start
  0.6 0.8 copy-done
  1.5 0.8 shard_map.77
  2.3 10.9 %all-to-all-start = ((f32[8,16,1024]{2,1,0:T(8,128)}), f32[8,16,1024]{2,1,0:T(8,128)S(1)}, u32[]{:S(2)}, u32[]{:S(2)}) async-start(f32[8,16,1024]{2,1,0:T(8,128)} %shard_map.77), calls=%async_computation | async-start | bytes 1048576 | tf_op jit(solution)/shard_map/all_to_all | solution.py:375
  13.2 4.6 %collective-permute-start.1 = (f32[512,512]{1,0:T(8,128)}, f32[512,512]{1,0:T(8,128)S(1)}, u32[]{:S(2)}, u32[]{:S(2)}) collective-permute-start(f32[512,512]{1,0:T(8,128)} %bitcast.18), channel_id=1, source_target_pairs={{0,256},{256,0},{1,257},{257,1},{2,258},{258,2},{3,259},{259,3},{4... | collective-permute-start | bytes 3145736 | tf_op jit(solution)/shard_map/ppermute | solution.py:353
  17.8 13.3 %all-to-all-done = f32[8,16,1024]{2,1,0:T(8,128)S(1)} async-done(((f32[8,16,1024]{2,1,0:T(8,128)}), f32[8,16,1024]{2,1,0:T(8,128)S(1)}, u32[]{:S(2)}, u32[]{:S(2)}) %all-to-all-start) | async-done | bytes 524320 | tf_op jit(solution)/shard_map/all_to_all | solution.py:375
  31.1 3.1 %collective-permute-start = (f32[8,16,1024]{2,1,0:T(8,128)S(1)}, f32[8,16,1024]{2,1,0:T(8,128)S(1)}, u32[]{:S(2)}, u32[]{:S(2)}) collective-permute-start(f32[8,16,1024]{2,1,0:T(8,128)S(1)} %all-to-all-done), channel_id=1, source_target_pairs={{0,16},{16,0},{1,17},{17,1},{2,18},{18,2},{3,19},{19,3},{4,20},{20... | collective-permute-start | bytes 1572872 | tf_op jit(solution)/shard_map/ppermute | solution.py:377
  34.2 0.7 dynamic-slice_subtract_fusion
  35.0 4.3 %collective-permute-start.2 = (s32[2,1,512]{2,1,0:T(1,128)S(1)}, s32[2,1,512]{2,1,0:T(1,128)S(1)}, u32[]{:S(2)}, u32[]{:S(2)}) collective-permute-start(s32[2,1,512]{2,1,0:T(1,128)S(1)} %pad_add_fusion), channel_id=1, source_target_pairs={{0,256},{256,0},{1,257},{257,1},{2,258},{258,2},{3,259},{259,3},{4... | collective-permute-start | bytes 12296 | tf_op jit(solution)/shard_map/ppermute | solution.py:357
  40.0 0.1 stack.28.scalars
  40.0 0.0 copy-start.1
  40.0 1.6 %copy-done.1 = f32[1,512,1024]{2,1,0:T(8,128)S(1)} copy-done((f32[1,512,1024]{2,1,0:T(8,128)S(1)}, f32[1,512,1024]{2,1,0:T(8,128)}, u32[]{:S(2)}) %copy-start.1) | copy-done | bytes 2097176
  41.6 0.0 copy-start.2
  41.6 1.2 copy-done.2
  42.9 0.0 copy-start.3
  42.9 0.7 copy-done.3
  43.5 2.5 %shard_map.78.total = f32[1024,512]{1,0:T(8,128)S(1)} custom-call(s32[5]{0:T(128)S(1)} %stack.28.scalars, s32[4,4]{1,0:T(4,128)S(1)} %copy-done.3, f32[512,512]{1,0:T(8,128)S(1)} %bitcast.19, f32[512,1024]{1,0:T(8,128)S(1)} %bitcast.17, s32[1,512]{1,0:T(1,128)S(1)} %get-tuple-element.33.columns, s32[1,512]{1,0:T(1,128)S(1)} %get-tuple-element.32.targets), custom_call_target="tpu_custom_call" | custom-call | flops 2000000000 | bytes 5000000 | tf_op jit(solution)/shard_map/pallas_call | solution.py:79
  46.1 5.4 %collective-permute-done.2.maps = s32[2,1,512]{2,1,0:T(1,128)S(1)} collective-permute-done((s32[2,1,512]{2,1,0:T(1,128)S(1)}, s32[2,1,512]{2,1,0:T(1,128)S(1)}, u32[]{:S(2)}, u32[]{:S(2)}) %collective-permute-start.2) | collective-permute-done | bytes 4128 | tf_op jit(solution)/shard_map/ppermute | solution.py:357
  51.5 0.0 collective-permute-done.1.block
  51.5 2.5 %shard_map.79 = (bf16[1024,512]{1,0:T(8,128)(2,1)S(1)}, bf16[1024,512]{1,0:T(8,128)(2,1)S(1)}) custom-call(s32[5]{0:T(128)S(1)} %stack.28.scalars, f32[1024,512]{1,0:T(8,128)S(1)} %shard_map.78.total, f32[512,512]{1,0:T(8,128)S(1)} %collective-permute-done.1.block, s32[2,1,512]{2,1,0:T(1,128)S(1)} %collective-permute-done.2.maps), custom_call_target="tpu_custom_call" | custom-call | flops 2000000000 | bytes 5000000 | tf_op jit(solution)/shard_map/pallas_call | solution.py:92
  54.0 0.0 collective-permute-done
  54.0 1.6 %shard_map.80 = (f32[8,16,512]{2,1,0:T(8,128)S(1)}, f32[8,16,512]{2,1,0:T(8,128)S(1)}) custom-call(s32[5]{0:T(128)S(1)} %stack.28.scalars, f32[8,2,8,1024]{3,2,1,0:T(8,128)S(1)} %bitcast.13, f32[8,2,8,1024]{3,2,1,0:T(8,128)S(1)} %bitcast.20, bf16[1024,512]{1,0:T(8,128)(2,1)S(1)} %get-tuple-element.19.top, bf16[1024,512]{1,0:T(8,128)(2,1)S(1)} %get-tuple-element.20.low), custom_call_target="tpu_custom_call" | custom-call | flops 1000000000 | bytes 6000000 | tf_op jit(solution)/shard_map/pallas_call | solution.py:136
  55.6 4.1 %collective-permute-start.3 = (f32[8,16,512]{2,1,0:T(8,128)S(1)}, f32[8,16,512]{2,1,0:T(8,128)S(1)}, u32[]{:S(2)}, u32[]{:S(2)}) collective-permute-start(f32[8,16,512]{2,1,0:T(8,128)S(1)} %get-tuple-element.22), channel_id=1, source_target_pairs={{0,1},{1,0},{2,3},{3,2},{4,5},{5,4},{6,7},{7,6},{8,9},{9,8},{10,11... | collective-permute-start | bytes 786440 | tf_op jit(solution)/shard_map/ppermute | solution.py:383
  59.7 1.1 collective-permute-done.3
  60.9 17.7 %all_to_all.15 = f32[8,16,512]{2,1,0:T(8,128)S(1)} all-to-all(f32[8,16,512]{2,1,0:T(8,128)S(1)} %add.24), channel_id=1, replica_groups=mesh['child'=2,'z'=8,'xl'=2,'y'=8,'core'=2] {'y'}, dimensions={0} | all-to-all | bytes 524288 | tf_op jit(solution)/shard_map/all_to_all | solution.py:384
  78.6 0.1 broadcast_in_dim.6
  78.7 18.9 %all_to_all.16.mine = f32[16,16,512]{2,1,0:T(8,128)S(1)} all-to-all(f32[16,16,512]{2,1,0:T(8,128)S(1)} %broadcast_in_dim.6), channel_id=1, replica_groups=mesh['child'=2,'z'=8,'xl'=2,'y'=8,'core'=2] {'child','y'}, dimensions={0} | all-to-all | bytes 1048576 | tf_op jit(solution)/shard_map/all_to_all | solution.py:386
  97.6 4.9 %collective-permute-start.4 = (f32[16,16,512]{2,1,0:T(8,128)S(1)}, f32[16,16,512]{2,1,0:T(8,128)S(1)}, u32[]{:S(2)}, u32[]{:S(2)}) collective-permute-start(f32[16,16,512]{2,1,0:T(8,128)S(1)} %all_to_all.16.mine), channel_id=1, source_target_pairs={{0,1},{1,0},{2,3},{3,2},{4,5},{5,4},{6,7},{7,6},{8,9},{9,8},{10,11... | collective-permute-start | bytes 1572872 | tf_op jit(solution)/shard_map/ppermute | solution.py:389
  102.5 1.5 %collective-permute-done.4.theirs = f32[16,16,512]{2,1,0:T(8,128)S(1)} collective-permute-done((f32[16,16,512]{2,1,0:T(8,128)S(1)}, f32[16,16,512]{2,1,0:T(8,128)S(1)}, u32[]{:S(2)}, u32[]{:S(2)}) %collective-permute-start.4) | collective-permute-done | bytes 524320 | tf_op jit(solution)/shard_map/ppermute | solution.py:389
  104.0 6.2 %shard_map.81 = (f32[256,1024]{1,0:T(8,128)S(1)}, f32[2,128,256]{2,1,0:T(8,128)S(1)}, f32[2,128,128]{2,1,0:T(8,128)S(1)}, f32[2,128,256]{2,1,0:T(8,128)S(1)}) custom-call(s32[5]{0:T(128)S(1)} %stack.28.scalars, f32[16,16,512]{2,1,0:T(8,128)S(1)} %all_to_all.16.mine, f32[16,16,512]{2,1,0:T(8,128)S(1)} %collective-permute-done.4.theirs), custom_call_target="tpu_custom_call" | custom-call | tf_op jit(solution)/shard_map/pallas_call | solution.py:260
  110.2 2.2 %collective-permute-start.5 = (f32[2,128,256]{2,1,0:T(8,128)S(1)}, f32[2,128,256]{2,1,0:T(8,128)S(1)}, u32[]{:S(2)}, u32[]{:S(2)}) collective-permute-start(f32[2,128,256]{2,1,0:T(8,128)S(1)} %get-tuple-element.24.u_head), channel_id=1, source_target_pairs={{0,16},{16,0},{1,17},{17,1},{2,18},{18,2},{3,19},{19,3},{4,20},{20... | collective-permute-start | bytes 786440 | tf_op jit(solution)/shard_map/ppermute | solution.py:392
  112.4 5.0 %shard_map.82 = (f32[136,128]{1,0:T(8,128)S(1)}, f32[2,8,256]{2,1,0:T(8,128)S(1)}, f32[2,8,256]{2,1,0:T(8,128)S(1)}) custom-call(s32[5]{0:T(128)S(1)} %stack.28.scalars, f32[2,128,256]{2,1,0:T(8,128)S(1)} %get-tuple-element.24.u_head, f32[2,128,128]{2,1,0:T(8,128)S(1)} %get-tuple-element.25.x_head, f32[2,128,256]{2,1,0:T(8,128)S(1)} %get-tuple-element.26.rest), custom_call_target="tpu_custom_call" | custom-call | flops 8000000000 | bytes 1000000 | tf_op jit(solution)/shard_map/pallas_call | solution.py:306
  117.4 3.0 %collective-permute-start.6 = (f32[136,128]{1,0:T(8,128)S(1)}, f32[136,128]{1,0:T(8,128)S(1)}, u32[]{:S(2)}, u32[]{:S(2)}) collective-permute-start(f32[136,128]{1,0:T(8,128)S(1)} %get-tuple-element.31), channel_id=1, source_target_pairs={{0,16},{16,0},{1,17},{17,1},{2,18},{18,2},{3,19},{19,3},{4,20},{20... | collective-permute-start | bytes 208904 | tf_op jit(solution)/shard_map/ppermute | solution.py:394
  120.5 0.0 collective-permute-done.5.sib_head
  120.5 1.5 %shard_map.83 = (f32[8,1024]{1,0:T(8,128)}, f32[2,8,128]{2,1,0:T(8,128)S(1)}) custom-call(s32[5]{0:T(128)S(1)} %stack.28.scalars, f32[256,1024]{1,0:T(8,128)S(1)} %get-tuple-element.23.window, f32[2,8,256]{2,1,0:T(8,128)S(1)} %get-tuple-element.27.x_own, f32[2,8,256]{2,1,0:T(8,128)S(1)} %get-tuple-element.28.u_own, ...), custom_call_target="tpu_custom_call" | custom-call | flops 1000000000 | bytes 1000000 | tf_op jit(solution)/shard_map/pallas_call | solution.py:395
  122.0 0.5 collective-permute-done.6.packed
  122.5 1.0 shard_map.84
  (3 shorter events, 0.1 us)
Async XLA Ops:
  0.6 0.8 copy-start
  2.3 28.8 %all-to-all-start = ((f32[8,16,1024]{2,1,0:T(8,128)}), f32[8,16,1024]{2,1,0:T(8,128)S(1)}, u32[]{:S(2)}, u32[]{:S(2)}) async-start(f32[8,16,1024]{2,1,0:T(8,128)} %shard_map.77), calls=%async_computation | async-start | bytes 1048576 | tf_op jit(solution)/shard_map/all_to_all | solution.py:375
  13.2 38.3 %collective-permute-start.1 = (f32[512,512]{1,0:T(8,128)}, f32[512,512]{1,0:T(8,128)S(1)}, u32[]{:S(2)}, u32[]{:S(2)}) collective-permute-start(f32[512,512]{1,0:T(8,128)} %bitcast.18), channel_id=1, source_target_pairs={{0,256},{256,0},{1,257},{257,1},{2,258},{258,2},{3,259},{259,3},{4... | collective-permute-start | bytes 3145736 | tf_op jit(solution)/shard_map/ppermute | solution.py:353
  31.1 22.9 %collective-permute-start = (f32[8,16,1024]{2,1,0:T(8,128)S(1)}, f32[8,16,1024]{2,1,0:T(8,128)S(1)}, u32[]{:S(2)}, u32[]{:S(2)}) collective-permute-start(f32[8,16,1024]{2,1,0:T(8,128)S(1)} %all-to-all-done), channel_id=1, source_target_pairs={{0,16},{16,0},{1,17},{17,1},{2,18},{18,2},{3,19},{19,3},{4,20},{20... | collective-permute-start | bytes 1572872 | tf_op jit(solution)/shard_map/ppermute | solution.py:377
  35.0 16.6 %collective-permute-start.2 = (s32[2,1,512]{2,1,0:T(1,128)S(1)}, s32[2,1,512]{2,1,0:T(1,128)S(1)}, u32[]{:S(2)}, u32[]{:S(2)}) collective-permute-start(s32[2,1,512]{2,1,0:T(1,128)S(1)} %pad_add_fusion), channel_id=1, source_target_pairs={{0,256},{256,0},{1,257},{257,1},{2,258},{258,2},{3,259},{259,3},{4... | collective-permute-start | bytes 12296 | tf_op jit(solution)/shard_map/ppermute | solution.py:357
  40.0 1.6 %copy-start.1 = (f32[1,512,1024]{2,1,0:T(8,128)S(1)}, f32[1,512,1024]{2,1,0:T(8,128)}, u32[]{:S(2)}) copy-start(f32[1,512,1024]{2,1,0:T(8,128)} %param.7) | copy-start | bytes 6291460
  41.6 1.2 copy-start.2
  42.9 0.7 copy-start.3
  55.6 5.2 %collective-permute-start.3 = (f32[8,16,512]{2,1,0:T(8,128)S(1)}, f32[8,16,512]{2,1,0:T(8,128)S(1)}, u32[]{:S(2)}, u32[]{:S(2)}) collective-permute-start(f32[8,16,512]{2,1,0:T(8,128)S(1)} %get-tuple-element.22), channel_id=1, source_target_pairs={{0,1},{1,0},{2,3},{3,2},{4,5},{5,4},{6,7},{7,6},{8,9},{9,8},{10,11... | collective-permute-start | bytes 786440 | tf_op jit(solution)/shard_map/ppermute | solution.py:383
  97.6 6.4 %collective-permute-start.4 = (f32[16,16,512]{2,1,0:T(8,128)S(1)}, f32[16,16,512]{2,1,0:T(8,128)S(1)}, u32[]{:S(2)}, u32[]{:S(2)}) collective-permute-start(f32[16,16,512]{2,1,0:T(8,128)S(1)} %all_to_all.16.mine), channel_id=1, source_target_pairs={{0,1},{1,0},{2,3},{3,2},{4,5},{5,4},{6,7},{7,6},{8,9},{9,8},{10,11... | collective-permute-start | bytes 1572872 | tf_op jit(solution)/shard_map/ppermute | solution.py:389
  110.2 10.3 %collective-permute-start.5 = (f32[2,128,256]{2,1,0:T(8,128)S(1)}, f32[2,128,256]{2,1,0:T(8,128)S(1)}, u32[]{:S(2)}, u32[]{:S(2)}) collective-permute-start(f32[2,128,256]{2,1,0:T(8,128)S(1)} %get-tuple-element.24.u_head), channel_id=1, source_target_pairs={{0,16},{16,0},{1,17},{17,1},{2,18},{18,2},{3,19},{19,3},{4,20},{20... | collective-permute-start | bytes 786440 | tf_op jit(solution)/shard_map/ppermute | solution.py:392
  117.4 5.1 %collective-permute-start.6 = (f32[136,128]{1,0:T(8,128)S(1)}, f32[136,128]{1,0:T(8,128)S(1)}, u32[]{:S(2)}, u32[]{:S(2)}) collective-permute-start(f32[136,128]{1,0:T(8,128)S(1)} %get-tuple-element.31), channel_id=1, source_target_pairs={{0,16},{16,0},{1,17},{17,1},{2,18},{18,2},{3,19},{19,3},{4,20},{20... | collective-permute-start | bytes 208904 | tf_op jit(solution)/shard_map/ppermute | solution.py:394

commit v12 on v8

--- a/solution.py
+++ b/solution.py
@@ -111,13 +111,11 @@
         [piece[:, side].reshape(-1, depth) for side in range(2) for piece in (own, ahead, behind)]
     )
     high_lines, low_lines = two_parts(ordered)
+    stacked = jnp.concatenate([high_lines, low_lines])
     for tile in range(half_rows // BT):
         lanes = slice(tile * BT, (tile + 1) * BT)
-        out = (
-            dot(high_lines, top[:, lanes], NN)
-            + dot(low_lines, top[:, lanes], NN)
-            + dot(high_lines, low[:, lanes], NN)
-        )
+        wide = dot(stacked, top[:, lanes], NN)
+        out = wide[: 2 * rows] + wide[2 * rows :] + dot(high_lines, low[:, lanes], NN)
         first, second = out[:rows], out[rows:]
         for target, value in (
             (give, jnp.where(core == 0, second, first)),

time: 116 us -> 116 us (level)
  no operation moved by 1% of the time
where the time goes in v12:
time: 116 us; the launch traced here: 115 us
  starting transfers between devices  36.7 us (32%)
  blocking collectives  36.6 us (32%)
  Pallas kernels  21.7 us (19%)
  waiting for transfers between devices  15.8 us (14%)
  local copies, waits for them, and re-layouts  2.23 us (2%)
  between operations  1.48 us (1%)
    all_to_all x1, blocking collectives, local(): lax.all_to_all(jnp.broadcast_to(samples, (groups,) + samples.shape), ('ch...  18.9 us
    all_to_all x1, blocking collectives, local(): terms = lax.all_to_all(parts, 'y', 0, 0)  17.7 us
    all_to_all x1, starting transfers between devices, local(): own = lax.all_to_all(copies, 'z', 0, 0)  10.9 us
    all_to_all x1, waiting for transfers between devices, local(): own = lax.all_to_all(copies, 'z', 0, 0)  9.71 us
    ppermute x2, starting transfers between devices, local(): lax.ppermute(piece, ('child', 'xl'), [(i, (i + step) % ring) for i in ran...  6.49 us
    pallas_call x1, Pallas kernels, factor_head(): pl.pallas_call(head_kernel, in_specs=[SMEM, VMEM, VMEM], out_specs=[VMEM]...  6.17 us
    pallas_call x1, Pallas kernels, factor_tail(): pl.pallas_call(tail_kernel, in_specs=[SMEM] + [VMEM] * 3, out_specs=[VMEM...  5.04 us
    ppermute x1, starting transfers between devices, local(): theirs = lax.ppermute(mine, 'core', SWAP)  4.86 us
  transfers between devices with their start and end apart: 9, of which 5 were waited for; matrix products, arithmetic and copies ran while one was open for 1% of the time, Pallas kernels for 11%

profile of v12, /device:TPU:1, one launch (start us, length us, event | category | flops | bytes accessed | tf_op | source)
XLA Modules:
  0.0 115.3 jit_solution(12049320622132646515)
XLA Ops:
  0.6 0.0 copy-start
  0.6 0.8 copy-done
  1.5 0.0 copy-start.1
  1.5 0.0 copy-start.3
  1.5 0.9 shard_map.77
  2.3 10.9 %all-to-all-start = ((f32[8,16,1024]{2,1,0:T(8,128)}), f32[8,16,1024]{2,1,0:T(8,128)S(1)}, u32[]{:S(2)}, u32[]{:S(2)}) async-start(f32[8,16,1024]{2,1,0:T(8,128)} %shard_map.77), calls=%async_computation | async-start | bytes 1048576 | tf_op jit(solution)/shard_map/all_to_all | solution.py:373
  13.2 4.6 %collective-permute-start.2 = (f32[512,512]{1,0:T(8,128)}, f32[512,512]{1,0:T(8,128)}, u32[]{:S(2)}, u32[]{:S(2)}) collective-permute-start(f32[512,512]{1,0:T(8,128)} %bitcast.19), channel_id=1, source_target_pairs={{0,256},{256,0},{1,257},{257,1},{2,258},{258,2},{3,259},{259,3},{4... | collective-permute-start | bytes 3145736 | tf_op jit(solution)/shard_map/ppermute | solution.py:351
  17.9 0.7 dynamic-slice_subtract_fusion
  18.6 2.1 %collective-permute-start.3 = (s32[2,1,512]{2,1,0:T(1,128)S(1)}, s32[2,1,512]{2,1,0:T(1,128)S(1)}, u32[]{:S(2)}, u32[]{:S(2)}) collective-permute-start(s32[2,1,512]{2,1,0:T(1,128)S(1)} %pad_add_fusion), channel_id=1, source_target_pairs={{0,256},{256,0},{1,257},{257,1},{2,258},{258,2},{3,259},{259,3},{4... | collective-permute-start | bytes 12296 | tf_op jit(solution)/shard_map/ppermute | solution.py:355
  21.4 0.1 stack.28.scalars
  21.4 9.7 %all-to-all-done = f32[8,16,1024]{2,1,0:T(8,128)S(1)} async-done(((f32[8,16,1024]{2,1,0:T(8,128)}), f32[8,16,1024]{2,1,0:T(8,128)S(1)}, u32[]{:S(2)}, u32[]{:S(2)}) %all-to-all-start) | async-done | bytes 524320 | tf_op jit(solution)/shard_map/all_to_all | solution.py:373
  31.2 3.1 %collective-permute-start = (f32[4,16,1024]{2,1,0:T(8,128)S(1)}, f32[4,16,1024]{2,1,0:T(8,128)S(1)}, u32[]{:S(2)}, u32[]{:S(2)}) collective-permute-start(f32[4,16,1024]{2,1,0:T(8,128)S(1)} %get-tuple-element.33), channel_id=1, source_target_pairs={{0,16},{16,256},{256,272},{272,0},{1,17},{17,257},{257,273},{273,1... | collective-permute-start | bytes 786440 | tf_op jit(solution)/shard_map/ppermute | solution.py:377
  34.3 3.4 %collective-permute-start.1 = (f32[4,16,1024]{2,1,0:T(8,128)S(1)}, f32[4,16,1024]{2,1,0:T(8,128)S(1)}, u32[]{:S(2)}, u32[]{:S(2)}) collective-permute-start(f32[4,16,1024]{2,1,0:T(8,128)S(1)} %get-tuple-element.32), channel_id=1, source_target_pairs={{0,272},{16,0},{256,16},{272,256},{1,273},{17,1},{257,17},{273,257... | collective-permute-start | bytes 786440 | tf_op jit(solution)/shard_map/ppermute | solution.py:377
  37.7 0.0 copy-done.1
  37.7 0.0 copy-done.3
  37.7 0.0 copy-start.2
  37.7 1.2 %copy-done.2 = f32[1,512,512]{2,1,0:T(8,128)S(1)} copy-done((f32[1,512,512]{2,1,0:T(8,128)S(1)}, f32[1,512,512]{2,1,0:T(8,128)}, u32[]{:S(2)}) %copy-start.2) | copy-done | bytes 1048600
  39.0 2.5 %shard_map.78.total = f32[1024,512]{1,0:T(8,128)S(1)} custom-call(s32[5]{0:T(128)S(1)} %stack.28.scalars, s32[4,4]{1,0:T(4,128)S(1)} %copy-done.3, f32[512,512]{1,0:T(8,128)S(1)} %bitcast.20, f32[512,1024]{1,0:T(8,128)S(1)} %bitcast.18, s32[1,512]{1,0:T(1,128)S(1)} %get-tuple-element.35.columns, s32[1,512]{1,0:T(1,128)S(1)} %get-tuple-element.34.targets), custom_call_target="tpu_custom_call" | custom-call | flops 2000000000 | bytes 5000000 | tf_op jit(solution)/shard_map/pallas_call | solution.py:79
  41.5 0.0 collective-permute-done.3.maps
  41.5 0.0 collective-permute-done.2.block
  41.5 3.2 %shard_map.79 = (bf16[1024,512]{1,0:T(8,128)(2,1)S(1)}, bf16[1024,512]{1,0:T(8,128)(2,1)S(1)}) custom-call(s32[5]{0:T(128)S(1)} %stack.28.scalars, f32[1024,512]{1,0:T(8,128)S(1)} %shard_map.78.total, f32[512,512]{1,0:T(8,128)} %collective-permute-done.2.block, s32[2,1,512]{2,1,0:T(1,128)S(1)} %collective-permute-done.3.maps), custom_call_target="tpu_custom_call" | custom-call | flops 2000000000 | bytes 5000000 | tf_op jit(solution)/shard_map/pallas_call | solution.py:92
  44.7 2.9 %collective-permute-done = f32[4,16,1024]{2,1,0:T(8,128)S(1)} collective-permute-done((f32[4,16,1024]{2,1,0:T(8,128)S(1)}, f32[4,16,1024]{2,1,0:T(8,128)S(1)}, u32[]{:S(2)}, u32[]{:S(2)}) %collective-permute-start) | collective-permute-done | bytes 262176 | tf_op jit(solution)/shard_map/ppermute | solution.py:377
  47.6 0.0 collective-permute-done.1
  47.6 1.5 %shard_map.80 = (f32[8,16,512]{2,1,0:T(8,128)S(1)}, f32[8,16,512]{2,1,0:T(8,128)S(1)}) custom-call(s32[5]{0:T(128)S(1)} %stack.28.scalars, f32[8,2,8,1024]{3,2,1,0:T(8,128)S(1)} %bitcast.14, f32[4,2,8,1024]{3,2,1,0:T(8,128)S(1)} %bitcast.21, f32[4,2,8,1024]{3,2,1,0:T(8,128)S(1)} %bitcast.22, bf16[1024,512]{1,0:T(8,128)(2,1)S(1)} %get-tuple-element.19.top, ...), custom_call_target="tpu_custom_call" | custom-call | flops 1000000000 | bytes 6000000 | tf_op jit(solution)/shard_map/pallas_call | solution.py:134
  49.1 2.5 %collective-permute-start.4 = (f32[8,16,512]{2,1,0:T(8,128)S(1)}, f32[8,16,512]{2,1,0:T(8,128)S(1)}, u32[]{:S(2)}, u32[]{:S(2)}) collective-permute-start(f32[8,16,512]{2,1,0:T(8,128)S(1)} %get-tuple-element.22), channel_id=1, source_target_pairs={{0,1},{1,0},{2,3},{3,2},{4,5},{5,4},{6,7},{7,6},{8,9},{9,8},{10,11... | collective-permute-start | bytes 786440 | tf_op jit(solution)/shard_map/ppermute | solution.py:385
  51.6 1.1 collective-permute-done.4
  52.8 17.7 %all_to_all.15 = f32[8,16,512]{2,1,0:T(8,128)S(1)} all-to-all(f32[8,16,512]{2,1,0:T(8,128)S(1)} %add.24), channel_id=1, replica_groups=mesh['child'=2,'z'=8,'xl'=2,'y'=8,'core'=2] {'y'}, dimensions={0} | all-to-all | bytes 524288 | tf_op jit(solution)/shard_map/all_to_all | solution.py:386
  70.5 0.1 broadcast_in_dim.6
  70.6 18.9 %all_to_all.16.mine = f32[16,16,512]{2,1,0:T(8,128)S(1)} all-to-all(f32[16,16,512]{2,1,0:T(8,128)S(1)} %broadcast_in_dim.6), channel_id=1, replica_groups=mesh['child'=2,'z'=8,'xl'=2,'y'=8,'core'=2] {'child','y'}, dimensions={0} | all-to-all | bytes 1048576 | tf_op jit(solution)/shard_map/all_to_all | solution.py:388
  89.4 4.9 %collective-permute-start.5 = (f32[16,16,512]{2,1,0:T(8,128)S(1)}, f32[16,16,512]{2,1,0:T(8,128)S(1)}, u32[]{:S(2)}, u32[]{:S(2)}) collective-permute-start(f32[16,16,512]{2,1,0:T(8,128)S(1)} %all_to_all.16.mine), channel_id=1, source_target_pairs={{0,1},{1,0},{2,3},{3,2},{4,5},{5,4},{6,7},{7,6},{8,9},{9,8},{10,11... | collective-permute-start | bytes 1572872 | tf_op jit(solution)/shard_map/ppermute | solution.py:391
  94.3 1.5 %collective-permute-done.5.theirs = f32[16,16,512]{2,1,0:T(8,128)S(1)} collective-permute-done((f32[16,16,512]{2,1,0:T(8,128)S(1)}, f32[16,16,512]{2,1,0:T(8,128)S(1)}, u32[]{:S(2)}, u32[]{:S(2)}) %collective-permute-start.5) | collective-permute-done | bytes 524320 | tf_op jit(solution)/shard_map/ppermute | solution.py:391
  95.8 6.2 %shard_map.81 = (f32[256,1024]{1,0:T(8,128)S(1)}, f32[2,128,256]{2,1,0:T(8,128)S(1)}, f32[2,128,128]{2,1,0:T(8,128)S(1)}, f32[2,128,256]{2,1,0:T(8,128)S(1)}) custom-call(s32[5]{0:T(128)S(1)} %stack.28.scalars, f32[16,16,512]{2,1,0:T(8,128)S(1)} %all_to_all.16.mine, f32[16,16,512]{2,1,0:T(8,128)S(1)} %collective-permute-done.5.theirs), custom_call_target="tpu_custom_call" | custom-call | tf_op jit(solution)/shard_map/pallas_call | solution.py:258
  102.0 2.2 %collective-permute-start.6 = (f32[2,128,256]{2,1,0:T(8,128)S(1)}, f32[2,128,256]{2,1,0:T(8,128)S(1)}, u32[]{:S(2)}, u32[]{:S(2)}) collective-permute-start(f32[2,128,256]{2,1,0:T(8,128)S(1)} %get-tuple-element.24.u_head), channel_id=1, source_target_pairs={{0,16},{16,0},{1,17},{17,1},{2,18},{18,2},{3,19},{19,3},{4,20},{20... | collective-permute-start | bytes 786440 | tf_op jit(solution)/shard_map/ppermute | solution.py:394
  104.2 5.0 %shard_map.82 = (f32[136,128]{1,0:T(8,128)S(1)}, f32[2,8,256]{2,1,0:T(8,128)S(1)}, f32[2,8,256]{2,1,0:T(8,128)S(1)}) custom-call(s32[5]{0:T(128)S(1)} %stack.28.scalars, f32[2,128,256]{2,1,0:T(8,128)S(1)} %get-tuple-element.24.u_head, f32[2,128,128]{2,1,0:T(8,128)S(1)} %get-tuple-element.25.x_head, f32[2,128,256]{2,1,0:T(8,128)S(1)} %get-tuple-element.26.rest), custom_call_target="tpu_custom_call" | custom-call | flops 8000000000 | bytes 1000000 | tf_op jit(solution)/shard_map/pallas_call | solution.py:304
  109.3 3.1 %collective-permute-start.7 = (f32[136,128]{1,0:T(8,128)S(1)}, f32[136,128]{1,0:T(8,128)S(1)}, u32[]{:S(2)}, u32[]{:S(2)}) collective-permute-start(f32[136,128]{1,0:T(8,128)S(1)} %get-tuple-element.31), channel_id=1, source_target_pairs={{0,16},{16,0},{1,17},{17,1},{2,18},{18,2},{3,19},{19,3},{4,20},{20... | collective-permute-start | bytes 208904 | tf_op jit(solution)/shard_map/ppermute | solution.py:396
  112.3 0.0 collective-permute-done.6.sib_head
  112.3 1.4 %shard_map.83 = (f32[8,1024]{1,0:T(8,128)}, f32[2,8,128]{2,1,0:T(8,128)S(1)}) custom-call(s32[5]{0:T(128)S(1)} %stack.28.scalars, f32[256,1024]{1,0:T(8,128)S(1)} %get-tuple-element.23.window, f32[2,8,256]{2,1,0:T(8,128)S(1)} %get-tuple-element.27.x_own, f32[2,8,256]{2,1,0:T(8,128)S(1)} %get-tuple-element.28.u_own, ...), custom_call_target="tpu_custom_call" | custom-call | flops 1000000000 | bytes 1000000 | tf_op jit(solution)/shard_map/pallas_call | solution.py:397
  113.8 0.5 collective-permute-done.7.packed
  114.3 1.0 shard_map.84
  (4 shorter events, 0.1 us)
Async XLA Ops:
  0.6 0.8 copy-start
  1.5 36.2 %copy-start.1 = (f32[1,512,1024]{2,1,0:T(8,128)S(1)}, f32[1,512,1024]{2,1,0:T(8,128)}, u32[]{:S(2)}) copy-start(f32[1,512,1024]{2,1,0:T(8,128)} %param.7) | copy-start | bytes 6291460
  1.5 36.2 %copy-start.3 = (s32[4,4]{1,0:T(4,128)S(1)}, s32[4,4]{1,0:T(4,128)}, u32[]{:S(2)}) copy-start(s32[4,4]{1,0:T(4,128)} %pattern.1) | copy-start | bytes 196
  2.3 28.8 %all-to-all-start = ((f32[8,16,1024]{2,1,0:T(8,128)}), f32[8,16,1024]{2,1,0:T(8,128)S(1)}, u32[]{:S(2)}, u32[]{:S(2)}) async-start(f32[8,16,1024]{2,1,0:T(8,128)} %shard_map.77), calls=%async_computation | async-start | bytes 1048576 | tf_op jit(solution)/shard_map/all_to_all | solution.py:373
  13.2 28.3 %collective-permute-start.2 = (f32[512,512]{1,0:T(8,128)}, f32[512,512]{1,0:T(8,128)}, u32[]{:S(2)}, u32[]{:S(2)}) collective-permute-start(f32[512,512]{1,0:T(8,128)} %bitcast.19), channel_id=1, source_target_pairs={{0,256},{256,0},{1,257},{257,1},{2,258},{258,2},{3,259},{259,3},{4... | collective-permute-start | bytes 3145736 | tf_op jit(solution)/shard_map/ppermute | solution.py:351
  18.6 22.9 %collective-permute-start.3 = (s32[2,1,512]{2,1,0:T(1,128)S(1)}, s32[2,1,512]{2,1,0:T(1,128)S(1)}, u32[]{:S(2)}, u32[]{:S(2)}) collective-permute-start(s32[2,1,512]{2,1,0:T(1,128)S(1)} %pad_add_fusion), channel_id=1, source_target_pairs={{0,256},{256,0},{1,257},{257,1},{2,258},{258,2},{3,259},{259,3},{4... | collective-permute-start | bytes 12296 | tf_op jit(solution)/shard_map/ppermute | solution.py:355
  31.2 16.4 %collective-permute-start = (f32[4,16,1024]{2,1,0:T(8,128)S(1)}, f32[4,16,1024]{2,1,0:T(8,128)S(1)}, u32[]{:S(2)}, u32[]{:S(2)}) collective-permute-start(f32[4,16,1024]{2,1,0:T(8,128)S(1)} %get-tuple-element.33), channel_id=1, source_target_pairs={{0,16},{16,256},{256,272},{272,0},{1,17},{17,257},{257,273},{273,1... | collective-permute-start | bytes 786440 | tf_op jit(solution)/shard_map/ppermute | solution.py:377
  34.3 13.3 %collective-permute-start.1 = (f32[4,16,1024]{2,1,0:T(8,128)S(1)}, f32[4,16,1024]{2,1,0:T(8,128)S(1)}, u32[]{:S(2)}, u32[]{:S(2)}) collective-permute-start(f32[4,16,1024]{2,1,0:T(8,128)S(1)} %get-tuple-element.32), channel_id=1, source_target_pairs={{0,272},{16,0},{256,16},{272,256},{1,273},{17,1},{257,17},{273,257... | collective-permute-start | bytes 786440 | tf_op jit(solution)/shard_map/ppermute | solution.py:377
  37.7 1.2 %copy-start.2 = (f32[1,512,512]{2,1,0:T(8,128)S(1)}, f32[1,512,512]{2,1,0:T(8,128)}, u32[]{:S(2)}) copy-start(f32[1,512,512]{2,1,0:T(8,128)} %param.6) | copy-start | bytes 3145732
  49.1 3.6 %collective-permute-start.4 = (f32[8,16,512]{2,1,0:T(8,128)S(1)}, f32[8,16,512]{2,1,0:T(8,128)S(1)}, u32[]{:S(2)}, u32[]{:S(2)}) collective-permute-start(f32[8,16,512]{2,1,0:T(8,128)S(1)} %get-tuple-element.22), channel_id=1, source_target_pairs={{0,1},{1,0},{2,3},{3,2},{4,5},{5,4},{6,7},{7,6},{8,9},{9,8},{10,11... | collective-permute-start | bytes 786440 | tf_op jit(solution)/shard_map/ppermute | solution.py:385
  89.4 6.4 %collective-permute-start.5 = (f32[16,16,512]{2,1,0:T(8,128)S(1)}, f32[16,16,512]{2,1,0:T(8,128)S(1)}, u32[]{:S(2)}, u32[]{:S(2)}) collective-permute-start(f32[16,16,512]{2,1,0:T(8,128)S(1)} %all_to_all.16.mine), channel_id=1, source_target_pairs={{0,1},{1,0},{2,3},{3,2},{4,5},{5,4},{6,7},{7,6},{8,9},{9,8},{10,11... | collective-permute-start | bytes 1572872 | tf_op jit(solution)/shard_map/ppermute | solution.py:391
  102.0 10.3 %collective-permute-start.6 = (f32[2,128,256]{2,1,0:T(8,128)S(1)}, f32[2,128,256]{2,1,0:T(8,128)S(1)}, u32[]{:S(2)}, u32[]{:S(2)}) collective-permute-start(f32[2,128,256]{2,1,0:T(8,128)S(1)} %get-tuple-element.24.u_head), channel_id=1, source_target_pairs={{0,16},{16,0},{1,17},{17,1},{2,18},{18,2},{3,19},{19,3},{4,20},{20... | collective-permute-start | bytes 786440 | tf_op jit(solution)/shard_map/ppermute | solution.py:394
  109.3 5.1 %collective-permute-start.7 = (f32[136,128]{1,0:T(8,128)S(1)}, f32[136,128]{1,0:T(8,128)S(1)}, u32[]{:S(2)}, u32[]{:S(2)}) collective-permute-start(f32[136,128]{1,0:T(8,128)S(1)} %get-tuple-element.31), channel_id=1, source_target_pairs={{0,16},{16,0},{1,17},{17,1},{2,18},{18,2},{3,19},{19,3},{4,20},{20... | collective-permute-start | bytes 208904 | tf_op jit(solution)/shard_map/ppermute | solution.py:396
